TPU v7x, 32 devices: a whole 2x2x4 slice. The times are simulated.
32 devices in a mesh: dp: 2 (over y), row: 4 (over z), col: 4 (over x, core).
Axes of the slice: x: 2, y: 2, z: 4, core: 2. Of those that a mesh axis runs over, the one named last changes fastest.
Arguments:
- tokens: bfloat16 [32768, 1024], P(('dp', 'col'), 'row'), may hold values from -6 to 6
- w_query: bfloat16 [1024, 1024], P('row', 'col'), may hold values from -0.1875 to 0.1875
- w_key: bfloat16 [1024, 1024], P('row', 'col'), may hold values from -0.1875 to 0.1875
- w_value: bfloat16 [1024, 1024], P('row', 'col'), may hold values from -0.1875 to 0.1875
- w_out: bfloat16 [1024, 1024], P('col', 'row'), may hold values from -0.75 to 0.75
- w_act: bfloat16 [1024, 2624], P('row', 'col'), may hold values from -0.1875 to 0.1875
- w_gate: bfloat16 [1024, 2624], P('row', 'col'), may hold values from -0.1875 to 0.1875
- w_down: bfloat16 [2624, 1024], P('col', 'row'), may hold values from -0.125 to 0.125
- gain_attn: bfloat16 [1024], P('row'), may hold values from 0.5 to 1.5
- gain_ffn: bfloat16 [1024], P('row'), may hold values from 0.5 to 1.5
- cotangent: bfloat16 [32768, 1024], P(('dp', 'col'), 'row'), may hold values from -6 to 6
- segment_ids: int32 [8, 4096], P(('dp', 'row')), may hold values from 0 to 63, never falling along the last dimension, each value on 1 to 1024 neighbouring positions
- valid_mask: int32 [8, 4096], P(('dp', 'row')), may hold values from 0 to 1, as said below
Outputs:
- layer_out: bfloat16 [32768, 1024], P(('dp', 'col'), 'row')
- token_gradient: float32 [32768, 1024], P(('dp', 'col'), 'row')
- grad_query: float32 [1024, 1024], P('row', 'col')
- grad_key: float32 [1024, 1024], P('row', 'col')
- grad_value: float32 [1024, 1024], P('row', 'col')
- grad_out: float32 [1024, 1024], P('col', 'row')
- grad_act: float32 [1024, 2624], P('row', 'col')
- grad_gate: float32 [1024, 2624], P('row', 'col')
- grad_down: float32 [2624, 1024], P('col', 'row')
- grad_gain_attn: float32 [1024], P('row')
- grad_gain_ffn: float32 [1024], P('row')
Inputs may be any that keep to these rules, and one draw needn't show every extreme that they name: `valid_mask`: in each sequence the ones come first, then 1 to 512 zeros of padding.
All inputs are finite; a program needn't handle non-finite values.
Results may differ from a plain program's by a relative error of at most 0.015.
Values may be sent and summed in bfloat16 or wider, within the bound.
No kernel may reach another device: no remote copies, remote signals or barrier semaphores. Data moves between devices by JAX's collectives and lax.ppermute only.
A program may use at most 384 MiB of HBM per device.

v0:
```python
import jax
import jax.numpy as jnp
from jax import lax
from jax.sharding import PartitionSpec as P

MODEL_WIDTH = 1024
HEAD = 64
WINDOW = 128


EPSILON = 1e-05
ROPE_THETA = 10000.0
MASKED_SCORE = -1e30


def feature_moments(first_term, second_term):
    return lax.psum((jnp.sum(first_term, axis=1), jnp.sum(second_term, axis=1)), "row")


def apply_norm(values):
    row_sum_total, squares = feature_moments(values, values * values)
    average = row_sum_total / MODEL_WIDTH
    variance = squares / MODEL_WIDTH - average * average
    inverse_norm = lax.rsqrt(variance + EPSILON)
    return ((values - average[:, None]) * inverse_norm[:, None], inverse_norm)


def norm_backward(normed_gradient, centered_unit_rows, inverse_norm, gain_row_values):
    scaled_rows = normed_gradient * gain_row_values[None, :]
    row_sum_total, crossed_product = feature_moments(scaled_rows, scaled_rows * centered_unit_rows)
    return inverse_norm[:, None] * (
        scaled_rows
        - row_sum_total[:, None] / MODEL_WIDTH
        - centered_unit_rows * (crossed_product[:, None] / MODEL_WIDTH)
    )


def gather_cols(values):
    return lax.all_gather(values, "col", axis=0, tiled=True)


def gather_rows(values):
    return lax.all_gather(values, "row", axis=0, tiled=True)


def sum_rows(whole, weights, contract):
    row_share = whole.shape[0] // lax.axis_size("row")

    def partial_value(first_row, amount):
        return lax.dot_general(
            whole, weights, (((1,), (contract,)), ((), ())), preferred_element_type=jnp.float32
        )

    return lax.psum_scatter(
        partial_value(jnp.int32(0), row_share * lax.axis_size("row")),
        "row",
        scatter_dimension=0,
        tiled=True,
    )


def sum_cols(whole, weights, contract):
    row_share = whole.shape[0] // lax.axis_size("col")

    def partial_value(first_row, amount):
        return lax.dot_general(
            whole, weights, (((1,), (contract,)), ((), ())), preferred_element_type=jnp.float32
        )

    return lax.psum_scatter(
        partial_value(jnp.int32(0), row_share * lax.axis_size("col")),
        "col",
        scatter_dimension=0,
        tiled=True,
    )


def outer_tokens(left, right):
    return lax.dot_general(
        left, right, (((0,), (0,)), ((), ())), preferred_element_type=jnp.float32
    )


def rotary(segments):
    position_index = lax.broadcasted_iota(jnp.int32, segments.shape, 1)
    starts = jnp.concatenate(
        [jnp.ones_like(segments[:, :1]), (segments[:, 1:] != segments[:, :-1]).astype(jnp.int32)],
        axis=1,
    )
    first_index = lax.cummax(jnp.where(starts == 1, position_index, 0), axis=1)
    where_in = (position_index - first_index).astype(jnp.float32).reshape(-1)
    frequency = ROPE_THETA ** (-(jnp.arange(HEAD // 2, dtype=jnp.float32) * 2.0) / HEAD)
    angles = where_in[:, None] * frequency[None, :]
    return (jnp.cos(angles)[:, None, :], jnp.sin(angles)[:, None, :])


def rotate_half(values, cosine, sine_table):
    half_size = values.shape[-1] // 2
    first_half = values[..., :half_size]
    second = values[..., half_size:]
    return jnp.concatenate(
        [first_half * cosine - second * sine_table, second * cosine + first_half * sine_table],
        axis=-1,
    )


def rotate_back(values, cosine, sine_table):
    half_size = values.shape[-1] // 2
    first_half = values[..., :half_size]
    second = values[..., half_size:]
    return jnp.concatenate(
        [first_half * cosine + second * sine_table, second * cosine - first_half * sine_table],
        axis=-1,
    )


def geglu(acts):
    half_size = acts.shape[1] // 2
    return jax.nn.gelu(acts[:, :half_size], approximate=False) * acts[:, half_size:]


def window_setup(queries, key_rows, value_rows, segments, valid):
    seqs_dev, length, heads_dev, head_size = queries.shape
    half_window = WINDOW // 2
    block_rows = min(512, length)
    blocks = length // block_rows
    span_rows = block_rows + 2 * half_window
    spread = ((0, 0), (half_window, half_window), (0, 0), (0, 0))
    key_pad = jnp.pad(key_rows, spread)
    value_pad = jnp.pad(value_rows, spread)
    seg_pad = jnp.pad(segments, ((0, 0), (half_window, half_window)), constant_values=-1)
    valid_pad = jnp.pad(valid, ((0, 0), (half_window, half_window)))
    score_scale = head_size ** (-0.5)

    def block_scores(block_index):
        sequence = block_index // blocks
        first_row = block_index % blocks * block_rows
        q_block = lax.dynamic_slice(
            queries, (sequence, first_row, 0, 0), (1, block_rows, heads_dev, head_size)
        )[0]
        k_block = lax.dynamic_slice(
            key_pad, (sequence, first_row, 0, 0), (1, span_rows, heads_dev, head_size)
        )[0]
        v_block = lax.dynamic_slice(
            value_pad, (sequence, first_row, 0, 0), (1, span_rows, heads_dev, head_size)
        )[0]
        seg_query = lax.dynamic_slice(
            seg_pad, (sequence, first_row + half_window), (1, block_rows)
        )[0]
        seg_key = lax.dynamic_slice(seg_pad, (sequence, first_row), (1, span_rows))[0]
        valid_key = lax.dynamic_slice(valid_pad, (sequence, first_row), (1, span_rows))[0]
        offset = (
            lax.broadcasted_iota(jnp.int32, (block_rows, span_rows), 1)
            - half_window
            - lax.broadcasted_iota(jnp.int32, (block_rows, span_rows), 0)
        )
        allowed = (
            (jnp.abs(offset) <= half_window)
            & (seg_query[:, None] == seg_key[None, :])
            & ((valid_key[None, :] == 1) | (offset == 0))
        )
        raw_scores = (
            jnp.einsum("qhe,khe->hqk", q_block, k_block, preferred_element_type=jnp.float32)
            * score_scale
        )
        masked = jnp.where(allowed[None], raw_scores, MASKED_SCORE)
        return (masked, q_block, k_block, v_block, sequence, first_row)

    geometry = (
        seqs_dev,
        length,
        heads_dev,
        head_size,
        half_window,
        block_rows,
        blocks,
        span_rows,
        score_scale,
    )
    return (block_scores, key_pad, geometry)


def attend(queries, key_rows, value_rows, segments, valid):
    block_scores, key_pad, geometry = window_setup(queries, key_rows, value_rows, segments, valid)
    (
        seqs_dev,
        length,
        heads_dev,
        head_size,
        half_window,
        block_rows,
        blocks,
        span_rows,
        score_scale,
    ) = geometry

    def forward_block(block_index):
        masked, q_block, k_block, v_block, sequence, first_row = block_scores(block_index)
        row_max = jnp.max(masked, axis=-1, keepdims=True)
        exponent = jnp.exp(masked - row_max)
        row_sum_total = jnp.sum(exponent, axis=-1, keepdims=True)
        probability = (exponent / row_sum_total).astype(jnp.bfloat16)
        result = jnp.einsum(
            "hqk,khe->qhe", probability, v_block, preferred_element_type=jnp.float32
        ).astype(jnp.bfloat16)
        return (result, (row_max + jnp.log(row_sum_total))[..., 0])

    results, log_totals = lax.map(forward_block, jnp.arange(seqs_dev * blocks, dtype=jnp.int32))
    return (results.reshape(seqs_dev * length, heads_dev * head_size), log_totals)


def attend_back(queries, key_rows, value_rows, segments, valid, log_totals, grad_attended):
    block_scores, key_pad, geometry = window_setup(queries, key_rows, value_rows, segments, valid)
    (
        seqs_dev,
        length,
        heads_dev,
        head_size,
        half_window,
        block_rows,
        blocks,
        span_rows,
        score_scale,
    ) = geometry
    grad_rows = grad_attended.reshape(seqs_dev, length, heads_dev, head_size)
    key_span = (1, span_rows, heads_dev, head_size)

    def back_block(carried, block_index):
        key_grad, value_grad = carried
        masked, q_block, k_block, v_block, sequence, first_row = block_scores(block_index)
        weight = jnp.exp(masked - log_totals[block_index][..., None])
        g_block = lax.dynamic_slice(
            grad_rows, (sequence, first_row, 0, 0), (1, block_rows, heads_dev, head_size)
        )[0]
        d_weight = jnp.einsum("qhe,khe->hqk", g_block, v_block, preferred_element_type=jnp.float32)
        g_score = (weight * (d_weight - jnp.sum(weight * d_weight, axis=-1, keepdims=True))).astype(
            jnp.bfloat16
        )
        q_grad = (
            jnp.einsum("hqk,khe->qhe", g_score, k_block, preferred_element_type=jnp.float32)
            * score_scale
        )
        k_part = (
            jnp.einsum("hqk,qhe->khe", g_score, q_block, preferred_element_type=jnp.float32)
            * score_scale
        )
        v_part = jnp.einsum(
            "hqk,qhe->khe", weight.astype(jnp.bfloat16), g_block, preferred_element_type=jnp.float32
        )
        corner = (sequence, first_row, 0, 0)
        key_grad = lax.dynamic_update_slice(
            key_grad, lax.dynamic_slice(key_grad, corner, key_span) + k_part[None], corner
        )
        value_grad = lax.dynamic_update_slice(
            value_grad, lax.dynamic_slice(value_grad, corner, key_span) + v_part[None], corner
        )
        return ((key_grad, value_grad), q_grad)

    empty = jnp.zeros(key_pad.shape, jnp.float32)
    (key_grad, value_grad), q_grads = lax.scan(
        back_block, (empty, empty), jnp.arange(seqs_dev * blocks, dtype=jnp.int32)
    )
    key_grad = key_grad[:, half_window : half_window + length].reshape(
        seqs_dev * length, heads_dev, head_size
    )
    value_grad = value_grad[:, half_window : half_window + length].reshape(
        seqs_dev * length, heads_dev * head_size
    )
    return (q_grads.reshape(seqs_dev * length, heads_dev, head_size), key_grad, value_grad)


def body(
    tokens,
    w_query,
    w_key,
    w_value,
    w_out,
    w_act,
    w_gate,
    w_down,
    gain_attn,
    gain_ffn,
    cotangent,
    segment_ids,
    valid_mask,
):
    source_input = tokens.astype(jnp.float32)
    leading_gain = gain_attn.astype(jnp.float32)
    trailing_gain = gain_ffn.astype(jnp.float32)
    attention_centered_unit, attention_inverse_norm = apply_norm(source_input)
    attention_normed_input = (attention_centered_unit * leading_gain[None, :]).astype(jnp.bfloat16)
    attn_cols = gather_cols(attention_normed_input)
    proj_weights = jnp.concatenate([w_query, w_key, w_value], axis=1)
    projected = sum_rows(attn_cols, proj_weights, 0)
    head_width = w_query.shape[1]
    heads_dev = head_width // HEAD
    seqs_dev, length = segment_ids.shape
    cosine, sine_table = rotary(segment_ids)
    queries = rotate_half(
        projected[:, :head_width].reshape(-1, heads_dev, HEAD), cosine, sine_table
    ).astype(jnp.bfloat16)
    key_rows = rotate_half(
        projected[:, head_width : 2 * head_width].reshape(-1, heads_dev, HEAD), cosine, sine_table
    ).astype(jnp.bfloat16)
    value_rows = projected[:, 2 * head_width :].astype(jnp.bfloat16)
    queries = queries.reshape(seqs_dev, length, heads_dev, HEAD)
    key_rows = key_rows.reshape(seqs_dev, length, heads_dev, HEAD)
    value_rows = value_rows.reshape(seqs_dev, length, heads_dev, HEAD)
    attended, log_totals = attend(queries, key_rows, value_rows, segment_ids, valid_mask)
    attended_all = gather_rows(attended)
    residual_mixed_state = source_input + sum_cols(attended_all, w_out, 0)
    feedforward_centered_unit, feedforward_inverse_norm = apply_norm(residual_mixed_state)
    feedforward_normed_input = (feedforward_centered_unit * trailing_gain[None, :]).astype(
        jnp.bfloat16
    )
    hidden_width = w_act.shape[1]
    act_gate = jnp.concatenate([w_act, w_gate], axis=1)
    ffn_cols = gather_cols(feedforward_normed_input)
    acts = sum_rows(ffn_cols, act_gate, 0)
    hidden, pullback = jax.vjp(geglu, acts)
    hidden_all = gather_rows(hidden.astype(jnp.bfloat16))
    ffn_out = sum_cols(hidden_all, w_down, 0)
    grad_cols = gather_cols(cotangent)
    grad_down = outer_tokens(hidden_all, grad_cols)
    g_hidden = sum_rows(grad_cols, w_down, 1)
    g_acts = pullback(g_hidden)[0].astype(jnp.bfloat16)
    g_acts_all = gather_rows(g_acts)
    paired = outer_tokens(ffn_cols, g_acts_all)
    grad_act = paired[:, :hidden_width]
    grad_gate = paired[:, hidden_width:]
    feedforward_normed_gradient = sum_cols(g_acts_all, act_gate, 1)
    layer_out = (residual_mixed_state + ffn_out).astype(jnp.bfloat16)
    feedforward_gain_part = jnp.sum(feedforward_normed_gradient * feedforward_centered_unit, axis=0)
    mixed_gradient = cotangent.astype(jnp.float32) + norm_backward(
        feedforward_normed_gradient,
        feedforward_centered_unit,
        feedforward_inverse_norm,
        trailing_gain,
    )
    branch_cols = gather_cols(mixed_gradient.astype(jnp.bfloat16))
    grad_out = outer_tokens(attended_all, branch_cols)
    g_attended = sum_rows(branch_cols, w_out, 1).astype(jnp.bfloat16)
    q_grad, k_grad, v_grad = attend_back(
        queries, key_rows, value_rows, segment_ids, valid_mask, log_totals, g_attended
    )
    g_query = rotate_back(q_grad, cosine, sine_table).reshape(-1, head_width)
    g_key = rotate_back(k_grad, cosine, sine_table).reshape(-1, head_width)
    g_proj = jnp.concatenate([g_query, g_key, v_grad], axis=1).astype(jnp.bfloat16)
    g_proj_all = gather_rows(g_proj)
    grad_proj = outer_tokens(attn_cols, g_proj_all)
    attention_normed_gradient = sum_cols(g_proj_all, proj_weights, 1)
    attention_gain_part = jnp.sum(attention_normed_gradient * attention_centered_unit, axis=0)
    token_gradient = mixed_gradient + norm_backward(
        attention_normed_gradient, attention_centered_unit, attention_inverse_norm, leading_gain
    )
    summed = (
        lax.psum(grad_proj[:, :head_width].astype(jnp.bfloat16), "dp").astype(jnp.float32),
        lax.psum(grad_proj[:, head_width : 2 * head_width].astype(jnp.bfloat16), "dp").astype(
            jnp.float32
        ),
        lax.psum(grad_proj[:, 2 * head_width :].astype(jnp.bfloat16), "dp").astype(jnp.float32),
        lax.psum(grad_out.astype(jnp.bfloat16), "dp").astype(jnp.float32),
        lax.psum(grad_act.astype(jnp.bfloat16), "dp").astype(jnp.float32),
        lax.psum(grad_gate.astype(jnp.bfloat16), "dp").astype(jnp.float32),
        lax.psum(grad_down.astype(jnp.bfloat16), "dp").astype(jnp.float32),
    )
    gain_totals = lax.psum((attention_gain_part, feedforward_gain_part), ("dp", "col"))
    return (
        layer_out,
        token_gradient,
        summed[0],
        summed[1],
        summed[2],
        summed[3],
        summed[4],
        summed[5],
        summed[6],
        gain_totals[0],
        gain_totals[1],
    )


def solution(mesh):
    in_specs = (
        P(("dp", "col"), "row"),
        P("row", "col"),
        P("row", "col"),
        P("row", "col"),
        P("col", "row"),
        P("row", "col"),
        P("row", "col"),
        P("col", "row"),
        P("row"),
        P("row"),
        P(("dp", "col"), "row"),
        P(("dp", "row"), None),
        P(("dp", "row"), None),
    )
    out_specs = (
        P(("dp", "col"), "row"),
        P(("dp", "col"), "row"),
        P("row", "col"),
        P("row", "col"),
        P("row", "col"),
        P("col", "row"),
        P("row", "col"),
        P("row", "col"),
        P("col", "row"),
        P("row"),
        P("row"),
    )
    return jax.shard_map(body, mesh=mesh, in_specs=in_specs, out_specs=out_specs, check_vma=False)
```

profile of v0, /device:TPU:0, one launch (start us, length us, event | category | flops | bytes accessed | tf_op | source)
XLA Modules:
  0.0 6375.9 jit_solution(10855780097400951504)
XLA Ops:
  35.8 56.5 all-gather.9.cloned.1.call-done
  118.0 816.9 %reduce-scatter.9.cloned.1.call-done = f32[4096,768]{1,0:T(8,128)} async-done(((f32[16384,768]{1,0:T(8,128)}), f32[4096,768]{1,0:T(8,128)}) %reduce-scatter.9.cloned.1.call-update) | async-done | bytes 12582928 | tf_op jit(solution)/shard_map/reduce_scatter | solution.py:54
  968.5 89.9 %while.30 = (s32[]{:T(128)}, bf16[8,512,4,64]{1,3,2,0:T(8,128)(2,1)}, f32[8,4,512]{2,1,0:T(4,128)}, s32[8]{0:T(128)S(1)}, bf16[1,4224,4,64]{1,3,2,0:T(8,128)(2,1...) while((s32[]{:T(128)}, ...), condition=%wide.region_10.11_spmd, body=%wide.region_7.10_spmd.sunk | while | flops 354024704 | bytes 18308780 | solution.py:208
  1064.5 151.6 %all-gather.11.cloned.1.call-done = bf16[16384,256]{0,1:T(8,128)(2,1)} async-done(((bf16[4096,256]{0,1:T(8,128)(2,1)}), bf16[16384,256]{0,1:T(8,128)(2,1)}) %all-gather.11.cloned.1.call-update) | async-done | bytes 8388624 | tf_op jit(solution)/shard_map/all_gather | solution.py:43
  1228.4 123.8 %reduce-scatter.11.cloned.1.call-done = f32[4096,256]{1,0:T(8,128)} async-done(((f32[16384,256]{1,0:T(8,128)}), f32[4096,256]{1,0:T(8,128)}) %reduce-scatter.11.cloned.1.call-update) | async-done | bytes 4194320 | tf_op jit(solution)/shard_map/reduce_scatter | solution.py:70
  1380.7 31.3 all-gather.17.cloned.1.call-done
  1411.9 22.8 fusion.106
  1435.9 36.4 all-gather.13.cloned.1.call-done
  1472.2 34.2 fusion.104
  1506.8 671.0 %reduce-scatter.17.cloned.1.call-done = f32[4096,656]{0,1:T(8,128)} async-done(((f32[16384,656]{0,1:T(8,128)}), f32[4096,656]{0,1:T(8,128)}) %reduce-scatter.17.cloned.1.call-update) | async-done | bytes 10747920 | tf_op jit(solution)/shard_map/reduce_scatter | solution.py:54
  2177.8 1402.2 %reduce-scatter.13.cloned.1.call-done = f32[4096,1312]{0,1:T(8,128)} async-done(((f32[16384,1312]{0,1:T(8,128)}), f32[4096,1312]{0,1:T(8,128)}) %reduce-scatter.13.cloned.1.call-update) | async-done | bytes 21495824 | tf_op jit(solution)/shard_map/reduce_scatter | solution.py:54
  3580.0 26.6 fusion.86
  3635.4 717.8 %all-gather.19.cloned.1.call-done = bf16[16384,1312]{0,1:T(8,128)(2,1)} async-done(((bf16[4096,1312]{0,1:T(8,128)(2,1)}), bf16[16384,1312]{0,1:T(8,128)(2,1)}) %all-gather.19.cloned.1.call-update) | async-done | bytes 42991632 | tf_op jit(solution)/shard_map/all_gather | solution.py:43
  4353.3 26.7 fusion.107
  4380.4 337.9 %all-gather.15.cloned.1.call-done = bf16[16384,656]{0,1:T(8,128)(2,1)} async-done(((bf16[4096,656]{0,1:T(8,128)(2,1)}), bf16[16384,656]{0,1:T(8,128)(2,1)}) %all-gather.15.cloned.1.call-update) | async-done | bytes 21495824 | tf_op jit(solution)/shard_map/all_gather | solution.py:43
  4735.8 109.7 %reduce-scatter.19.cloned.1.call-done = f32[4096,256]{1,0:T(8,128)} async-done(((f32[16384,256]{1,0:T(8,128)}), f32[4096,256]{1,0:T(8,128)}) %reduce-scatter.19.cloned.1.call-update) | async-done | bytes 4194320 | tf_op jit(solution)/shard_map/reduce_scatter | solution.py:70
  4869.8 104.5 %reduce-scatter.15.cloned.1.call-done = f32[4096,256]{1,0:T(8,128)} async-done(((f32[16384,256]{1,0:T(8,128)}), f32[4096,256]{1,0:T(8,128)}) %reduce-scatter.15.cloned.1.call-update) | async-done | bytes 4194320 | tf_op jit(solution)/shard_map/reduce_scatter | solution.py:70
  4983.4 58.4 all-gather.21.cloned.1.call-done
  5053.4 280.4 %reduce-scatter.21.cloned.1.call-done = f32[4096,256]{1,0:T(8,128)} async-done(((f32[16384,256]{1,0:T(8,128)}), f32[4096,256]{1,0:T(8,128)}) %reduce-scatter.21.cloned.1.call-update) | async-done | bytes 4194320 | tf_op jit(solution)/shard_map/reduce_scatter | solution.py:54
  5343.9 338.4 %while.31 = (s32[]{:T(128)}, f32[1,4224,4,64]{1,3,2,0:T(8,128)}, f32[1,4224,4,64]{1,3,2,0:T(8,128)}, f32[8,512,4,64]{1,0,3,2:T(8,128)}, s32[8]{0:T(128)S(1)}, /*...) while((s32[]{:T(128)}, f32[1,4224,4,64]{1,3,2,0:T(8,128)}, ...), condition=%wide.region_27.28_spmd, body=%wide.region_25.27_spmd.sunk | while | flops 861764864 | bytes 74201920 | solution.py:260
  5720.2 23.8 convolution_convert_fusion
  5753.8 377.5 %all-gather.23.cloned.1.call-done = bf16[16384,768]{0,1:T(8,128)(2,1)} async-done(((bf16[4096,768]{0,1:T(8,128)(2,1)}), bf16[16384,768]{0,1:T(8,128)(2,1)}) %all-gather.23.cloned.1.call-update) | async-done | bytes 25165840 | tf_op jit(solution)/shard_map/all_gather | solution.py:43
  6162.0 34.4 all-reduce.14.cloned.1.call-done
  6208.6 116.7 %reduce-scatter.23.cloned.1.call-done = f32[4096,256]{1,0:T(8,128)} async-done(((f32[16384,256]{1,0:T(8,128)}), f32[4096,256]{1,0:T(8,128)}) %reduce-scatter.23.cloned.1.call-update) | async-done | bytes 4194320 | tf_op jit(solution)/shard_map/reduce_scatter | solution.py:70
  (454 shorter events, 757.6 us)
Async XLA Ops:
  7.2 1404.8 %copy-start = (bf16[656,256]{1,0:T(8,128)(2,1)S(1)}, bf16[656,256]{1,0:T(8,128)(2,1)}, u32[]{:S(2)}) copy-start(bf16[656,256]{1,0:T(8,128)(2,1)} %param.24) | copy-start | bytes 1007620
  7.2 85.1 %all-gather.9.cloned.1.call-start = ((), (), s32[]{:S(2)}) async-start(), calls=%async_computation.8 | async-start | bytes 10485760 | tf_op jit(solution)/shard_map/all_gather | solution.py:39
  35.7 899.2 %reduce-scatter.9.cloned.1.call-start = ((), (), s32[]{:S(2)}) async-start(), calls=%async_computation.9 | async-start | bytes 62914560 | tf_op jit(solution)/shard_map/reduce_scatter | solution.py:54
  114.1 1102.1 %all-gather.11.cloned.1.call-start = ((), (), s32[]{:S(2)}) async-start(), calls=%async_computation.10 | async-start | bytes 10485760 | tf_op jit(solution)/shard_map/all_gather | solution.py:43
  117.9 841.3 %copy-start.10 = (f32[4096,32]{0,1:T(8,128)}, f32[4096,32]{0,1:T(8,128)S(1)}, u32[]{:S(2)}) copy-start(f32[4096,32]{0,1:T(8,128)S(1)} %get-tuple-element.399) | copy-start | bytes 1572868
  117.9 841.3 %copy-start.12 = (f32[4096,32]{0,1:T(8,128)}, f32[4096,32]{0,1:T(8,128)S(1)}, u32[]{:S(2)}) copy-start(f32[4096,32]{0,1:T(8,128)S(1)} %get-tuple-element.400) | copy-start | bytes 1572868
  1064.3 287.9 %reduce-scatter.11.cloned.1.call-start = ((), (), s32[]{:S(2)}) async-start(), calls=%async_computation.11 | async-start | bytes 20971520 | tf_op jit(solution)/shard_map/reduce_scatter | solution.py:70
  1227.7 184.2 %all-gather.17.cloned.1.call-start = ((), (), s32[]{:S(2)}) async-start(), calls=%async_computation.16 | async-start | bytes 10485760 | tf_op jit(solution)/shard_map/all_gather | solution.py:39
  1228.3 243.9 %all-gather.13.cloned.1.call-start = ((), (), s32[]{:S(2)}) async-start(), calls=%async_computation.12 | async-start | bytes 10485760 | tf_op jit(solution)/shard_map/all_gather | solution.py:39
  1380.6 797.2 %reduce-scatter.17.cloned.1.call-start = ((), (), s32[]{:S(2)}) async-start(), calls=%async_computation.17 | async-start | bytes 53739520 | tf_op jit(solution)/shard_map/reduce_scatter | solution.py:54
  1434.8 2145.2 %reduce-scatter.13.cloned.1.call-start = ((), (), s32[]{:S(2)}) async-start(), calls=%async_computation.13 | async-start | bytes 107479040 | tf_op jit(solution)/shard_map/reduce_scatter | solution.py:54
  1506.5 2846.7 %all-gather.19.cloned.1.call-start = ((), (), s32[]{:S(2)}) async-start(), calls=%async_computation.18 | async-start | bytes 53739520 | tf_op jit(solution)/shard_map/all_gather | solution.py:43
  3634.8 1083.5 %all-gather.15.cloned.1.call-start = ((), (), s32[]{:S(2)}) async-start(), calls=%async_computation.14 | async-start | bytes 26869760 | tf_op jit(solution)/shard_map/all_gather | solution.py:43
  3635.4 1210.1 %reduce-scatter.19.cloned.1.call-start = ((), (), s32[]{:S(2)}) async-start(), calls=%async_computation.19 | async-start | bytes 20971520 | tf_op jit(solution)/shard_map/reduce_scatter | solution.py:70
  4379.9 594.4 %reduce-scatter.15.cloned.1.call-start = ((), (), s32[]{:S(2)}) async-start(), calls=%async_computation.15 | async-start | bytes 20971520 | tf_op jit(solution)/shard_map/reduce_scatter | solution.py:70
  4735.8 238.6 %copy-start.8 = (bf16[4096,256]{1,0:T(8,128)(2,1)S(1)}, bf16[4096,256]{1,0:T(8,128)(2,1)}, u32[]{:S(2)}) copy-start(bf16[4096,256]{1,0:T(8,128)(2,1)} %param.27) | copy-start | bytes 6291460
  4735.8 306.0 %all-gather.21.cloned.1.call-start = ((), (), s32[]{:S(2)}) async-start(), calls=%async_computation.20 | async-start | bytes 10485760 | tf_op jit(solution)/shard_map/all_gather | solution.py:39
  4983.3 350.5 %reduce-scatter.21.cloned.1.call-start = ((), (), s32[]{:S(2)}) async-start(), calls=%async_computation.21 | async-start | bytes 20971520 | tf_op jit(solution)/shard_map/reduce_scatter | solution.py:54
  5053.4 1077.9 %all-gather.23.cloned.1.call-start = ((), (), s32[]{:S(2)}) async-start(), calls=%async_computation.22 | async-start | bytes 31457280 | tf_op jit(solution)/shard_map/all_gather | solution.py:43
  5705.2 491.2 %all-reduce.14.cloned.1.call-start = ((), (), s32[]{:S(2)}) async-start(), calls=%async_computation.24 | async-start | bytes 3063808 | tf_op jit(solution)/shard_map/psum | solution.py:357
  5753.8 392.7 %copy-start.15 = (bf16[256,768]{1,0:T(8,128)(2,1)S(1)}, bf16[256,768]{1,0:T(8,128)(2,1)}, u32[]{:S(2)}) copy-start(bf16[256,768]{1,0:T(8,128)(2,1)} %copy-done.14) | copy-start | bytes 1179652
  6146.4 178.9 %reduce-scatter.23.cloned.1.call-start = ((), (), s32[]{:S(2)}) async-start(), calls=%async_computation.23 | async-start | bytes 20971520 | tf_op jit(solution)/shard_map/reduce_scatter | solution.py:70
  6162.0 163.4 %copy-start.4 = (bf16[4096,256]{1,0:T(8,128)(2,1)S(1)}, bf16[4096,256]{1,0:T(8,128)(2,1)}, u32[]{:S(2)}) copy-start(bf16[4096,256]{1,0:T(8,128)(2,1)} %param.17) | copy-start | bytes 6291460
  6162.0 163.4 %copy-start.21 = (f32[4096]{0:T(1024)S(1)}, f32[4096]{0:T(1024)}, u32[]{:S(2)}) copy-start(f32[4096]{0:T(1024)} %copy-done.20) | copy-start | bytes 49156
  (57 other events, 1685.6 us)
Sparse Core Ops, SparseCore 0:
  35.8 56.5 all-gather.8
  114.2 820.6 reduce-scatter.8
  1064.4 151.6 all-gather.10
  1227.9 124.3 reduce-scatter.10
  1353.6 58.2 all-gather.16
  1413.9 58.2 all-gather.12
  1474.6 703.1 reduce-scatter.16
  2180.2 1399.7 reduce-scatter.12
  3634.9 718.2 all-gather.18
  4354.7 363.5 all-gather.14
  4720.9 124.6 reduce-scatter.18
  4848.1 126.1 reduce-scatter.14
  4983.5 58.2 all-gather.20
  5053.5 280.2 reduce-scatter.20
  5705.3 425.8 all-gather.22
  6146.6 49.7 all-reduce.13
  6199.0 126.2 reduce-scatter.22
where the time goes:
time: 6390 us; the launch traced here: 6380 us
  waiting for transfers between devices  5430 us (85%)
  matrix products  428 us (7%)
  local copies, waits for them, and re-layouts  193 us (3%)
  other arithmetic  178 us (3%)
  blocking collectives  90.2 us (1%)
    reduce_scatter x4, waiting for transfers between devices, sum_rows(): lax.psum_scatter(partial_value(jnp.int32(0), row_share * lax.axis_size('r...  3170 us
    all_gather x4, waiting for transfers between devices, gather_rows(): return lax.all_gather(values, 'row', axis=0, tiled=True)  1580 us
    reduce_scatter x4, waiting for transfers between devices, sum_cols(): lax.psum_scatter(partial_value(jnp.int32(0), row_share * lax.axis_size('c...  455 us
    all_gather x4, waiting for transfers between devices, gather_cols(): return lax.all_gather(values, 'col', axis=0, tiled=True)  183 us
    dot_general x8, matrix products, partial_value(): lax.dot_general(whole, weights, (((1,), (contract,)), ((), ())), preferre...  161 us
  transfers between devices with their start and end apart: 17, of which 17 were waited for; matrix products, arithmetic and copies ran while one was open for 3% of the time, Pallas kernels for 0%

commit v1 on v0

v1 whole, which is shorter than its diff:
```python
import functools
import math

import jax
import jax.numpy as jnp
from jax import lax
from jax.experimental import pallas as pl
from jax.experimental.pallas import tpu as pltpu
from jax.sharding import PartitionSpec as P

WIDTH = 1024
HEAD = 64
REACH = 64
EPSILON = 1e-05
ROPE_THETA = 10000.0
MASKED_SCORE = -1e30
LANES = 128
SLOTS = 4
GROUPS = 4
GROUP = 256
TILE = 256
QUERY = 128
VMEM = 60 * 1024 * 1024
F32 = jnp.float32
BF16 = jnp.bfloat16


def nt(left, right):
    return lax.dot_general(left, right, (((1,), (1,)), ((), ())), preferred_element_type=F32)


def nn(left, right):
    return lax.dot_general(left, right, (((1,), (0,)), ((), ())), preferred_element_type=F32)


def tn(left, right):
    return lax.dot_general(left, right, (((0,), (0,)), ((), ())), preferred_element_type=F32)


def call(kernel, grid, in_specs, out_specs, out_shape, scratch, flops, moved, name):
    return pl.pallas_call(
        kernel,
        grid=grid,
        in_specs=in_specs,
        out_specs=out_specs,
        out_shape=out_shape,
        scratch_shapes=scratch,
        compiler_params=pltpu.CompilerParams(
            vmem_limit_bytes=VMEM, dimension_semantics=("arbitrary",)
        ),
        cost_estimate=pl.CostEstimate(flops=flops, bytes_accessed=moved, transcendentals=0),
        name=name,
    )


def resident(shape):
    zeros = (0,) * len(shape)
    return pl.BlockSpec(shape, lambda i: zeros, pipeline_mode=pl.Buffered(1))


def rows_of(width, tile=TILE):
    return pl.BlockSpec((tile, width), lambda i: (i, 0))


def struct(shape, dtype):
    return jax.ShapeDtypeStruct(shape, dtype)


def lane_block(a, o):
    return pl.ds(a * SLOTS * LANES + o * LANES, LANES)


def whole_rows(slots):
    return jnp.concatenate(
        [slots[o][:, a * LANES : (a + 1) * LANES] for a in range(2) for o in range(SLOTS)], axis=1
    )


def place(pieces, target, first, rows, start):
    for p in range(GROUPS):
        for a in range(2):
            for o in range(SLOTS):
                target[pl.ds(start + p * rows, rows), lane_block(a, o)] = pieces[a * GROUPS + p][
                    o, pl.ds(first, rows), :
                ]


def norm(values):
    average = jnp.mean(values, axis=1, keepdims=True)
    centered = values - average
    variance = jnp.mean(centered * centered, axis=1, keepdims=True)
    inverse = lax.rsqrt(variance + EPSILON)
    return centered * inverse, inverse


def norm_back(gradient, unit, inverse, gain):
    scaled = gradient * gain
    average = jnp.mean(scaled, axis=1, keepdims=True)
    crossed = jnp.mean(scaled * unit, axis=1, keepdims=True)
    return inverse * (scaled - average - unit * crossed)


def add_gain(gain_part, products):
    @pl.when(pl.program_id(0) == 0)
    def _():
        gain_part[...] = jnp.zeros_like(gain_part)

    gain_part[...] += jnp.sum(products.reshape(-1, 8, WIDTH), axis=0)


def qkv_kernel(*refs):
    xs, (gain, cosine, sine), pieces = refs[:4], refs[4:7], refs[7:15]
    q, k, v, normed, held = refs[15:]

    @pl.when(pl.program_id(0) == 0)
    def _():
        for t in range(3):
            place(pieces, held, t * GROUP, GROUP, t * WIDTH)

    unit, _ = norm(whole_rows(xs).astype(F32))
    rows = (unit * gain[...]).astype(BF16)
    normed[...] = rows
    c, s = cosine[...], sine[...]
    for t, out in ((0, q), (1, k)):
        made = nt(rows, held[pl.ds(t * WIDTH, WIDTH), :])
        for p in range(GROUPS):
            first = made[:, p * GROUP : p * GROUP + LANES]
            second = made[:, p * GROUP + LANES : (p + 1) * GROUP]
            out[:, p * GROUP : p * GROUP + LANES] = (first * c - second * s).astype(BF16)
            out[:, p * GROUP + LANES : (p + 1) * GROUP] = (second * c + first * s).astype(BF16)
    v[...] = nt(rows, held[pl.ds(2 * WIDTH, WIDTH), :]).astype(BF16)


def project(xs, gain, cosine, sine, pieces):
    tokens = cosine.shape[0]
    return call(
        qkv_kernel,
        (tokens // TILE,),
        [rows_of(256)] * 4
        + [resident((1, WIDTH)), rows_of(LANES), rows_of(LANES)]
        + [resident((SLOTS, 3 * GROUP, LANES))] * 8,
        [rows_of(WIDTH)] * 4,
        [struct((tokens, WIDTH), BF16)] * 4,
        [pltpu.VMEM((3 * WIDTH, WIDTH), BF16)],
        2 * tokens * WIDTH * 3 * WIDTH,
        10 * tokens * WIDTH + 6 * WIDTH * WIDTH,
        "project",
    )(*xs, gain, cosine, sine, *pieces)


def head_masks():
    lane = lax.broadcasted_iota(jnp.int32, (1, GROUP), 1)
    halves = [((lane % LANES) // 32 == h) for h in range(4)]
    wholes = [(lane // HEAD == h) for h in range(4)]
    return halves, wholes


def spread(rows, masks):
    return jnp.concatenate([rows * m.astype(BF16) for m in masks], axis=0)


def collect(stacked, masks):
    total = jnp.where(masks[0], stacked[0:QUERY], 0.0)
    for h in range(1, 4):
        total = jnp.where(masks[h], stacked[h * QUERY : (h + 1) * QUERY], total)
    return total


def fill_span(span, low, own, high):
    count = own.shape[0]
    span[0:REACH, :] = low
    span[pl.ds(REACH, count), :] = own[...]
    span[pl.ds(REACH + count, REACH), :] = high


def attend_kernel(q, k, v, low, high, seg_query, seg_key, attended, probability, keys, values):
    step = pl.program_id(0)

    @pl.when(step == 0)
    def _():
        fill_span(keys, low[:, :WIDTH], k, high[:, :WIDTH])
        fill_span(values, low[:, WIDTH:], v, high[:, WIDTH:])

    span = pl.ds(pl.multiple_of(step * QUERY, QUERY), QUERY + 2 * REACH)
    shape = (QUERY, QUERY + 2 * REACH)
    offset = (
        lax.broadcasted_iota(jnp.int32, shape, 1)
        - lax.broadcasted_iota(jnp.int32, shape, 0)
        - REACH
    )
    allowed = (jnp.abs(offset) <= REACH) & ((seg_query[...] == seg_key[0]) | (offset == 0))
    halves, wholes = head_masks()
    for p in range(GROUPS):
        lanes = slice(p * GROUP, (p + 1) * GROUP)
        stacked = spread(q[:, lanes], halves)
        scores = nt(stacked, keys[span, lanes]) * HEAD**-0.5
        scores = jnp.concatenate(
            [
                jnp.where(allowed, scores[h * QUERY : (h + 1) * QUERY], MASKED_SCORE)
                for h in range(4)
            ],
            axis=0,
        )
        exponent = jnp.exp(scores - jnp.max(scores, axis=1, keepdims=True))
        weight = (exponent * (1.0 / jnp.sum(exponent, axis=1, keepdims=True))).astype(BF16)
        probability[0, p] = weight
        attended[:, lanes] = collect(nn(weight, values[span, lanes]), wholes).astype(BF16)


def attend(q, k, v, low, high, seg_query, seg_key):
    tokens = q.shape[0]
    blocks = tokens // QUERY
    span = QUERY + 2 * REACH
    full = resident((tokens, WIDTH))
    return call(
        attend_kernel,
        (blocks,),
        [
            rows_of(WIDTH, QUERY),
            full,
            full,
            resident((REACH, 2 * WIDTH)),
            resident((REACH, 2 * WIDTH)),
            rows_of(1, QUERY),
            pl.BlockSpec((1, 1, span), lambda i: (i, 0, 0)),
        ],
        [
            rows_of(WIDTH, QUERY),
            pl.BlockSpec((1, GROUPS, 4 * QUERY, span), lambda i: (i, 0, 0, 0)),
        ],
        [
            struct((tokens, WIDTH), BF16),
            struct((blocks, GROUPS, 4 * QUERY, span), BF16),
        ],
        [pltpu.VMEM((tokens + 2 * REACH, WIDTH), BF16)] * 2,
        blocks * GROUPS * 2 * 2 * 4 * QUERY * span * GROUP,
        8 * tokens * WIDTH + blocks * GROUPS * 8 * QUERY * span,
        "attend",
    )(q, k, v, low, high, seg_query, seg_key)


def attend_back_kernel(*refs):
    q, grad, weights, k, v, low, high, cosine, sine = refs[:9]
    gq, gk, gv, edge_k, edge_v, keys, values, sum_k, sum_v, every_c, every_s = refs[9:]
    step, steps = pl.program_id(0), pl.num_programs(0)
    tokens = k.shape[0]

    @pl.when(step == 0)
    def _():
        fill_span(keys, low[:, :WIDTH], k, high[:, :WIDTH])
        fill_span(values, low[:, WIDTH:], v, high[:, WIDTH:])
        sum_k[...] = jnp.zeros_like(sum_k)
        sum_v[...] = jnp.zeros_like(sum_v)

    start = pl.multiple_of(step * QUERY, QUERY)
    span = pl.ds(start, QUERY + 2 * REACH)
    halves, wholes = head_masks()
    c, s = cosine[...], sine[...]
    every_c[pl.ds(start, QUERY), :] = c
    every_s[pl.ds(start, QUERY), :] = s
    for p in range(GROUPS):
        lanes = slice(p * GROUP, (p + 1) * GROUP)
        queries = spread(q[:, lanes], halves)
        grads = spread(grad[:, lanes], wholes)
        block_k, block_v = keys[span, lanes], values[span, lanes]
        weight = weights[0, p]
        wide = weight.astype(F32)
        d_weight = nt(grads, block_v)
        mean = jnp.sum(wide * d_weight, axis=1, keepdims=True)
        g_score = (wide * (d_weight - mean)).astype(BF16)
        made = collect(nn(g_score, block_k), halves) * HEAD**-0.5
        first, second = made[:, :LANES], made[:, LANES:]
        gq[:, p * GROUP : p * GROUP + LANES] = (first * c + second * s).astype(BF16)
        gq[:, p * GROUP + LANES : (p + 1) * GROUP] = (second * c - first * s).astype(BF16)
        sum_k[span, lanes] += tn(g_score, queries) * HEAD**-0.5
        sum_v[span, lanes] += tn(weight, grads)

    @pl.when(step == steps - 1)
    def _():
        for edge, total in ((edge_k, sum_k), (edge_v, sum_v)):
            edge[0 : 2 * REACH, :] = total[0 : 2 * REACH, :]
            edge[2 * REACH :, :] = total[pl.ds(tokens, 2 * REACH), :]
        for at in range(0, tokens, QUERY):
            own = pl.ds(REACH + at, QUERY)
            c, s = every_c[pl.ds(at, QUERY), :], every_s[pl.ds(at, QUERY), :]
            for p in range(GROUPS):
                one, two = p * GROUP, p * GROUP + LANES
                first, second = sum_k[own, pl.ds(one, LANES)], sum_k[own, pl.ds(two, LANES)]
                gk[pl.ds(at, QUERY), pl.ds(one, LANES)] = (first * c + second * s).astype(BF16)
                gk[pl.ds(at, QUERY), pl.ds(two, LANES)] = (second * c - first * s).astype(BF16)
            gv[pl.ds(at, QUERY), :] = sum_v[own, :].astype(BF16)


def attend_back(q, grad, weights, k, v, low, high, cosine, sine):
    tokens = q.shape[0]
    blocks = tokens // QUERY
    span = QUERY + 2 * REACH
    full = resident((tokens, WIDTH))
    edge = resident((4 * REACH, WIDTH))
    return call(
        attend_back_kernel,
        (blocks,),
        [
            rows_of(WIDTH, QUERY),
            rows_of(WIDTH, QUERY),
            pl.BlockSpec((1, GROUPS, 4 * QUERY, span), lambda i: (i, 0, 0, 0)),
            full,
            full,
            resident((REACH, 2 * WIDTH)),
            resident((REACH, 2 * WIDTH)),
            rows_of(LANES, QUERY),
            rows_of(LANES, QUERY),
        ],
        [rows_of(WIDTH, QUERY), full, full, edge, edge],
        [struct((tokens, WIDTH), BF16)] * 3 + [struct((4 * REACH, WIDTH), F32)] * 2,
        [pltpu.VMEM((tokens + 2 * REACH, WIDTH), BF16)] * 2
        + [pltpu.VMEM((tokens + 2 * REACH, WIDTH), F32)] * 2
        + [pltpu.VMEM((tokens, LANES), F32)] * 2,
        blocks * GROUPS * 2 * 4 * 4 * QUERY * span * GROUP,
        14 * tokens * WIDTH + blocks * GROUPS * 8 * QUERY * span,
        "attend_back",
    )(q, grad, weights, k, v, low, high, cosine, sine)


def mix_kernel(*refs):
    xs, (attended, gain), pieces = refs[:4], refs[4:6], refs[6:14]
    mixed, normed, held = refs[14:]

    @pl.when(pl.program_id(0) == 0)
    def _():
        place(pieces, held, 0, GROUP, 0)

    total = whole_rows(xs).astype(F32) + nn(attended[...], held[...])
    mixed[...] = total
    normed[...] = (norm(total)[0] * gain[...]).astype(BF16)


def mix(xs, attended, gain, pieces):
    tokens = attended.shape[0]
    return call(
        mix_kernel,
        (tokens // TILE,),
        [rows_of(256)] * 4
        + [rows_of(WIDTH), resident((1, WIDTH))]
        + [resident((SLOTS, GROUP, LANES))] * 8,
        [rows_of(WIDTH)] * 2,
        [struct((tokens, WIDTH), F32), struct((tokens, WIDTH), BF16)],
        [pltpu.VMEM((WIDTH, WIDTH), BF16)],
        2 * tokens * WIDTH * WIDTH,
        10 * tokens * WIDTH + 2 * WIDTH * WIDTH,
        "mix",
    )(*xs, attended, gain, *pieces)


def feed_kernel(*refs):
    normed, mixed = refs[:2]
    up, down = refs[2:10], refs[10:18]
    outs = refs[18:22]
    hidden, slope, gelu, held_up, held_down = refs[22:]
    ff = hidden.shape[2]

    @pl.when(pl.program_id(0) == 0)
    def _():
        place(up, held_up, 0, ff, 0)
        place(up, held_up, ff, ff, GROUPS * ff)
        place(down, held_down, 0, ff, 0)

    rows = normed[...]
    total = mixed[...]
    for p in range(GROUPS):
        act = nt(rows, held_up[pl.ds(p * ff, ff), :])
        gate = nt(rows, held_up[pl.ds((GROUPS + p) * ff, ff), :])
        spread_to = 0.5 * (1.0 + lax.erf(act * math.sqrt(0.5)))
        curve = act * spread_to
        density = jnp.exp(act * act * -0.5) * (1.0 / math.sqrt(2.0 * math.pi))
        slope[p] = (gate * (spread_to + act * density)).astype(BF16)
        gelu[p] = curve.astype(BF16)
        unit = (curve * gate).astype(BF16)
        hidden[p] = unit
        total = total + nn(unit, held_down[pl.ds(p * ff, ff), :])
    for o in range(SLOTS):
        for a in range(2):
            at = (a * SLOTS + o) * LANES
            outs[o][:, a * LANES : (a + 1) * LANES] = total[:, at : at + LANES].astype(BF16)


def feed(normed, mixed, up, down):
    tokens, ff = normed.shape[0], down[0].shape[1]
    units = pl.BlockSpec((GROUPS, TILE, ff), lambda i: (0, i, 0))
    return call(
        feed_kernel,
        (tokens // TILE,),
        [rows_of(WIDTH), rows_of(WIDTH)]
        + [resident((SLOTS, 2 * ff, LANES))] * 8
        + [resident((SLOTS, ff, LANES))] * 8,
        [rows_of(256)] * 4 + [units] * 3,
        [struct((tokens, 256), BF16)] * 4 + [struct((GROUPS, tokens, ff), BF16)] * 3,
        [pltpu.VMEM((2 * GROUPS * ff, WIDTH), BF16), pltpu.VMEM((GROUPS * ff, WIDTH), BF16)],
        2 * tokens * WIDTH * 3 * GROUPS * ff,
        8 * tokens * WIDTH + 6 * GROUPS * ff * (tokens + WIDTH),
        "feed",
    )(normed, mixed, *up, *down)


def feed_back_kernel(*refs):
    cots, (slope, gelu, mixed, gain) = refs[:4], refs[4:8]
    up, down, outward = refs[8:16], refs[16:24], refs[24:32]
    g_act, g_gate, g_mixed, g_branch, g_attended, gain_part = refs[32:38]
    held_up, held_down, held_out = refs[38:]
    ff = g_act.shape[2]

    @pl.when(pl.program_id(0) == 0)
    def _():
        place(up, held_up, 0, ff, 0)
        place(up, held_up, ff, ff, GROUPS * ff)
        place(down, held_down, 0, ff, 0)
        place(outward, held_out, 0, GROUP, 0)

    cot = whole_rows(cots)
    gradient = jnp.zeros((TILE, WIDTH), F32)
    for p in range(GROUPS):
        g_hidden = nt(cot, held_down[pl.ds(p * ff, ff), :])
        to_act = (g_hidden * slope[p].astype(F32)).astype(BF16)
        to_gate = (g_hidden * gelu[p].astype(F32)).astype(BF16)
        g_act[p] = to_act
        g_gate[p] = to_gate
        gradient = gradient + nn(to_act, held_up[pl.ds(p * ff, ff), :])
        gradient = gradient + nn(to_gate, held_up[pl.ds((GROUPS + p) * ff, ff), :])
    unit, inverse = norm(mixed[...])
    add_gain(gain_part, gradient * unit)
    total = cot.astype(F32) + norm_back(gradient, unit, inverse, gain[...])
    g_mixed[...] = total
    branch = total.astype(BF16)
    g_branch[...] = branch
    g_attended[...] = nt(branch, held_out[...]).astype(BF16)


def feed_back(cots, slope, gelu, mixed, gain, up, down, outward):
    tokens, ff = mixed.shape[0], down[0].shape[1]
    units = pl.BlockSpec((GROUPS, TILE, ff), lambda i: (0, i, 0))
    return call(
        feed_back_kernel,
        (tokens // TILE,),
        [rows_of(256)] * 4
        + [units, units, rows_of(WIDTH), resident((1, WIDTH))]
        + [resident((SLOTS, 2 * ff, LANES))] * 8
        + [resident((SLOTS, ff, LANES))] * 8
        + [resident((SLOTS, GROUP, LANES))] * 8,
        [units, units] + [rows_of(WIDTH)] * 3 + [resident((8, WIDTH))],
        [struct((GROUPS, tokens, ff), BF16)] * 2
        + [
            struct((tokens, WIDTH), F32),
            struct((tokens, WIDTH), BF16),
            struct((tokens, WIDTH), BF16),
            struct((8, WIDTH), F32),
        ],
        [
            pltpu.VMEM((2 * GROUPS * ff, WIDTH), BF16),
            pltpu.VMEM((GROUPS * ff, WIDTH), BF16),
            pltpu.VMEM((WIDTH, WIDTH), BF16),
        ],
        2 * tokens * WIDTH * (3 * GROUPS * ff + WIDTH),
        14 * tokens * WIDTH + 8 * GROUPS * ff * (tokens + WIDTH),
        "feed_back",
    )(*cots, slope, gelu, mixed, gain, *up, *down, *outward)


def unproject_kernel(*refs):
    xs, (gq, gk, gv, g_mixed, gain), pieces = refs[:4], refs[4:9], refs[9:17]
    outs, gain_part, held = refs[17:21], refs[21], refs[22]

    @pl.when(pl.program_id(0) == 0)
    def _():
        for t in range(3):
            place(pieces, held, t * GROUP, GROUP, t * WIDTH)

    gradient = nn(gq[...], held[pl.ds(0, WIDTH), :])
    gradient = gradient + nn(gk[...], held[pl.ds(WIDTH, WIDTH), :])
    gradient = gradient + nn(gv[...], held[pl.ds(2 * WIDTH, WIDTH), :])
    unit, inverse = norm(whole_rows(xs).astype(F32))
    add_gain(gain_part, gradient * unit)
    total = g_mixed[...] + norm_back(gradient, unit, inverse, gain[...])
    for o in range(SLOTS):
        for a in range(2):
            at = (a * SLOTS + o) * LANES
            outs[o][:, a * LANES : (a + 1) * LANES] = total[:, at : at + LANES].astype(BF16)


def unproject(xs, gq, gk, gv, g_mixed, gain, pieces):
    tokens = gq.shape[0]
    return call(
        unproject_kernel,
        (tokens // TILE,),
        [rows_of(256)] * 4
        + [rows_of(WIDTH)] * 4
        + [resident((1, WIDTH))]
        + [resident((SLOTS, 3 * GROUP, LANES))] * 8,
        [rows_of(256)] * 4 + [resident((8, WIDTH))],
        [struct((tokens, 256), BF16)] * 4 + [struct((8, WIDTH), F32)],
        [pltpu.VMEM((3 * WIDTH, WIDTH), BF16)],
        2 * tokens * WIDTH * 3 * WIDTH,
        14 * tokens * WIDTH + 6 * WIDTH * WIDTH,
        "unproject",
    )(*xs, gq, gk, gv, g_mixed, gain, *pieces)


def outer_halves_kernel(count, slots, more, *refs):
    inner, outer = refs[: 2 * count], refs[2 * count : 2 * count + slots]
    rest = refs[2 * count + slots :]
    added, outs = (rest[:2], rest[2:]) if more else ((None, None), rest)
    if slots > 1:
        right = jnp.concatenate([ref[...] for ref in outer], axis=1)
    else:
        right = outer[0][...]
    for b in range(2):
        for t in range(count):
            left = inner[2 * t + b]
            left = left[0] if len(left.shape) == 3 else left[...]
            made = tn(left, right)
            rows = slice(t * made.shape[0], (t + 1) * made.shape[0])
            for o in range(SLOTS):
                part = made[:, o * LANES : (o + 1) * LANES]
                if more:
                    part = part + added[b][0, o, rows, :].astype(F32)
                outs[b][0, o, rows, :] = part.astype(BF16)


def outer_groups_kernel(count, more, *refs):
    inner, outer, rest = refs[:count], refs[count], refs[count + 1 :]
    added, outs = (rest[:2], rest[2:]) if more else ((None, None), rest)
    right = outer[...]
    for t in range(count):
        left = inner[t]
        left = left[0] if len(left.shape) == 3 else left[...]
        made = tn(left, right)
        rows = slice(t * made.shape[0], (t + 1) * made.shape[0])
        for a in range(2):
            for o in range(SLOTS):
                at = (a * SLOTS + o) * LANES
                part = made[:, at : at + LANES]
                if more:
                    part = part + added[a][0, o, rows, :].astype(F32)
                outs[a][0, o, rows, :] = part.astype(BF16)


def inner_block(value, group):
    if value.ndim == 3:
        return pl.BlockSpec((1,) + value.shape[1:], lambda i: (group(i), 0, 0))
    return pl.BlockSpec((value.shape[0], GROUP), lambda i: (0, group(i)))


def outer_product(kind, inner, outer, d, added=None):
    tokens = outer[0].shape[0]
    width = inner[0].shape[2] if inner[0].ndim == 3 else GROUP
    rows = len(inner) * width
    block = pl.BlockSpec((1, SLOTS, rows, LANES), lambda i: (i, 0, 0, 0))
    if kind == "halves":
        kernel = functools.partial(
            outer_halves_kernel, len(inner), len(outer), added is not None
        )
        operands = [value for value in inner for _ in range(2)]
        specs = [inner_block(v, lambda i, b=b: 2 * b + d) for v in inner for b in range(2)]
        step = LANES if len(outer) > 1 else SLOTS * LANES
        specs += [pl.BlockSpec((tokens, step), lambda i: (0, i)) for _ in outer]
    else:
        kernel = functools.partial(outer_groups_kernel, len(inner), added is not None)
        operands = list(inner)
        specs = [inner_block(v, lambda i: 2 * i + d) for v in inner]
        specs += [resident((tokens, WIDTH))]
    operands += list(outer)
    if added is not None:
        operands += list(added)
        specs += [block] * 2
    return call(
        kernel,
        (2,),
        specs,
        [block] * 2,
        [struct((2, SLOTS, rows, LANES), BF16)] * 2,
        [],
        2 * tokens * 2 * rows * WIDTH,
        4 * rows * (tokens + WIDTH) + 2 * tokens * WIDTH,
        "outer_product",
    )(*operands)


ROTATE = 4


def over_dp(value):
    return lax.ppermute(value, "dp", [(0, 1), (1, 0)])


def over_chip(value):
    return lax.ppermute(value, "col", [(i, i ^ 2) for i in range(4)])


def over_core(value):
    return lax.ppermute(value, "col", [(i, i ^ 1) for i in range(4)])


def from_row(value, o):
    return lax.ppermute(value, "row", [((i + o) % ROTATE, i) for i in range(ROTATE)])


def to_row(value, o):
    return lax.ppermute(value, "row", [(i, (i + o) % ROTATE) for i in range(ROTATE)])


def gather_pieces(shard, chips_last):
    half = lax.dynamic_slice_in_dim(shard, lax.axis_index("dp") * LANES, LANES, 1)
    own = jnp.stack([half] + [from_row(half, o) for o in range(1, SLOTS)])
    if chips_last:
        other = over_dp(own)
        held = {(0, 0): own, (1, 0): other, (0, 1): over_chip(own), (1, 1): over_chip(other)}
    else:
        other = over_chip(own)
        held = {(0, 0): own, (0, 1): other, (1, 0): over_dp(own), (1, 1): over_dp(other)}
    pieces = {}
    for (a, b), value in held.items():
        pieces[a, b, 0] = value
        pieces[a, b, 1] = over_core(value)
    return [pieces[a, b, d] for a in range(2) for b in range(2) for d in range(2)]


def plus(left, right):
    return (left.astype(F32) + right.astype(F32)).astype(BF16)


def reduce_pieces(kind, parts):
    near, far = parts
    cross, turn = (over_chip, over_dp) if kind == "halves" else (over_dp, over_chip)
    came = cross(far)
    came_too = turn(plus(near[1], came[1]))
    total = plus(plus(near[0], came[0]), came_too)
    half = total[0].astype(F32)
    for o in range(1, SLOTS):
        half = half + to_row(total[o], o).astype(F32)
    half = half.astype(BF16)
    other = over_dp(half)
    first = lax.axis_index("dp") == 0
    return jnp.where(
        first,
        jnp.concatenate([half, other], axis=1),
        jnp.concatenate([other, half], axis=1),
    ).astype(F32)


def own_half_first(value):
    return jnp.where(lax.axis_index("dp") == 0, value, jnp.roll(value, LANES, axis=-1))


def slots_of(value):
    me = lax.axis_index("row")
    blocks = value.reshape(ROTATE, -1, 256)
    outs = [lax.dynamic_index_in_dim(blocks, me, 0, False)]
    for o in range(1, ROTATE):
        mine = lax.dynamic_index_in_dim(blocks, (me + ROTATE - o) % ROTATE, 0, False)
        outs.append(from_row(own_half_first(mine), o))
    outs[0] = own_half_first(outs[0])
    return outs


def from_slots(slots, dtype):
    me = lax.axis_index("row")
    tokens = slots[0].shape[0]
    whole = jnp.zeros((ROTATE * tokens, 256), dtype)
    for o in range(ROTATE):
        came = slots[0] if o == 0 else to_row(slots[o], o)
        at = ((me + ROTATE - o) % ROTATE) * tokens
        whole = lax.dynamic_update_slice(whole, own_half_first(came).astype(dtype), (at, 0))
    return whole


def sum_gains(parts):
    total = parts.reshape(2, 2, SLOTS, LANES)
    both = total + over_dp(total)[:, ::-1]
    both = both + over_chip(both)
    both = both + over_core(both)
    mine = both[:, :, 0]
    for o in range(1, SLOTS):
        mine = mine + to_row(both[:, :, o], o)
    return own_half_first(mine.reshape(2, 2 * LANES))


def pieces_of(whole):
    rows = whole.shape[0] // GROUPS
    cut = whole.reshape(GROUPS, rows, SLOTS, 2, LANES).transpose(3, 0, 2, 1, 4)
    return [cut[a, p] for a in range(2) for p in range(GROUPS)]


def whole_of(kind, near_far_by_d, types):
    cut = jnp.stack([jnp.stack(pair) for pair in near_far_by_d])
    cut = cut.transpose((1, 0, 4, 3, 2, 5) if kind == "halves" else (2, 0, 4, 3, 1, 5))
    b, d, rows, o, a, lanes = cut.shape
    cut = cut.reshape(b * d, types, rows // types, WIDTH)
    return [cut[:, t].reshape(-1, WIDTH) for t in range(types)]


def split_heads(rows):
    return rows.reshape(-1, 4, 2, 32, rows.shape[1]).swapaxes(1, 2).reshape(rows.shape)


def join_heads(rows):
    return rows.reshape(-1, 2, 4, 32, rows.shape[1]).swapaxes(1, 2).reshape(rows.shape)


def positions_and_masks(segment_ids, valid_mask, tokens, rows, cols):
    length = segment_ids.shape[1]
    both = lax.all_gather(jnp.stack([segment_ids, valid_mask]), "row", axis=1, tiled=True)
    at = (lax.axis_index("col") * rows + lax.axis_index("row")) * tokens
    sequence, first = at // length, at % length
    segments, valid = lax.dynamic_index_in_dim(both, sequence, 1, False)
    own = lax.dynamic_slice_in_dim(segments, first, tokens, 0)
    ids = jnp.arange(64, dtype=jnp.int32)
    before = jnp.sum((segments[None, :] < ids[:, None]).astype(jnp.int32), axis=1)
    begin = jnp.sum(jnp.where(own[:, None] == ids[None, :], before[None, :], 0), axis=1)
    where_in = (first + jnp.arange(tokens, dtype=jnp.int32) - begin).astype(F32)
    frequency = ROPE_THETA ** (-(jnp.arange(32, dtype=F32) * 2.0) / HEAD)
    angles = where_in[:, None] * frequency[None, :]
    cosine, sine = jnp.tile(jnp.cos(angles), (1, 4)), jnp.tile(jnp.sin(angles), (1, 4))
    code = jnp.pad(jnp.where(valid == 1, segments, -1), (REACH, REACH), constant_values=-1)
    code = lax.dynamic_slice_in_dim(code, first, tokens + 2 * REACH, 0)
    span = QUERY + 2 * REACH
    keys = jnp.stack([code[i : i + span] for i in range(0, tokens, QUERY)])[:, None, :]
    return cosine, sine, own[:, None], keys


def body(
    dp,
    rows,
    cols,
    tokens_in,
    w_query,
    w_key,
    w_value,
    w_out,
    w_act,
    w_gate,
    w_down,
    gain_attn,
    gain_ffn,
    cotangent,
    segment_ids,
    valid_mask,
):
    own_slice = (dp, rows, cols) == (2, 4, 4)
    tokens = tokens_in.shape[0] // rows
    length = segment_ids.shape[1]
    gains = jnp.stack([gain_attn, gain_ffn])
    if own_slice:
        xs = slots_of(tokens_in)
        cots = slots_of(cotangent)
        gain_slots = own_half_first(gains)
        gain_slots = jnp.stack([gain_slots] + [from_row(gain_slots, o) for o in range(1, SLOTS)])
        gather = gather_pieces
        project_rows = jnp.concatenate(
            [split_heads(w_query.T), split_heads(w_key.T), w_value.T], axis=0
        )
        project_w = gather(project_rows, True)
        out_w = gather(w_out, False)
        up_w = gather(jnp.concatenate([w_act.T, w_gate.T], axis=0), False)
        down_w = gather(w_down, True)
    else:

        def exchange(value):
            return lax.all_to_all(value.reshape(rows, tokens, 256), "row", 0, 0)

        def full(value, inner_first):
            first, second = ("col", "row") if inner_first else ("row", "col")
            value = lax.all_gather(value, first, axis=0, tiled=True)
            value = lax.all_gather(value, second, axis=1, tiled=True)
            return value if inner_first else value.T

        xs = list(exchange(tokens_in))
        cots = list(exchange(cotangent))
        gain_slots = lax.all_gather(gains, "row", axis=0)

        def joined(*parts):
            lists = [pieces_of(part) for part in parts]
            return [jnp.concatenate(same, axis=1) for same in zip(*lists)]

        project_w = joined(
            split_heads(full(w_query, False)),
            split_heads(full(w_key, False)),
            full(w_value, False),
        )
        out_w = joined(full(w_out, True))
        up_w = joined(full(w_act, False), full(w_gate, False))
        down_w = joined(full(w_down, True))
    gain_rows = (
        gain_slots.reshape(SLOTS, 2, 2, LANES).transpose(1, 2, 0, 3).reshape(2, 1, WIDTH)
    ).astype(F32)

    cosine, sine, seg_query, seg_key = positions_and_masks(
        segment_ids, valid_mask, tokens, rows, cols
    )
    q, k, v, normed_attn = project(xs, gain_rows[0], cosine, sine, project_w)

    count = rows * cols
    joins = [i for i in range(count - 1) if ((i + 1) * tokens) % length]
    upward, downward = [(i, i + 1) for i in joins], [(i + 1, i) for i in joins]

    def shift(value, perm):
        place_of = [(i % rows) * cols + i // rows for i in range(count)]
        return lax.ppermute(value, ("row", "col"), [(place_of[i], place_of[j]) for i, j in perm])

    low = shift(jnp.concatenate([k[-REACH:], v[-REACH:]], axis=1), upward)
    high = shift(jnp.concatenate([k[:REACH], v[:REACH]], axis=1), downward)
    attended, weights = attend(q, k, v, low, high, seg_query, seg_key)
    mixed, normed_ffn = mix(xs, attended, gain_rows[1], out_w)
    *out_slots, hidden, slope, gelu = feed(normed_ffn, mixed, up_w, down_w)

    def outer_sum(kind, inner, outer):
        far = outer_product(kind, inner, outer, 1)
        if own_slice:
            came = [over_core(value) for value in far]
            return outer_product(kind, inner, outer, 0, came)
        return [outer_product(kind, inner, outer, 0), far]

    down_parts = outer_sum("halves", [hidden], cots)
    g_act, g_gate, g_mixed, g_branch, g_attended, gain_part_ffn = feed_back(
        cots, slope, gelu, mixed, gain_rows[1], up_w, down_w, out_w
    )
    up_parts = outer_sum("groups", [g_act, g_gate], [normed_ffn])
    out_parts = outer_sum("groups", [attended], [g_branch])
    gq, gk, gv, edge_k, edge_v = attend_back(
        q, g_attended, weights, k, v, low, high, cosine, sine
    )
    to_low = jnp.concatenate([edge_k[:REACH], edge_v[:REACH]], axis=1).astype(BF16)
    to_high = jnp.concatenate([edge_k[-REACH:], edge_v[-REACH:]], axis=1).astype(BF16)
    from_high = shift(to_low, downward).astype(F32)
    from_low = shift(to_high, upward).astype(F32)

    def turned(value, c, s):
        cut = value.reshape(-1, GROUPS, 2, LANES)
        first, second = cut[:, :, 0], cut[:, :, 1]
        c, s = c[:, None], s[:, None]
        back = jnp.stack([first * c + second * s, second * c - first * s], axis=2)
        return back.reshape(value.shape).astype(BF16)

    near_k = edge_k[REACH : 2 * REACH] + from_low[:, :WIDTH]
    near_v = edge_v[REACH : 2 * REACH] + from_low[:, WIDTH:]
    last_k = edge_k[2 * REACH : 3 * REACH] + from_high[:, :WIDTH]
    last_v = edge_v[2 * REACH : 3 * REACH] + from_high[:, WIDTH:]
    gk = gk.at[:REACH].set(turned(near_k, cosine[:REACH], sine[:REACH]))
    gk = gk.at[-REACH:].set(turned(last_k, cosine[-REACH:], sine[-REACH:]))
    gv = gv.at[:REACH].set(near_v.astype(BF16))
    gv = gv.at[-REACH:].set(last_v.astype(BF16))

    *grad_slots, gain_part_attn = unproject(xs, gq, gk, gv, g_mixed, gain_rows[0], project_w)
    project_parts = outer_sum("halves", [gq, gk, gv], [normed_attn])

    gain_parts = jnp.stack([jnp.sum(gain_part_attn, axis=0), jnp.sum(gain_part_ffn, axis=0)])
    if own_slice:
        layer_out = from_slots(out_slots, BF16)
        token_gradient = from_slots(grad_slots, F32)
        down_sum = reduce_pieces("halves", down_parts)
        up_sum = reduce_pieces("groups", up_parts)
        out_sum = reduce_pieces("groups", out_parts)
        project_sum = reduce_pieces("halves", project_parts)
        ff = w_act.shape[1]
        grads = (
            join_heads(project_sum[:GROUP]).T,
            join_heads(project_sum[GROUP : 2 * GROUP]).T,
            project_sum[2 * GROUP :].T,
            out_sum,
            up_sum[:ff].T,
            up_sum[ff:].T,
            down_sum,
        )
        gain_grads = sum_gains(gain_parts)
    else:

        def back(slots):
            return lax.all_to_all(jnp.stack(slots), "row", 0, 0).reshape(-1, 256)

        def share(value, inner_first):
            first, second = ("col", "row") if inner_first else ("row", "col")
            value = value if inner_first else value.T
            value = lax.psum_scatter(value, first, scatter_dimension=0, tiled=True)
            value = lax.psum_scatter(value, second, scatter_dimension=1, tiled=True)
            return lax.psum(value, "dp").astype(F32)

        layer_out = back(out_slots)
        token_gradient = back(grad_slots).astype(F32)
        (down_whole,) = whole_of("halves", down_parts, 1)
        act_whole, gate_whole = whole_of("groups", up_parts, 2)
        (out_whole,) = whole_of("groups", out_parts, 1)
        query_whole, key_whole, value_whole = whole_of("halves", project_parts, 3)
        grads = (
            share(join_heads(query_whole), False),
            share(join_heads(key_whole), False),
            share(value_whole, False),
            share(out_whole, True),
            share(act_whole, False),
            share(gate_whole, False),
            share(down_whole, True),
        )
        totals = lax.psum(gain_parts, ("dp", "row", "col"))
        totals = totals.reshape(2, 2, SLOTS, LANES).swapaxes(1, 2).reshape(2, SLOTS, 256)
        gain_grads = lax.dynamic_index_in_dim(totals, lax.axis_index("row"), 1, False)
    return (layer_out, token_gradient) + grads + (gain_grads[0], gain_grads[1])


def solution(mesh):
    sizes = tuple(mesh.shape[axis] for axis in ("dp", "row", "col"))
    in_specs = (
        P(("dp", "col"), "row"),
        P("row", "col"),
        P("row", "col"),
        P("row", "col"),
        P("col", "row"),
        P("row", "col"),
        P("row", "col"),
        P("col", "row"),
        P("row"),
        P("row"),
        P(("dp", "col"), "row"),
        P(("dp", "row"), None),
        P(("dp", "row"), None),
    )
    out_specs = (
        P(("dp", "col"), "row"),
        P(("dp", "col"), "row"),
        P("row", "col"),
        P("row", "col"),
        P("row", "col"),
        P("col", "row"),
        P("row", "col"),
        P("row", "col"),
        P("col", "row"),
        P("row"),
        P("row"),
    )
    return jax.shard_map(
        functools.partial(body, *sizes),
        mesh=mesh,
        in_specs=in_specs,
        out_specs=out_specs,
        check_vma=False,
    )
```

time: 6390 us -> 772 us (0.12)
  waiting for transfers between devices: 5430 us -> 299 us
  matrix products: 428 us -> 0 us
  Pallas kernels: 0 us -> 216 us
  local copies, waits for them, and re-layouts: 193 us -> 47 us
  starting transfers between devices: 1.49 us -> 143 us
  other arithmetic: 178 us -> 40.9 us
  blocking collectives: 90.2 us -> 14.2 us
    reduce_scatter x8 -> x0, waiting for transfers between devices: 3630 us -> none  [the longest x4 3170 us: sum_rows(): lax.psum_scatter(partial_value(jnp.int32(0), row_share * lax.axis_size('r...]
    all_gather x8 -> x0, waiting for transfers between devices: 1770 us -> none  [the longest x4 1580 us: gather_rows(): return lax.all_gather(values, 'row', axis=0, tiled=True)]
    dot_general x68 -> x0, matrix products: 428 us -> none  [the longest x8 161 us: partial_value(): lax.dot_general(whole, weights, (((1,), (contract,)), ((), ())), preferre...]
    ppermute x0 -> x97, waiting for transfers between devices: none -> 299 us  [the longest x15 84.6 us: over_dp(): return lax.ppermute(value, 'dp', [(0, 1), (1, 0)])]
    pallas_call x0 -> x15, Pallas kernels: none -> 216 us  [the longest x8 56.9 us: outer_product(): call(kernel, (2,), specs, [block] * 2, [struct((2, SLOTS, rows, LANES), B...]
    ppermute x0 -> x97, starting transfers between devices: none -> 143 us  [the longest x21 52.6 us: from_row(): lax.ppermute(value, 'row', [((i + o) % ROTATE, i) for i in range(ROTATE)])]
    dynamic_update_slice x16 -> x0, local copies, waits for them, and re-layouts: 96.5 us -> none  [attend_back(): lax.scan(back_block, (empty, empty), jnp.arange(seqs_dev * blocks, dtype=...]
    psum x5 -> x0, blocking collectives: 90.2 us -> none  [the longest x4 77.8 us: feature_moments(): lax.psum((jnp.sum(first_term, axis=1), jnp.sum(second_term, axis=1)), 'row')]
  transfers between devices with their start and end apart: 17 -> 97, of which waited for: 17 -> 33; matrix products, arithmetic and copies ran while one was open for 3% -> 10% of each run, Pallas kernels for 0% -> 19%
where the time goes in v1:
time: 772 us; the launch traced here: 762 us
  waiting for transfers between devices  299 us (39%)
  Pallas kernels  216 us (28%)
  starting transfers between devices  143 us (19%)
  local copies, waits for them, and re-layouts  47 us (6%)
  other arithmetic  40.9 us (5%)
  blocking collectives  14.2 us (2%)
    ppermute x15, waiting for transfers between devices, over_dp(): return lax.ppermute(value, 'dp', [(0, 1), (1, 0)])  84.6 us
    ppermute x21, waiting for transfers between devices, to_row(): lax.ppermute(value, 'row', [(i, (i + o) % ROTATE) for i in range(ROTATE)])  80.8 us
    ppermute x11, waiting for transfers between devices, over_chip(): return lax.ppermute(value, 'col', [(i, i ^ 2) for i in range(4)])  66 us
    ppermute x21, waiting for transfers between devices, from_row(): lax.ppermute(value, 'row', [((i + o) % ROTATE, i) for i in range(ROTATE)])  60.4 us
    pallas_call x8, Pallas kernels, outer_product(): call(kernel, (2,), specs, [block] * 2, [struct((2, SLOTS, rows, LANES), B...  56.9 us
    ppermute x21, starting transfers between devices, from_row(): lax.ppermute(value, 'row', [((i + o) % ROTATE, i) for i in range(ROTATE)])  52.6 us
    pallas_call x1, Pallas kernels, feed_back(): call(feed_back_kernel, (tokens // TILE,), [rows_of(256)] * 4 + [units, un...  43.1 us
    ppermute x21, starting transfers between devices, to_row(): lax.ppermute(value, 'row', [(i, (i + o) % ROTATE) for i in range(ROTATE)])  36.5 us
  transfers between devices with their start and end apart: 97, of which 33 were waited for; matrix products, arithmetic and copies ran while one was open for 10% of the time, Pallas kernels for 19%

profile of v1, /device:TPU:0, one launch (start us, length us, event | category | flops | bytes accessed | tf_op | source)
XLA Modules:
  0.0 762.1 jit_solution(11340703570890548087)
XLA Ops:
  14.3 14.2 %all_gather.3 = s32[2,4,4096]{2,0,1:T(2,128)} all-gather(s32[2,1,4096]{2,0,1:T(2,128)S(1)} %pad_add_fusion), channel_id=1, replica_groups=mesh['dp'=2,'row'=4,'col'=4] {'row'}, dimensions={1}, use_global_device_ids=true | all-gather | bytes 163840 | tf_op jit(solution)/shard_map/all_gather | solution.py:710
  70.7 15.6 %collective-permute-start.8 = (bf16[768,128]{1,0:T(8,128)(2,1)S(1)}, bf16[768,128]{1,0:T(8,128)(2,1)S(1)}, u32[]{:S(2)}, u32[]{:S(2)}) collective-permute-start(bf16[768,128]{1,0:T(8,128)(2,1)S(1)} %fusion.32), channel_id=1, source_target_pairs={{12,0},{0,4},{4,8},{8,12},{13,1},{1,5},{5,9},{9,13},{14,2},{2,6},{... | collective-permute-start | bytes 589832 | tf_op jit(solution)/shard_map/ppermute | solution.py:603
  103.2 31.3 %collective-permute-done.29 = bf16[1312,128]{1,0:T(8,128)(2,1)S(1)} collective-permute-done((bf16[1312,128]{1,0:T(8,128)(2,1)S(1)}, bf16[1312,128]{1,0:T(8,128)(2,1)S(1)}, u32[]{:S(2)}, u32[]{:S(2)}) %collective-permute-start.29) | collective-permute-done | bytes 335904 | tf_op jit(solution)/shard_map/ppermute | solution.py:603
  137.0 9.9 %collective-permute-done.30 = bf16[1312,128]{1,0:T(8,128)(2,1)S(1)} collective-permute-done((bf16[1312,128]{1,0:T(8,128)(2,1)S(1)}, bf16[1312,128]{1,0:T(8,128)(2,1)S(1)}, u32[]{:S(2)}, u32[]{:S(2)}) %collective-permute-start.30) | collective-permute-done | bytes 335904 | tf_op jit(solution)/shard_map/ppermute | solution.py:603
  155.8 13.3 %collective-permute-done.26.refs_12_.refs_30_ = bf16[4,256,128]{2,1,0:T(8,128)(2,1)S(1)} collective-permute-done((bf16[4,256,128]{2,1,0:T(8,128)(2,1)S(1)}, bf16[4,256,128]{2,1,0:T(8,128)(2,1)S(1)}, u32[]{:S(2)}, u32[]{:S(2)}) %collective-permute-start.26) | collective-permute-done | bytes 262176 | tf_op jit(solution)/shard_map/ppermute | solution.py:591
  176.7 39.3 %collective-permute-done.14.refs_13_.refs_15_ = bf16[4,768,128]{2,1,0:T(8,128)(2,1)} collective-permute-done((bf16[4,768,128]{2,1,0:T(8,128)(2,1)}, bf16[4,768,128]{2,1,0:T(8,128)(2,1)}, u32[]{:S(2)}, u32[]{:S(2)}) %collective-permute-start.14) | collective-permute-done | bytes 786464 | tf_op jit(solution)/shard_map/ppermute | solution.py:595
  219.8 14.4 %project.1 = (bf16[1024,1024]{1,0:T(8,128)(2,1)}, bf16[1024,1024]{1,0:T(8,128)(2,1)}, bf16[1024,1024]{1,0:T(8,128)(2,1)}, bf16[1024,1024]{1,0:T(8,128)(2,1)}) custom-call(bf16[1024,256]{1,0:T(8,128)(2,1)} %maximum_select_fusion.1.refs_0_, bf16[1024,256]{1,0:T(8,128)(2,1)} %copy-done.49, bf16[1024,256]{1,0:T(8,128)(2,1)} %copy-done.48, ...), custom_call_target="tpu_custom_call" | custom-call | flops 6442450944 | bytes 16777216 | tf_op jit(solution)/shard_map/project/pallas_call | solution.py:136
  238.9 13.2 %collective-permute-done.46.refs_16_.refs_22_ = bf16[4,656,128]{2,1,0:T(8,128)(2,1)S(1)} collective-permute-done((bf16[4,656,128]{2,1,0:T(8,128)(2,1)}, bf16[4,656,128]{2,1,0:T(8,128)(2,1)S(1)}, u32[]{:S(2)}, u32[]{:S(2)}) %collective-permute-start.46) | collective-permute-done | bytes 671776 | tf_op jit(solution)/shard_map/ppermute | solution.py:595
  253.9 24.0 %collective-permute-done.36.refs_8_.refs_14_ = bf16[4,1312,128]{2,1,0:T(8,128)(2,1)} collective-permute-done((bf16[4,1312,128]{2,1,0:T(8,128)(2,1)}, bf16[4,1312,128]{2,1,0:T(8,128)(2,1)}, u32[]{:S(2)}, u32[]{:S(2)}) %collective-permute-start.36) | collective-permute-done | bytes 1343520 | tf_op jit(solution)/shard_map/ppermute | solution.py:591
  279.2 18.5 %collective-permute-start.16 = (bf16[64,2048]{1,0:T(8,128)(2,1)S(1)}, bf16[64,2048]{1,0:T(8,128)(2,1)S(1)}, u32[]{:S(2)}, u32[]{:S(2)}) collective-permute-start(bf16[64,2048]{1,0:T(8,128)(2,1)S(1)} %pad_maximum_fusion.3), channel_id=1, source_target_pairs={{0,4},{4,8},{8,12},{1,5},{5,9},{9,13},{2,6},{6,10},{10,14},{3,7},{... | collective-permute-start | bytes 786440 | tf_op jit(solution)/shard_map/ppermute | solution.py:806
  306.7 16.4 %attend.1 = (bf16[1024,1024]{1,0:T(8,128)(2,1)}, bf16[8,4,512,256]{3,2,1,0:T(8,128)(2,1)}) custom-call(bf16[1024,1024]{1,0:T(8,128)(2,1)} %get-tuple-element.106.q.refs_0_, bf16[1024,1024]{1,0:T(8,128)(2,1)} %get-tuple-element.107.k.refs_3_, bf16[1024,1024]{1,0:T(8,128)(2,1)} %get-tuple-element.108.v.refs_4_, bf16[64,2048]{1,0:T(8,128)(2,1)} %copy-done.62, ...), custom_call_target="tpu_custom_call" | custom-call | flops 4294967296 | bytes 16777216 | tf_op jit(solution)/shard_map/attend/pallas_call | solution.py:215
  338.1 34.3 %feed.1 = (bf16[1024,256]{1,0:T(8,128)(2,1)}, bf16[1024,256]{1,0:T(8,128)(2,1)}, bf16[1024,256]{1,0:T(8,128)(2,1)}, bf16[1024,256]{1,0:T(8,128)(2,1)}, bf16[4,10...) custom-call(bf16[1024,1024]{1,0:T(8,128)(2,1)} %get-tuple-element.110.refs_0_.refs_2_, ...), custom_call_target="tpu_custom_call" | custom-call | flops 16508780544 | bytes 40632320 | tf_op jit(solution)/shard_map/feed/pallas_call | solution.py:390
  372.3 9.8 %collective-permute-done.52.refs_2_.refs_4_ = bf16[1024,256]{1,0:T(8,128)(2,1)S(1)} collective-permute-done((bf16[1024,256]{1,0:T(8,128)(2,1)S(1)}, bf16[1024,256]{1,0:T(8,128)(2,1)S(1)}, u32[]{:S(2)}, u32[]{:S(2)}) %collective-permute-start.52) | collective-permute-done | bytes 524320 | tf_op jit(solution)/shard_map/ppermute | solution.py:603
  383.1 43.1 %feed_back.1 = (bf16[4,1024,656]{2,1,0:T(8,128)(2,1)}, bf16[4,1024,656]{2,1,0:T(8,128)(2,1)}, f32[1024,1024]{1,0:T(8,128)}, bf16[1024,1024]{1,0:T(8,128)(2,1)}, ...) custom-call(bf16[1024,256]{1,0:T(8,128)(2,1)} %maximum_select_fusion.9.refs_0_.refs_2_, bf16[1024,256]{1,0:T(8,128)(2,1)} %copy-done.7, ...), custom_call_target="tpu_custom_call" | custom-call | flops 18656264192 | bytes 57671680 | tf_op jit(solution)/shard_map/feed_back/pallas_call | solution.py:441
  426.3 25.9 %attend_back.1 = (bf16[1024,1024]{1,0:T(8,128)(2,1)}, bf16[1024,1024]{1,0:T(8,128)(2,1)}, bf16[1024,1024]{1,0:T(8,128)(2,1)}, f32[256,1024]{1,0:T(8,128)}, f32[256,1024]{1,0:T(8,128)}) custom-call(bf16[1024,1024]{1,0:T(8,128)(2,1)} %get-tuple-element.106.q.refs_0_, bf16[1024,1024]{1,0:T(8,128)(2,1)} %get-tuple-element.118.refs_1_, ...), custom_call_target="tpu_custom_call" | custom-call | flops 8589934592 | bytes 23068672 | tf_op jit(solution)/shard_map/attend_back/pallas_call | solution.py:300
  457.4 10.1 %outer_product.12 = (bf16[2,4,1312,128]{3,2,1,0:T(8,128)(2,1)}, bf16[2,4,1312,128]{3,2,1,0:T(8,128)(2,1)}) custom-call(bf16[4,1024,656]{2,1,0:T(8,128)(2,1)} %get-tuple-element.140.refs_0_, bf16[4,1024,656]{2,1,0:T(8,128)(2,1)} %get-tuple-element.141.refs_1_, bf16[1024,1024]{1,0:T(8,128)(2,1)} %get-tuple-element.110.refs_0_.refs_2_), custom_call_target="tpu_custom_call" | custom-call | flops 5502926848 | bytes 12845056 | tf_op jit(solution)/shard_map/outer_product/pallas_call | solution.py:574
  482.5 16.3 %unproject.1 = (bf16[1024,256]{1,0:T(8,128)(2,1)}, bf16[1024,256]{1,0:T(8,128)(2,1)}, bf16[1024,256]{1,0:T(8,128)(2,1)}, bf16[1024,256]{1,0:T(8,128)(2,1)}, f32[8,1024]{1,0:T(8,128)}) custom-call(bf16[1024,256]{1,0:T(8,128)(2,1)} %maximum_select_fusion.1.refs_0_, bf16[1024,256]{1,0:T(8,128)(2,1)} %copy-done.49, bf16[1024,256]{1,0:T(8,128)(2,1)} %copy-done.48, ...), custom_call_target="tpu_custom_call" | custom-call | flops 6442450944 | bytes 20971520 | tf_op jit(solution)/shard_map/unproject/pallas_call | solution.py:491
  526.7 14.7 %collective-permute-done.48 = bf16[1024,256]{1,0:T(8,128)(2,1)S(1)} collective-permute-done((bf16[1024,256]{1,0:T(8,128)(2,1)S(1)}, bf16[1024,256]{1,0:T(8,128)(2,1)S(1)}, u32[]{:S(2)}, u32[]{:S(2)}) %collective-permute-start.48) | collective-permute-done | bytes 524320 | tf_op jit(solution)/shard_map/ppermute | solution.py:607
  541.5 21.8 %collective-permute-done.49 = bf16[1024,256]{1,0:T(8,128)(2,1)S(1)} collective-permute-done((bf16[1024,256]{1,0:T(8,128)(2,1)S(1)}, bf16[1024,256]{1,0:T(8,128)(2,1)S(1)}, u32[]{:S(2)}, u32[]{:S(2)}) %collective-permute-start.49) | collective-permute-done | bytes 524320 | tf_op jit(solution)/shard_map/ppermute | solution.py:607
  566.0 9.2 %collective-permute-start.56 = (bf16[1024,256]{1,0:T(8,128)(2,1)}, bf16[1024,256]{1,0:T(8,128)(2,1)S(1)}, u32[]{:S(2)}, u32[]{:S(2)}) collective-permute-start(bf16[1024,256]{1,0:T(8,128)(2,1)} %get-tuple-element.127), channel_id=1, source_target_pairs={{0,4},{4,8},{8,12},{12,0},{1,5},{5,9},{9,13},{13,1},{2,6},{6,10},{... | collective-permute-start | bytes 1572872 | tf_op jit(solution)/shard_map/ppermute | solution.py:607
  600.3 10.9 %outer_product.13 = (bf16[2,4,1312,128]{3,2,1,0:T(8,128)(2,1)}, bf16[2,4,1312,128]{3,2,1,0:T(8,128)(2,1)}) custom-call(bf16[4,1024,656]{2,1,0:T(8,128)(2,1)} %get-tuple-element.140.refs_0_, bf16[4,1024,656]{2,1,0:T(8,128)(2,1)} %get-tuple-element.141.refs_1_, bf16[1024,1024]{1,0:T(8,128)(2,1)} %get-tuple-element.110.refs_0_.refs_2_, ...), custom_call_target="tpu_custom_call" | custom-call | flops 5502926848 | bytes 12845056 | tf_op jit(solution)/shard_map/outer_product/pallas_call | solution.py:574
  651.0 39.7 %collective-permute-done.86 = bf16[4,656,128]{2,1,0:T(8,128)(2,1)S(1)} collective-permute-done((bf16[4,656,128]{2,1,0:T(8,128)(2,1)S(1)}, bf16[4,656,128]{2,1,0:T(8,128)(2,1)S(1)}, u32[]{:S(2)}, u32[]{:S(2)}) %collective-permute-start.86) | collective-permute-done | bytes 671776 | tf_op jit(solution)/shard_map/ppermute | solution.py:591
  728.0 9.1 %collective-permute-done.64 = bf16[768,128]{1,0:T(8,128)(2,1)S(1)} collective-permute-done((bf16[768,128]{1,0:T(8,128)(2,1)S(1)}, bf16[768,128]{1,0:T(8,128)(2,1)S(1)}, u32[]{:S(2)}, u32[]{:S(2)}) %collective-permute-start.64) | collective-permute-done | bytes 196640 | tf_op jit(solution)/shard_map/ppermute | solution.py:607
  737.9 13.6 %collective-permute-done.80 = bf16[1312,128]{1,0:T(8,128)(2,1)S(1)} collective-permute-done((bf16[1312,128]{1,0:T(8,128)(2,1)S(1)}, bf16[1312,128]{1,0:T(8,128)(2,1)S(1)}, u32[]{:S(2)}, u32[]{:S(2)}) %collective-permute-start.80) | collective-permute-done | bytes 335904 | tf_op jit(solution)/shard_map/ppermute | solution.py:607
  (469 shorter events, 291.3 us)
Async XLA Ops:
  2.1 52.9 %collective-permute-start.3 = (bf16[2,256]{1,0:T(2,128)(2,1)S(1)}, bf16[2,256]{1,0:T(2,128)(2,1)S(1)}, u32[]{:S(2)}, u32[]{:S(2)}) collective-permute-start(bf16[2,256]{1,0:T(2,128)(2,1)S(1)} %broadcast_select_fusion.1), channel_id=1, source_target_pairs={{4,0},{8,4},{12,8},{0,12},{5,1},{9,5},{13,9},{1,13},{6,2},{10,6},{... | collective-permute-start | bytes 3080 | tf_op jit(solution)/shard_map/ppermute | solution.py:603
  7.2 47.8 %collective-permute-start.4 = (bf16[2,256]{1,0:T(2,128)(2,1)S(1)}, bf16[2,256]{1,0:T(2,128)(2,1)S(1)}, u32[]{:S(2)}, u32[]{:S(2)}) collective-permute-start(bf16[2,256]{1,0:T(2,128)(2,1)S(1)} %broadcast_select_fusion.1), channel_id=1, source_target_pairs={{8,0},{12,4},{0,8},{4,12},{9,1},{13,5},{1,9},{5,13},{10,2},{14,6},... | collective-permute-start | bytes 3080 | tf_op jit(solution)/shard_map/ppermute | solution.py:603
  7.2 51.7 %collective-permute-start.5 = (bf16[2,256]{1,0:T(2,128)(2,1)S(1)}, bf16[2,256]{1,0:T(2,128)(2,1)S(1)}, u32[]{:S(2)}, u32[]{:S(2)}) collective-permute-start(bf16[2,256]{1,0:T(2,128)(2,1)S(1)} %broadcast_select_fusion.1), channel_id=1, source_target_pairs={{12,0},{0,4},{4,8},{8,12},{13,1},{1,5},{5,9},{9,13},{14,2},{2,6},{... | collective-permute-start | bytes 3080 | tf_op jit(solution)/shard_map/ppermute | solution.py:603
  9.6 49.2 %collective-permute-start.18 = (bf16[256,128]{1,0:T(8,128)(2,1)}, bf16[256,128]{1,0:T(8,128)(2,1)}, u32[]{:S(2)}, u32[]{:S(2)}) collective-permute-start(bf16[256,128]{1,0:T(8,128)(2,1)} %constant_dynamic-slice_fusion.2), channel_id=1, source_target_pairs={{4,0},{8,4},{12,8},{0,12},{5,1},{9,5},{13,9},{1,13},{6,2},{10,6},{... | collective-permute-start | bytes 196616 | tf_op jit(solution)/shard_map/ppermute | solution.py:603
  12.5 47.0 %collective-permute-start.19 = (bf16[256,128]{1,0:T(8,128)(2,1)}, bf16[256,128]{1,0:T(8,128)(2,1)}, u32[]{:S(2)}, u32[]{:S(2)}) collective-permute-start(bf16[256,128]{1,0:T(8,128)(2,1)} %constant_dynamic-slice_fusion.2), channel_id=1, source_target_pairs={{8,0},{12,4},{0,8},{4,12},{9,1},{13,5},{1,9},{5,13},{10,2},{14,6},... | collective-permute-start | bytes 196616 | tf_op jit(solution)/shard_map/ppermute | solution.py:603
  95.8 52.0 %collective-permute-start.2 = (bf16[1024,256]{1,0:T(8,128)(2,1)}, bf16[1024,256]{1,0:T(8,128)(2,1)S(1)}, u32[]{:S(2)}, u32[]{:S(2)}) collective-permute-start(bf16[1024,256]{1,0:T(8,128)(2,1)} %maximum_select_fusion.4), channel_id=1, source_target_pairs={{12,0},{0,4},{4,8},{8,12},{13,1},{1,5},{5,9},{9,13},{14,2},{2,6},{... | collective-permute-start | bytes 1572872 | tf_op jit(solution)/shard_map/ppermute | solution.py:603
  97.8 55.1 %collective-permute-start.1 = (bf16[1024,256]{1,0:T(8,128)(2,1)}, bf16[1024,256]{1,0:T(8,128)(2,1)S(1)}, u32[]{:S(2)}, u32[]{:S(2)}) collective-permute-start(bf16[1024,256]{1,0:T(8,128)(2,1)} %maximum_select_fusion.3), channel_id=1, source_target_pairs={{8,0},{12,4},{0,8},{4,12},{9,1},{13,5},{1,9},{5,13},{10,2},{14,6},... | collective-permute-start | bytes 1572872 | tf_op jit(solution)/shard_map/ppermute | solution.py:603
  100.1 53.7 %collective-permute-start = (bf16[1024,256]{1,0:T(8,128)(2,1)S(1)}, bf16[1024,256]{1,0:T(8,128)(2,1)S(1)}, u32[]{:S(2)}, u32[]{:S(2)}) collective-permute-start(bf16[1024,256]{1,0:T(8,128)(2,1)S(1)} %copy-done.32), channel_id=1, source_target_pairs={{4,0},{8,4},{12,8},{0,12},{5,1},{9,5},{13,9},{1,13},{6,2},{10,6},{... | collective-permute-start | bytes 1572872 | tf_op jit(solution)/shard_map/ppermute | solution.py:603
  101.9 67.7 %collective-permute-start.12 = (bf16[4,768,128]{2,1,0:T(8,128)(2,1)}, bf16[4,768,128]{2,1,0:T(8,128)(2,1)}, u32[]{:S(2)}, u32[]{:S(2)}) collective-permute-start(bf16[4,768,128]{2,1,0:T(8,128)(2,1)} %pad_maximum_fusion.1.refs_7_.refs_9_), channel_id=1, source_target_pairs={{0,16},{16,0},{1,17},{17,1},{2,18},{18,2},{3,19},{19,3},{4,20},{20... | collective-permute-start | bytes 2359304 | tf_op jit(solution)/shard_map/ppermute | solution.py:591
  169.1 47.8 %collective-permute-start.32 = (bf16[4,1312,128]{2,1,0:T(8,128)(2,1)}, bf16[4,1312,128]{2,1,0:T(8,128)(2,1)}, u32[]{:S(2)}, u32[]{:S(2)}) collective-permute-start(bf16[4,1312,128]{2,1,0:T(8,128)(2,1)} %pad_maximum_fusion.refs_2_.refs_8_), channel_id=1, source_target_pairs={{0,2},{1,3},{2,0},{3,1},{4,6},{5,7},{6,4},{7,5},{8,10},{9,11},{10,... | collective-permute-start | bytes 4030472 | tf_op jit(solution)/shard_map/ppermute | solution.py:595
  169.6 46.5 %collective-permute-start.14 = (bf16[4,768,128]{2,1,0:T(8,128)(2,1)}, bf16[4,768,128]{2,1,0:T(8,128)(2,1)}, u32[]{:S(2)}, u32[]{:S(2)}) collective-permute-start(bf16[4,768,128]{2,1,0:T(8,128)(2,1)} %collective-permute-done.12.refs_11_.refs_13_), channel_id=1, source_target_pairs={{0,2},{1,3},{2,0},{3,1},{4,6},{5,7},{6,4},{7,5},{8,10},{9,11},{10,... | collective-permute-start | bytes 2359304 | tf_op jit(solution)/shard_map/ppermute | solution.py:595
  218.0 59.9 %collective-permute-start.36 = (bf16[4,1312,128]{2,1,0:T(8,128)(2,1)}, bf16[4,1312,128]{2,1,0:T(8,128)(2,1)}, u32[]{:S(2)}, u32[]{:S(2)}) collective-permute-start(bf16[4,1312,128]{2,1,0:T(8,128)(2,1)} %collective-permute-done.32.refs_4_.refs_10_), channel_id=1, source_target_pairs={{0,16},{16,0},{1,17},{17,1},{2,18},{18,2},{3,19},{19,3},{4,20},{20... | collective-permute-start | bytes 4030472 | tf_op jit(solution)/shard_map/ppermute | solution.py:591
  252.1 79.3 %collective-permute-start.31 = (bf16[4,1312,128]{2,1,0:T(8,128)(2,1)}, bf16[4,1312,128]{2,1,0:T(8,128)(2,1)}, u32[]{:S(2)}, u32[]{:S(2)}) collective-permute-start(bf16[4,1312,128]{2,1,0:T(8,128)(2,1)} %pad_maximum_fusion.refs_2_.refs_8_), channel_id=1, source_target_pairs={{0,1},{1,0},{2,3},{3,2},{4,5},{5,4},{6,7},{7,6},{8,9},{9,8},{10,11... | collective-permute-start | bytes 4030472 | tf_op jit(solution)/shard_map/ppermute | solution.py:599
  252.1 83.9 %collective-permute-start.33 = (bf16[4,1312,128]{2,1,0:T(8,128)(2,1)}, bf16[4,1312,128]{2,1,0:T(8,128)(2,1)}, u32[]{:S(2)}, u32[]{:S(2)}) collective-permute-start(bf16[4,1312,128]{2,1,0:T(8,128)(2,1)} %collective-permute-done.32.refs_4_.refs_10_), channel_id=1, source_target_pairs={{0,1},{1,0},{2,3},{3,2},{4,5},{5,4},{6,7},{7,6},{8,9},{9,8},{10,11... | collective-permute-start | bytes 4030472 | tf_op jit(solution)/shard_map/ppermute | solution.py:599
  252.6 85.5 %collective-permute-start.35 = (bf16[4,1312,128]{2,1,0:T(8,128)(2,1)}, bf16[4,1312,128]{2,1,0:T(8,128)(2,1)}, u32[]{:S(2)}, u32[]{:S(2)}) collective-permute-start(bf16[4,1312,128]{2,1,0:T(8,128)(2,1)} %collective-permute-done.34.refs_6_.refs_12_), channel_id=1, source_target_pairs={{0,1},{1,0},{2,3},{3,2},{4,5},{5,4},{6,7},{7,6},{8,9},{9,8},{10,11... | collective-permute-start | bytes 4030472 | tf_op jit(solution)/shard_map/ppermute | solution.py:599
  278.0 60.1 %collective-permute-start.37 = (bf16[4,1312,128]{2,1,0:T(8,128)(2,1)}, bf16[4,1312,128]{2,1,0:T(8,128)(2,1)}, u32[]{:S(2)}, u32[]{:S(2)}) collective-permute-start(bf16[4,1312,128]{2,1,0:T(8,128)(2,1)} %collective-permute-done.36.refs_8_.refs_14_), channel_id=1, source_target_pairs={{0,1},{1,0},{2,3},{3,2},{4,5},{5,4},{6,7},{7,6},{8,9},{9,8},{10,11... | collective-permute-start | bytes 4030472 | tf_op jit(solution)/shard_map/ppermute | solution.py:599
  335.6 46.5 %collective-permute-start.52 = (bf16[1024,256]{1,0:T(8,128)(2,1)S(1)}, bf16[1024,256]{1,0:T(8,128)(2,1)S(1)}, u32[]{:S(2)}, u32[]{:S(2)}) collective-permute-start(bf16[1024,256]{1,0:T(8,128)(2,1)S(1)} %maximum_select_fusion.11), channel_id=1, source_target_pairs={{8,0},{12,4},{0,8},{4,12},{9,1},{13,5},{1,9},{5,13},{10,2},{14,6},... | collective-permute-start | bytes 1572872 | tf_op jit(solution)/shard_map/ppermute | solution.py:603
  467.5 130.6 %collective-permute-start.75 = (bf16[2,4,1312,128]{3,2,1,0:T(8,128)(2,1)}, bf16[2,4,1312,128]{3,2,1,0:T(8,128)(2,1)}, u32[]{:S(2)}, u32[]{:S(2)}) collective-permute-start(bf16[2,4,1312,128]{3,2,1,0:T(8,128)(2,1)} %get-tuple-element.142), channel_id=1, source_target_pairs={{0,1},{1,0},{2,3},{3,2},{4,5},{5,4},{6,7},{7,6},{8,9},{9,8},{10,11... | collective-permute-start | bytes 8060936 | tf_op jit(solution)/shard_map/ppermute | solution.py:599
  467.5 131.4 %collective-permute-start.76 = (bf16[2,4,1312,128]{3,2,1,0:T(8,128)(2,1)}, bf16[2,4,1312,128]{3,2,1,0:T(8,128)(2,1)}, u32[]{:S(2)}, u32[]{:S(2)}) collective-permute-start(bf16[2,4,1312,128]{3,2,1,0:T(8,128)(2,1)} %get-tuple-element.143), channel_id=1, source_target_pairs={{0,1},{1,0},{2,3},{3,2},{4,5},{5,4},{6,7},{7,6},{8,9},{9,8},{10,11... | collective-permute-start | bytes 8060936 | tf_op jit(solution)/shard_map/ppermute | solution.py:599
  526.6 61.3 %collective-permute-start.83 = (bf16[2,4,656,128]{3,2,1,0:T(8,128)(2,1)}, bf16[2,4,656,128]{3,2,1,0:T(8,128)(2,1)S(1)}, u32[]{:S(2)}, u32[]{:S(2)}) collective-permute-start(bf16[2,4,656,128]{3,2,1,0:T(8,128)(2,1)} %get-tuple-element.147), channel_id=1, source_target_pairs={{0,1},{1,0},{2,3},{3,2},{4,5},{5,4},{6,7},{7,6},{8,9},{9,8},{10,11... | collective-permute-start | bytes 4030472 | tf_op jit(solution)/shard_map/ppermute | solution.py:599
  615.8 77.4 %collective-permute-start.77 = (bf16[2,4,1312,128]{3,2,1,0:T(8,128)(2,1)}, bf16[2,4,1312,128]{3,2,1,0:T(8,128)(2,1)S(1)}, u32[]{:S(2)}, u32[]{:S(2)}) collective-permute-start(bf16[2,4,1312,128]{3,2,1,0:T(8,128)(2,1)} %get-tuple-element.145), channel_id=1, source_target_pairs={{0,16},{16,0},{1,17},{17,1},{2,18},{18,2},{3,19},{19,3},{4,20},{20... | collective-permute-start | bytes 8060936 | tf_op jit(solution)/shard_map/ppermute | solution.py:591
  630.1 62.0 %collective-permute-start.61 = (bf16[2,4,768,128]{3,2,1,0:T(8,128)(2,1)}, bf16[2,4,768,128]{3,2,1,0:T(8,128)(2,1)S(1)}, u32[]{:S(2)}, u32[]{:S(2)}) collective-permute-start(bf16[2,4,768,128]{3,2,1,0:T(8,128)(2,1)} %get-tuple-element.134), channel_id=1, source_target_pairs={{0,2},{1,3},{2,0},{3,1},{4,6},{5,7},{6,4},{7,5},{8,10},{9,11},{10,... | collective-permute-start | bytes 4718600 | tf_op jit(solution)/shard_map/ppermute | solution.py:595
  640.8 50.0 %collective-permute-start.86 = (bf16[4,656,128]{2,1,0:T(8,128)(2,1)S(1)}, bf16[4,656,128]{2,1,0:T(8,128)(2,1)S(1)}, u32[]{:S(2)}, u32[]{:S(2)}) collective-permute-start(bf16[4,656,128]{2,1,0:T(8,128)(2,1)S(1)} %fusion.8), channel_id=1, source_target_pairs={{0,16},{16,0},{1,17},{17,1},{2,18},{18,2},{3,19},{19,3},{4,20},{20... | collective-permute-start | bytes 2015240 | tf_op jit(solution)/shard_map/ppermute | solution.py:591
  649.9 47.5 %collective-permute-start.74 = (bf16[256,128]{1,0:T(8,128)(2,1)S(1)}, bf16[256,128]{1,0:T(8,128)(2,1)S(1)}, u32[]{:S(2)}, u32[]{:S(2)}) collective-permute-start(bf16[256,128]{1,0:T(8,128)(2,1)S(1)} %fusion.38), channel_id=1, source_target_pairs={{0,16},{16,0},{1,17},{17,1},{2,18},{18,2},{3,19},{19,3},{4,20},{20... | collective-permute-start | bytes 196616 | tf_op jit(solution)/shard_map/ppermute | solution.py:591
  (136 other events, 2547.5 us)

commit v2 on v1

v2 whole, which is shorter than its diff:
```python
import functools
import math

import jax
import jax.numpy as jnp
from jax import lax
from jax.experimental import pallas as pl
from jax.experimental.pallas import tpu as pltpu
from jax.sharding import PartitionSpec as P

WIDTH = 1024
HEAD = 64
REACH = 64
EPSILON = 1e-05
ROPE_THETA = 10000.0
MASKED_SCORE = -1e30
LANES = 128
SLOTS = 4
GROUPS = 4
GROUP = 256
TILE = 256
QUERY = 128
VMEM = 60 * 1024 * 1024
F32 = jnp.float32
BF16 = jnp.bfloat16


def nt(left, right):
    return lax.dot_general(left, right, (((1,), (1,)), ((), ())), preferred_element_type=F32)


def nn(left, right):
    return lax.dot_general(left, right, (((1,), (0,)), ((), ())), preferred_element_type=F32)


def tn(left, right):
    return lax.dot_general(left, right, (((0,), (0,)), ((), ())), preferred_element_type=F32)


def call(kernel, grid, in_specs, out_specs, out_shape, scratch, flops, moved, name):
    return pl.pallas_call(
        kernel,
        grid=grid,
        in_specs=in_specs,
        out_specs=out_specs,
        out_shape=out_shape,
        scratch_shapes=scratch,
        compiler_params=pltpu.CompilerParams(
            vmem_limit_bytes=VMEM, dimension_semantics=("arbitrary",)
        ),
        cost_estimate=pl.CostEstimate(flops=flops, bytes_accessed=moved, transcendentals=0),
        name=name,
    )


def resident(shape):
    zeros = (0,) * len(shape)
    return pl.BlockSpec(shape, lambda i: zeros, pipeline_mode=pl.Buffered(1))


def rows_of(width, tile=TILE):
    return pl.BlockSpec((tile, width), lambda i: (i, 0))


BLOCKS = pl.BlockSpec((SLOTS, TILE, 256), lambda i: (0, i, 0))


def later_rows(width):
    return pl.BlockSpec((TILE, width), lambda i: (jnp.maximum(i - GROUPS, 0), 0))


LATER_BLOCKS = pl.BlockSpec((SLOTS, TILE, 256), lambda i: (0, jnp.maximum(i - GROUPS, 0), 0))


def group_of(i):
    return jnp.minimum(i, GROUPS - 1)


def weight_rows(rows, at=0):
    return [
        pl.BlockSpec(
            (1, SLOTS, rows, LANES), lambda i, a=a: (a * GROUPS + group_of(i), 0, at, 0)
        )
        for a in range(2)
    ]


def joined_rows(halves, rows=slice(None)):
    return jnp.concatenate([w[0, o, rows, :] for o in range(SLOTS) for w in halves], axis=1)


def at_first(run):
    pl.when(pl.program_id(0) == 0)(run)


def add_up(total, part):
    @at_first
    def _():
        total[...] = part

    @pl.when((pl.program_id(0) > 0) & (pl.program_id(0) < GROUPS))
    def _():
        total[...] += part


def struct(shape, dtype):
    return jax.ShapeDtypeStruct(shape, dtype)


def whole_rows(slots, rows=slice(None)):
    return jnp.concatenate([slots[o, rows, :] for o in range(SLOTS)], axis=1)


def inner_rows(tile):
    return pl.ds(pl.multiple_of(pl.program_id(0) * tile + REACH, REACH), tile)


def put_rows(slots, total):
    for o in range(SLOTS):
        slots[o] = total[:, o * 256 : (o + 1) * 256].astype(slots.dtype)


def norm(values):
    average = jnp.mean(values, axis=1, keepdims=True)
    centered = values - average
    variance = jnp.mean(centered * centered, axis=1, keepdims=True)
    inverse = lax.rsqrt(variance + EPSILON)
    return centered * inverse, inverse


def norm_back(gradient, unit, inverse, gain):
    scaled = gradient * gain
    average = jnp.mean(scaled, axis=1, keepdims=True)
    crossed = jnp.mean(scaled * unit, axis=1, keepdims=True)
    return inverse * (scaled - average - unit * crossed)


def add_gain(gain_part, products):
    @pl.when(pl.program_id(0) == GROUPS)
    def _():
        gain_part[...] = jnp.zeros_like(gain_part)

    gain_part[...] += jnp.sum(products.reshape(-1, 8, WIDTH), axis=0)


def project_kernel(xs, gain, cosine, sine, low, high, q, k, v, normed, rows):
    @at_first
    def _():
        for at in range(0, rows.shape[0], QUERY):
            cut = slice(at, at + QUERY)
            values = jnp.concatenate([xs[o, cut, :] for o in range(SLOTS)], axis=1)
            made = (norm(values.astype(F32))[0] * gain[...]).astype(BF16)
            rows[cut, :] = made
            normed[cut, :] = made

    made = nt(rows[...], joined_rows((low, high)))
    c, s = cosine[...], sine[...]
    for t, out in ((0, q), (1, k)):
        first = made[:, t * GROUP : t * GROUP + LANES]
        second = made[:, t * GROUP + LANES : (t + 1) * GROUP]
        out[:, :LANES] = (first * c - second * s).astype(BF16)
        out[:, LANES:] = (second * c + first * s).astype(BF16)
    v[...] = made[:, 2 * GROUP :].astype(BF16)


def project(xs, gain, cosine, sine, weight):
    tokens = cosine.shape[0]
    return call(
        project_kernel,
        (GROUPS,),
        [resident(xs.shape), resident((1, WIDTH))]
        + [resident((tokens, LANES))] * 2
        + weight_rows(3 * GROUP),
        [pl.BlockSpec((tokens, GROUP), lambda i: (0, i))] * 3 + [resident((tokens, WIDTH))],
        [struct((tokens, WIDTH), BF16)] * 4,
        [pltpu.VMEM((tokens, WIDTH), BF16)],
        2 * tokens * WIDTH * 3 * WIDTH,
        10 * tokens * WIDTH + 6 * WIDTH * WIDTH,
        "project",
    )(xs, gain, cosine, sine, weight, weight)


def head_masks():
    lane = lax.broadcasted_iota(jnp.int32, (1, GROUP), 1)
    halves = [((lane % LANES) // 32 == h) for h in range(4)]
    wholes = [(lane // HEAD == h) for h in range(4)]
    return halves, wholes


def spread(rows, masks):
    return jnp.concatenate([rows * m.astype(BF16) for m in masks], axis=0)


def collect(stacked, masks):
    total = jnp.where(masks[0], stacked[0:QUERY], 0.0)
    for h in range(1, 4):
        total = jnp.where(masks[h], stacked[h * QUERY : (h + 1) * QUERY], total)
    return total


def attend_kernel(q, k, v, seg_query, seg_key, attended, probability):
    span = pl.ds(pl.multiple_of(pl.program_id(0) * QUERY, QUERY), QUERY + 2 * REACH)
    own = inner_rows(QUERY)
    shape = (QUERY, QUERY + 2 * REACH)
    offset = (
        lax.broadcasted_iota(jnp.int32, shape, 1)
        - lax.broadcasted_iota(jnp.int32, shape, 0)
        - REACH
    )
    allowed = (jnp.abs(offset) <= REACH) & ((seg_query[...] == seg_key[0]) | (offset == 0))
    halves, wholes = head_masks()
    for p in range(GROUPS):
        lanes = slice(p * GROUP, (p + 1) * GROUP)
        stacked = spread(q[own, lanes], halves)
        scores = nt(stacked, k[span, lanes]) * HEAD**-0.5
        scores = jnp.concatenate(
            [
                jnp.where(allowed, scores[h * QUERY : (h + 1) * QUERY], MASKED_SCORE)
                for h in range(4)
            ],
            axis=0,
        )
        exponent = jnp.exp(scores - jnp.max(scores, axis=1, keepdims=True))
        weight = (exponent * (1.0 / jnp.sum(exponent, axis=1, keepdims=True))).astype(BF16)
        probability[0, p] = weight
        attended[:, lanes] = collect(nn(weight, v[span, lanes]), wholes).astype(BF16)


def attend(q, k, v, seg_query, seg_key):
    tokens = seg_query.shape[0]
    blocks = tokens // QUERY
    span = QUERY + 2 * REACH
    return call(
        attend_kernel,
        (blocks,),
        [resident(q.shape)] * 3
        + [rows_of(1, QUERY), pl.BlockSpec((1, 1, span), lambda i: (i, 0, 0))],
        [
            rows_of(WIDTH, QUERY),
            pl.BlockSpec((1, GROUPS, 4 * QUERY, span), lambda i: (i, 0, 0, 0)),
        ],
        [
            struct((tokens, WIDTH), BF16),
            struct((blocks, GROUPS, 4 * QUERY, span), BF16),
        ],
        [],
        blocks * GROUPS * 2 * 2 * 4 * QUERY * span * GROUP,
        8 * tokens * WIDTH + blocks * GROUPS * 8 * QUERY * span,
        "attend",
    )(q, k, v, seg_query, seg_key)


def attend_back_kernel(*refs):
    q, grad, weights, k, v, cosine, sine = refs[:7]
    gq, gk, gv, edge_k, edge_v, sum_k, sum_v = refs[7:]
    step, steps = pl.program_id(0), pl.num_programs(0)
    tokens = gk.shape[0]

    @at_first
    def _():
        sum_k[...] = jnp.zeros_like(sum_k)
        sum_v[...] = jnp.zeros_like(sum_v)

    start = pl.multiple_of(step * QUERY, QUERY)
    span = pl.ds(start, QUERY + 2 * REACH)
    halves, wholes = head_masks()
    own = inner_rows(QUERY)
    c, s = cosine[own, :], sine[own, :]
    for p in range(GROUPS):
        lanes = slice(p * GROUP, (p + 1) * GROUP)
        queries = spread(q[own, lanes], halves)
        grads = spread(grad[:, lanes], wholes)
        block_k, block_v = k[span, lanes], v[span, lanes]
        weight = weights[0, p]
        wide = weight.astype(F32)
        d_weight = nt(grads, block_v)
        mean = jnp.sum(wide * d_weight, axis=1, keepdims=True)
        g_score = (wide * (d_weight - mean)).astype(BF16)
        made = collect(nn(g_score, block_k), halves) * HEAD**-0.5
        first, second = made[:, :LANES], made[:, LANES:]
        gq[:, p * GROUP : p * GROUP + LANES] = (first * c + second * s).astype(BF16)
        gq[:, p * GROUP + LANES : (p + 1) * GROUP] = (second * c - first * s).astype(BF16)
        sum_k[span, lanes] += tn(g_score, queries) * HEAD**-0.5
        sum_v[span, lanes] += tn(weight, grads)

    @pl.when(step == steps - 1)
    def _():
        for edge, total in ((edge_k, sum_k), (edge_v, sum_v)):
            edge[0 : 2 * REACH, :] = total[0 : 2 * REACH, :]
            edge[2 * REACH :, :] = total[pl.ds(tokens, 2 * REACH), :]
        for at in range(0, tokens, QUERY):
            own = pl.ds(REACH + at, QUERY)
            c, s = cosine[own, :], sine[own, :]
            for p in range(GROUPS):
                one, two = p * GROUP, p * GROUP + LANES
                first, second = sum_k[own, pl.ds(one, LANES)], sum_k[own, pl.ds(two, LANES)]
                gk[pl.ds(at, QUERY), pl.ds(one, LANES)] = (first * c + second * s).astype(BF16)
                gk[pl.ds(at, QUERY), pl.ds(two, LANES)] = (second * c - first * s).astype(BF16)
            gv[pl.ds(at, QUERY), :] = sum_v[own, :].astype(BF16)


def attend_back(q, grad, weights, k, v, cosine, sine):
    tokens = grad.shape[0]
    blocks = tokens // QUERY
    span = QUERY + 2 * REACH
    full = resident((tokens, WIDTH))
    edge = resident((4 * REACH, WIDTH))
    return call(
        attend_back_kernel,
        (blocks,),
        [
            resident(q.shape),
            rows_of(WIDTH, QUERY),
            pl.BlockSpec((1, GROUPS, 4 * QUERY, span), lambda i: (i, 0, 0, 0)),
            resident(q.shape),
            resident(q.shape),
            resident(cosine.shape),
            resident(cosine.shape),
        ],
        [rows_of(WIDTH, QUERY), full, full, edge, edge],
        [struct((tokens, WIDTH), BF16)] * 3 + [struct((4 * REACH, WIDTH), F32)] * 2,
        [pltpu.VMEM(q.shape, F32)] * 2,
        blocks * GROUPS * 2 * 4 * 4 * QUERY * span * GROUP,
        14 * tokens * WIDTH + blocks * GROUPS * 8 * QUERY * span,
        "attend_back",
    )(q, grad, weights, k, v, cosine, sine)


def mix_kernel(xs, attended, gain, low, high, mixed, normed, total):
    @pl.when(pl.program_id(0) < GROUPS)
    def _():
        add_up(total, nn(attended[...], joined_rows((low, high))))

    @pl.when(pl.program_id(0) >= GROUPS)
    def _():
        rows = step_rows()
        made = whole_rows(xs, between_rows()).astype(F32) + total[rows, :]
        mixed[...] = made.astype(mixed.dtype)
        normed[...] = (norm(made)[0] * gain[...]).astype(BF16)


def step_rows():
    return pl.ds(pl.multiple_of((pl.program_id(0) - GROUPS) * TILE, TILE), TILE)


def between_rows():
    at = (pl.program_id(0) - GROUPS) * TILE + REACH
    return pl.ds(pl.multiple_of(at, REACH), TILE)


def mix(xs, attended, gain, weight):
    tokens = attended.shape[0]
    return call(
        mix_kernel,
        (GROUPS + tokens // TILE,),
        [
            resident(xs.shape),
            pl.BlockSpec((tokens, GROUP), lambda i: (0, group_of(i))),
            resident((1, WIDTH)),
        ]
        + weight_rows(GROUP, 3),
        [later_rows(WIDTH)] * 2,
        [struct((tokens, WIDTH), BF16)] * 2,
        [pltpu.VMEM((tokens, WIDTH), F32)],
        2 * tokens * WIDTH * WIDTH,
        8 * tokens * WIDTH + 2 * WIDTH * WIDTH,
        "mix",
    )(xs, attended, gain, weight, weight)


def up_kernel(normed, low, high, hidden, slope, gelu):
    ff = hidden.shape[2]
    act = nt(normed[...], joined_rows((low, high), slice(0, ff)))
    gate = nt(normed[...], joined_rows((low, high), slice(ff, 2 * ff)))
    spread_to = 0.5 * (1.0 + lax.erf(act * math.sqrt(0.5)))
    curve = act * spread_to
    density = jnp.exp(act * act * -0.5) * (1.0 / math.sqrt(2.0 * math.pi))
    slope[0] = (gate * (spread_to + act * density)).astype(BF16)
    gelu[0] = curve.astype(BF16)
    hidden[0] = (curve * gate).astype(BF16)


def units_of(tokens, ff):
    return pl.BlockSpec((1, tokens, ff), lambda i: (group_of(i), 0, 0))


def feed_up(normed, weight):
    tokens, ff = normed.shape[0], weight.shape[2] // 2
    return call(
        up_kernel,
        (GROUPS,),
        [resident((tokens, WIDTH))] + weight_rows(2 * ff),
        [units_of(tokens, ff)] * 3,
        [struct((GROUPS, tokens, ff), BF16)] * 3,
        [],
        2 * tokens * WIDTH * 2 * GROUPS * ff,
        2 * tokens * WIDTH + 2 * GROUPS * ff * (3 * tokens + 2 * WIDTH),
        "feed_up",
    )(normed, weight, weight)


def down_kernel(hidden, mixed, low, high, early, late, total):
    @pl.when(pl.program_id(0) < GROUPS)
    def _():
        add_up(total, nn(hidden[0], joined_rows((low, high))))

    half = GROUPS + total.shape[0] // TILE // 2

    @pl.when((pl.program_id(0) >= GROUPS) & (pl.program_id(0) < half))
    def _():
        put_rows(early, mixed[...].astype(F32) + total[step_rows(), :])

    @pl.when(pl.program_id(0) >= half)
    def _():
        put_rows(late, mixed[...].astype(F32) + total[step_rows(), :])


def feed_down(hidden, mixed, weight):
    _, tokens, ff = hidden.shape
    steps = tokens // TILE // 2
    return call(
        down_kernel,
        (GROUPS + tokens // TILE,),
        [units_of(tokens, ff), later_rows(WIDTH)] + weight_rows(ff),
        [
            pl.BlockSpec(
                (SLOTS, TILE, 256),
                lambda i, first=first: (0, jnp.clip(i - GROUPS - first, 0, steps - 1), 0),
            )
            for first in (0, steps)
        ],
        [struct((SLOTS, tokens // 2, 256), BF16)] * 2,
        [pltpu.VMEM((tokens, WIDTH), F32)],
        2 * tokens * WIDTH * GROUPS * ff,
        4 * tokens * WIDTH + 2 * GROUPS * ff * (tokens + WIDTH),
        "feed_down",
    )(hidden, mixed, weight, weight)


def down_back_kernel(cots, slope, gelu, low, high, g_act, g_gate):
    g_hidden = nt(whole_rows(cots), joined_rows((low, high)))
    g_act[0] = (g_hidden * slope[0].astype(F32)).astype(BF16)
    g_gate[0] = (g_hidden * gelu[0].astype(F32)).astype(BF16)


def down_back(cots, slope, gelu, weight):
    _, tokens, ff = slope.shape
    return call(
        down_back_kernel,
        (GROUPS,),
        [resident(cots.shape)] + [units_of(tokens, ff)] * 2 + weight_rows(ff),
        [units_of(tokens, ff)] * 2,
        [struct((GROUPS, tokens, ff), BF16)] * 2,
        [],
        2 * tokens * WIDTH * GROUPS * ff,
        2 * tokens * WIDTH + 2 * GROUPS * ff * (4 * tokens + WIDTH),
        "down_back",
    )(cots, slope, gelu, weight, weight)


def up_back_kernel(*refs):
    cots, g_act, g_gate, mixed, gain, low, high, out_low, out_high = refs[:9]
    g_branch, g_attended, gain_part, total = refs[9:]
    ff = g_act.shape[2]

    @pl.when(pl.program_id(0) < GROUPS)
    def _():
        part = nn(g_act[0], joined_rows((low, high), slice(0, ff)))
        add_up(total, part + nn(g_gate[0], joined_rows((low, high), slice(ff, 2 * ff))))

    @pl.when(pl.program_id(0) >= GROUPS)
    def _():
        gradient = total[step_rows(), :]
        unit, inverse = norm(mixed[...].astype(F32))
        add_gain(gain_part, gradient * unit)
        made = whole_rows(cots).astype(F32) + norm_back(gradient, unit, inverse, gain[...])
        branch = made.astype(BF16)
        g_branch[...] = branch
        for p in range(GROUPS):
            parts = [ref[p, o] for o in range(SLOTS) for ref in (out_low, out_high)]
            held = jnp.concatenate(parts, axis=1)
            g_attended[:, p * GROUP : (p + 1) * GROUP] = nt(branch, held).astype(BF16)


def up_back(cots, g_act, g_gate, mixed, gain, up, heads):
    _, tokens, ff = g_act.shape
    out_shape = (GROUPS, SLOTS, GROUP, LANES)
    return call(
        up_back_kernel,
        (GROUPS + tokens // TILE,),
        [LATER_BLOCKS]
        + [units_of(tokens, ff)] * 2
        + [later_rows(WIDTH), resident((1, WIDTH))]
        + weight_rows(2 * ff)
        + [
            pl.BlockSpec(out_shape, lambda i, a=a: (a, 0, 3, 0), pipeline_mode=pl.Buffered(1))
            for a in range(2)
        ],
        [later_rows(WIDTH)] * 2 + [resident((8, WIDTH))],
        [struct((tokens, WIDTH), BF16)] * 2 + [struct((8, WIDTH), F32)],
        [pltpu.VMEM((tokens, WIDTH), F32)],
        2 * tokens * WIDTH * (2 * GROUPS * ff + WIDTH),
        8 * tokens * WIDTH + 4 * GROUPS * ff * (tokens + WIDTH),
        "up_back",
    )(cots, g_act, g_gate, mixed, gain, up, up, heads, heads)


def unproject_kernel(xs, gq, gk, gv, g_branch, gain, low, high, outs, gain_part, total):
    @pl.when(pl.program_id(0) < GROUPS)
    def _():
        inner = jnp.concatenate([gq[...], gk[...], gv[...]], axis=1)
        add_up(total, nn(inner, joined_rows((low, high))))

    @pl.when(pl.program_id(0) >= GROUPS)
    def _():
        gradient = total[step_rows(), :]
        unit, inverse = norm(whole_rows(xs, between_rows()).astype(F32))
        add_gain(gain_part, gradient * unit)
        back = norm_back(gradient, unit, inverse, gain[...])
        put_rows(outs, g_branch[...].astype(F32) + back)


def unproject(xs, gq, gk, gv, g_branch, gain, weight):
    tokens = gq.shape[0]
    return call(
        unproject_kernel,
        (GROUPS + tokens // TILE,),
        [resident(xs.shape)]
        + [pl.BlockSpec((tokens, GROUP), lambda i: (0, group_of(i)))] * 3
        + [later_rows(WIDTH), resident((1, WIDTH))]
        + weight_rows(3 * GROUP),
        [LATER_BLOCKS, resident((8, WIDTH))],
        [struct((SLOTS, tokens, 256), BF16), struct((8, WIDTH), F32)],
        [pltpu.VMEM((tokens, WIDTH), F32)],
        2 * tokens * WIDTH * 3 * WIDTH,
        12 * tokens * WIDTH + 6 * WIDTH * WIDTH,
        "unproject",
    )(xs, gq, gk, gv, g_branch, gain, weight, weight)


def outer_kernel(pairs, count, *refs):
    inner, outer, out = refs[: len(pairs)], refs[len(pairs) : -1], refs[-1]
    tokens = inner[0].shape[-2]

    def make(left, right):
        left = left[0] if len(left.shape) == 3 else left[...]
        if len(right.shape) == 3:
            right = whole_rows(right)
        else:
            right = right[pl.ds((right.shape[0] - tokens) // 2, tokens), :]
        made = tn(left, right)
        for a in range(2):
            for o in range(SLOTS):
                at = o * 256 + a * LANES
                out[a, 0, o] = made[:, at : at + LANES].astype(BF16)

    for t, j in enumerate(pairs):
        pl.when(pl.program_id(0) % count == t)(functools.partial(make, inner[t], outer[j]))


def outer_product(pairs, inner, outer):
    count = len(inner)
    tokens = inner[0].shape[-2]
    width = inner[0].shape[2] if inner[0].ndim == 3 else GROUP
    rows = count * width

    def inner_block(value):
        if value.ndim == 3:
            return pl.BlockSpec((1, tokens, width), lambda i: (i // count, 0, 0))
        return pl.BlockSpec((tokens, GROUP), lambda i: (0, i // count))

    return call(
        functools.partial(outer_kernel, pairs, count),
        (GROUPS * count,),
        [inner_block(value) for value in inner] + [resident(value.shape) for value in outer],
        [
            pl.BlockSpec(
                (2, 1, SLOTS, width, LANES), lambda i: (0, i // count, 0, i % count, 0)
            )
        ],
        [struct((2, GROUPS, SLOTS, rows, LANES), BF16)],
        [],
        2 * tokens * GROUPS * rows * WIDTH,
        8 * rows * (tokens + WIDTH) + 2 * tokens * WIDTH,
        "outer_product",
    )(*inner, *outer)[0]


def over_dp(value):
    return lax.ppermute(value, "dp", [(0, 1), (1, 0)])


def over_chip(value):
    return lax.ppermute(value, "col", [(i, i ^ 2) for i in range(4)])


def over_core(value):
    return lax.ppermute(value, "col", [(i, i ^ 1) for i in range(4)])


def exchange(value):
    return lax.all_to_all(value, "row", 0, 0)


def after(value, *earlier):
    return lax.optimization_barrier((value,) + earlier)[0]


def own_half(shard):
    return lax.dynamic_slice_in_dim(shard, lax.axis_index("dp") * LANES, LANES, 1)


def gather_rows(half):
    return exchange(jnp.broadcast_to(half, (SLOTS,) + half.shape))


def gather_groups(own):
    return lax.all_gather(own, ("dp", "col"), axis=0, tiled=False)


def reduce_groups(parts):
    parts = parts.reshape((2 * GROUPS,) + parts.shape[2:])
    return lax.psum_scatter(parts, ("dp", "col"), scatter_dimension=0, tiled=False)


def sum_rows(parts):
    half = jnp.sum(parts.astype(F32), axis=0).astype(BF16)
    other = over_dp(half)
    first = lax.axis_index("dp") == 0
    return jnp.where(
        first,
        jnp.concatenate([half, other], axis=1),
        jnp.concatenate([other, half], axis=1),
    ).astype(F32)


def sum_gains(parts):
    both = parts + over_dp(parts)
    both = both + over_chip(both)
    both = both + over_core(both)
    for bit in (1, 2):
        both = both + lax.ppermute(both, "row", [(i, i ^ bit) for i in range(SLOTS)])
    return lax.dynamic_slice_in_dim(both, lax.axis_index("row") * 256, 256, 1)


def groups_of(whole):
    rows = whole.shape[0] // GROUPS
    cut = whole.reshape(GROUPS, rows, SLOTS, 2, LANES).transpose(3, 0, 2, 1, 4)
    return cut.reshape(2 * GROUPS, SLOTS, rows, LANES)


def whole_of(parts, types):
    cut = parts.transpose(1, 3, 2, 0, 4).reshape(GROUPS, types, -1, WIDTH)
    return [cut[:, t].reshape(-1, WIDTH) for t in range(types)]


def split_heads(rows):
    return rows.reshape(-1, 4, 2, 32, rows.shape[1]).swapaxes(1, 2).reshape(rows.shape)


def join_heads(rows):
    return rows.reshape(-1, 2, 4, 32, rows.shape[1]).swapaxes(1, 2).reshape(rows.shape)


def positions_and_masks(segments, valid, first, tokens):
    length = segments.shape[0]
    index = first - REACH + jnp.arange(tokens + 2 * REACH, dtype=jnp.int32)
    pads = (REACH, REACH)
    near = lax.dynamic_slice_in_dim(jnp.pad(segments, pads), first, tokens + 2 * REACH, 0)
    ids = jnp.arange(64, dtype=jnp.int32)
    before = jnp.sum((segments[None, :] < ids[:, None]).astype(jnp.int32), axis=1)
    begin = jnp.sum(jnp.where(near[:, None] == ids[None, :], before[None, :], 0), axis=1)
    where_in = (index - begin).astype(F32)
    frequency = ROPE_THETA ** (-(jnp.arange(32, dtype=F32) * 2.0) / HEAD)
    angles = where_in[:, None] * frequency[None, :]
    cosine, sine = jnp.tile(jnp.cos(angles), (1, 4)), jnp.tile(jnp.sin(angles), (1, 4))
    code = jnp.pad(jnp.where(valid == 1, segments, -1), pads, constant_values=-1)
    code = lax.dynamic_slice_in_dim(code, first, tokens + 2 * REACH, 0)
    span = QUERY + 2 * REACH
    keys = jnp.stack([code[i : i + span] for i in range(0, tokens, QUERY)])[:, None, :]
    return cosine, sine, near[REACH:-REACH, None], keys


def body(
    dp,
    rows,
    cols,
    tokens_in,
    w_query,
    w_key,
    w_value,
    w_out,
    w_act,
    w_gate,
    w_down,
    gain_attn,
    gain_ffn,
    cotangent,
    segment_ids,
    valid_mask,
):
    tokens = tokens_in.shape[0] // rows
    length = segment_ids.shape[1]
    own_slice = (dp, rows, cols) == (2, 4, 4) and rows * tokens == length
    gains = jnp.stack([gain_attn, gain_ffn])
    at = (lax.axis_index("col") * rows + lax.axis_index("row")) * tokens
    sequence, first = at // length, at % length
    count = rows * cols
    joins = [i for i in range(count - 1) if ((i + 1) * tokens) % length]
    upward, downward = [(i, i + 1) for i in joins], [(i + 1, i) for i in joins]

    def shift(value, perm):
        place_of = [(i % rows) * cols + i // rows for i in range(count)]
        return lax.ppermute(value, ("row", "col"), [(place_of[i], place_of[j]) for i, j in perm])

    if own_slice:
        marks = jnp.concatenate([segment_ids, valid_mask]).astype(BF16).reshape(-1, LANES)
        heads_half = jnp.concatenate(
            [
                split_heads(own_half(w_query.T)),
                split_heads(own_half(w_key.T)),
                own_half(w_value.T),
                own_half(w_out),
                marks,
                gains.reshape(4, LANES),
                jnp.zeros((12, LANES), BF16),
            ],
            axis=0,
        )
        up_half = jnp.concatenate([own_half(w_act.T), own_half(w_gate.T)], axis=0)
        padded = jnp.pad(tokens_in, ((REACH, REACH), (0, 0)))
        spans = [padded[j * tokens : (j + 1) * tokens + 2 * REACH] for j in range(rows)]
        heads_own = gather_rows(heads_half)
        heads_w = gather_groups(heads_own[:, :WIDTH])
        up_own = gather_rows(after(up_half, heads_own))
        up_w = gather_groups(up_own)
        last = WIDTH + marks.shape[0]
        marks = heads_own[:, WIDTH:last].reshape(rows, 2, length)
        marks = lax.dynamic_index_in_dim(marks, sequence, 0, False).astype(jnp.int32)
        gain_slots = heads_own[:, last : last + 4].reshape(SLOTS, 2, 256)
        tables = positions_and_masks(*marks, first, tokens)
        xs = exchange(after(jnp.stack(spans), up_own, *tables))
        down_own = gather_rows(after(own_half(w_down), xs))
    else:
        xs = exchange(tokens_in.reshape(rows, tokens, 256))
        below, above = shift(xs[:, -REACH:], upward), shift(xs[:, :REACH], downward)
        xs = jnp.concatenate([below, xs, above], axis=1)
        cots = exchange(cotangent.reshape(rows, tokens, 256))
        gain_slots = exchange(jnp.broadcast_to(gains, (rows, 2, 256)))
        marks = lax.all_gather(jnp.stack([segment_ids, valid_mask]), "row", axis=1, tiled=True)
        marks = lax.dynamic_index_in_dim(marks, sequence, 1, False)
        tables = positions_and_masks(*marks, first, tokens)

        def full(value, inner_first):
            first, second = ("col", "row") if inner_first else ("row", "col")
            value = lax.all_gather(value, first, axis=0, tiled=True)
            value = lax.all_gather(value, second, axis=1, tiled=True)
            return value if inner_first else value.T

        def joined(*parts):
            return jnp.concatenate([groups_of(part) for part in parts], axis=2)

        heads_w = joined(
            split_heads(full(w_query, False)),
            split_heads(full(w_key, False)),
            full(w_value, False),
            full(w_out, True),
        )
        up_w = joined(full(w_act, False), full(w_gate, False))
        down_w = joined(full(w_down, True))
    gain_rows = gain_slots.swapaxes(0, 1).reshape(2, 1, WIDTH).astype(F32)
    cosine, sine, seg_query, seg_key = tables

    q, k, v, normed_attn = project(xs, gain_rows[0], cosine, sine, heads_w)
    if own_slice:
        down_own = after(down_own, q)
        down_w = gather_groups(down_own)
        cots = exchange(after(cotangent.reshape(rows, tokens, 256), down_own))
    attended, weights = attend(q, k, v, seg_query, seg_key)
    mixed, normed_ffn = mix(xs, attended, gain_rows[1], heads_w)
    hidden, slope, gelu = feed_up(normed_ffn, up_w)
    early, late = feed_down(hidden, mixed, down_w)
    hidden = after(hidden, early)
    early = exchange(after(early, cots))
    late = exchange(after(late, early))
    layer_out = jnp.concatenate([early, late], axis=1)
    down_parts = outer_product((0,), [hidden], [cots])
    g_act, g_gate = down_back(cots, after(slope, down_parts), gelu, down_w)
    up_parts = outer_product((0, 0), [after(g_act, early), g_gate], [normed_ffn])
    g_branch, g_attended, gain_part_ffn = up_back(
        cots, after(g_act, up_parts), g_gate, mixed, gain_rows[1], up_w, heads_w
    )
    if own_slice:
        down_own, up_own = reduce_groups(down_parts), reduce_groups(up_parts)
        down_sum = exchange(after(down_own, late))
        g_attended = after(g_attended, late, down_own)
    gq, gk, gv, edge_k, edge_v = attend_back(q, g_attended, weights, k, v, cosine, sine)
    to_low = jnp.concatenate([edge_k[:REACH], edge_v[:REACH]], axis=1).astype(BF16)
    to_high = jnp.concatenate([edge_k[-REACH:], edge_v[-REACH:]], axis=1).astype(BF16)
    from_high = shift(to_low, downward).astype(F32)
    from_low = shift(to_high, upward).astype(F32)

    def turned(value, c, s):
        cut = value.reshape(-1, GROUPS, 2, LANES)
        first, second = cut[:, :, 0], cut[:, :, 1]
        c, s = c[:, None], s[:, None]
        back = jnp.stack([first * c + second * s, second * c - first * s], axis=2)
        return back.reshape(value.shape).astype(BF16)

    near_k = edge_k[REACH : 2 * REACH] + from_low[:, :WIDTH]
    near_v = edge_v[REACH : 2 * REACH] + from_low[:, WIDTH:]
    last_k = edge_k[2 * REACH : 3 * REACH] + from_high[:, :WIDTH]
    last_v = edge_v[2 * REACH : 3 * REACH] + from_high[:, WIDTH:]
    gk = gk.at[:REACH].set(turned(near_k, cosine[REACH : 2 * REACH], sine[REACH : 2 * REACH]))
    gk = gk.at[-REACH:].set(
        turned(last_k, cosine[-2 * REACH : -REACH], sine[-2 * REACH : -REACH])
    )
    gv = gv.at[:REACH].set(near_v.astype(BF16))
    gv = gv.at[-REACH:].set(last_v.astype(BF16))

    if own_slice:
        gq = after(gq, down_sum, up_own)
    heads_parts = outer_product(
        (0, 0, 0, 1), [gq, gk, gv, attended], [normed_attn, g_branch]
    )
    grad_slots, gain_part_attn = unproject(
        xs, after(gq, heads_parts), gk, gv, g_branch, gain_rows[0], heads_w
    )

    gain_parts = jnp.stack([jnp.sum(gain_part_attn, axis=0), jnp.sum(gain_part_ffn, axis=0)])
    if own_slice:
        up_sum = exchange(after(up_own, down_sum))
        token_gradient = exchange(after(grad_slots, up_sum))
        gain_grads = sum_gains(gain_parts)
        heads_sum = exchange(after(reduce_groups(heads_parts), token_gradient, gain_grads))
        down_sum, up_sum, heads_sum = (sum_rows(v) for v in (down_sum, up_sum, heads_sum))
        ff = w_act.shape[1]
        grads = (
            join_heads(heads_sum[:GROUP]).T,
            join_heads(heads_sum[GROUP : 2 * GROUP]).T,
            heads_sum[2 * GROUP : 3 * GROUP].T,
            heads_sum[3 * GROUP :],
            up_sum[:ff].T,
            up_sum[ff:].T,
            down_sum,
        )
    else:

        def share(value, inner_first):
            first, second = ("col", "row") if inner_first else ("row", "col")
            value = value if inner_first else value.T
            value = lax.psum_scatter(value, first, scatter_dimension=0, tiled=True)
            value = lax.psum_scatter(value, second, scatter_dimension=1, tiled=True)
            return lax.psum(value, "dp").astype(F32)

        token_gradient = exchange(grad_slots)
        (down_whole,) = whole_of(down_parts, 1)
        act_whole, gate_whole = whole_of(up_parts, 2)
        query_whole, key_whole, value_whole, out_whole = whole_of(heads_parts, 4)
        grads = (
            share(join_heads(query_whole), False),
            share(join_heads(key_whole), False),
            share(value_whole, False),
            share(out_whole, True),
            share(act_whole, False),
            share(gate_whole, False),
            share(down_whole, True),
        )
        totals = lax.psum(gain_parts, ("dp", "row", "col")).reshape(2, SLOTS, 256)
        gain_grads = lax.dynamic_index_in_dim(totals, lax.axis_index("row"), 1, False)
    layer_out = layer_out.reshape(-1, 256)
    token_gradient = token_gradient.reshape(-1, 256).astype(F32)
    return (layer_out, token_gradient) + grads + (gain_grads[0], gain_grads[1])


def solution(mesh):
    sizes = tuple(mesh.shape[axis] for axis in ("dp", "row", "col"))
    in_specs = (
        P(("dp", "col"), "row"),
        P("row", "col"),
        P("row", "col"),
        P("row", "col"),
        P("col", "row"),
        P("row", "col"),
        P("row", "col"),
        P("col", "row"),
        P("row"),
        P("row"),
        P(("dp", "col"), "row"),
        P(("dp", "row"), None),
        P(("dp", "row"), None),
    )
    out_specs = (
        P(("dp", "col"), "row"),
        P(("dp", "col"), "row"),
        P("row", "col"),
        P("row", "col"),
        P("row", "col"),
        P("col", "row"),
        P("row", "col"),
        P("row", "col"),
        P("col", "row"),
        P("row"),
        P("row"),
    )
    return jax.shard_map(
        functools.partial(body, *sizes),
        mesh=mesh,
        in_specs=in_specs,
        out_specs=out_specs,
        check_vma=False,
    )
```

time: 772 us -> 561 us (0.73)
  waiting for transfers between devices: 299 us -> 142 us
  starting transfers between devices: 143 us -> 57.5 us
  blocking collectives: 14.2 us -> 68.4 us
  other arithmetic: 40.9 us -> 25.8 us
  local copies, waits for them, and re-layouts: 47 us -> 32.6 us
  between operations: 2 us -> 15.2 us
    ppermute x42 -> x2, waiting for transfers between devices: 141 us -> 32.2 us  [sum_gains(): lax.ppermute(both, 'row', [(i, i ^ bit) for i in range(SLOTS)])]
    all_to_all x0 -> x9, waiting for transfers between devices: none -> 88 us  [exchange(): return lax.all_to_all(value, 'row', 0, 0)]
    ppermute x42 -> x2, starting transfers between devices: 89.1 us -> 6.62 us  [sum_gains(): lax.ppermute(both, 'row', [(i, i ^ bit) for i in range(SLOTS)])]
    ppermute x15 -> x4, waiting for transfers between devices: 84.6 us -> 11.1 us  [over_dp(): return lax.ppermute(value, 'dp', [(0, 1), (1, 0)])]
    all_to_all x0 -> x2, blocking collectives: none -> 68.4 us  [exchange(): return lax.all_to_all(value, 'row', 0, 0)]
    ppermute x11 -> x1, waiting for transfers between devices: 66 us -> 2.46 us  [over_chip(): return lax.ppermute(value, 'col', [(i, i ^ 2) for i in range(4)])]
    all_to_all x0 -> x9, starting transfers between devices: none -> 38.2 us  [exchange(): return lax.all_to_all(value, 'row', 0, 0)]
    ppermute x4 -> x2, starting transfers between devices: 23.3 us -> 5.75 us  [shift(): lax.ppermute(value, ('row', 'col'), [(place_of[i], place_of[j]) for i, j...]
  transfers between devices with their start and end apart: 97 -> 25, of which waited for: 33 -> 13; matrix products, arithmetic and copies ran while one was open for 10% -> 8% of each run, Pallas kernels for 19% -> 33%
where the time goes in v2:
time: 561 us; the launch traced here: 553 us
  Pallas kernels  212 us (38%)
  waiting for transfers between devices  142 us (25%)
  blocking collectives  68.4 us (12%)
  starting transfers between devices  57.5 us (10%)
  local copies, waits for them, and re-layouts  32.6 us (6%)
  other arithmetic  25.8 us (5%)
  between operations  15.2 us (3%)
    all_to_all x9, waiting for transfers between devices, exchange(): return lax.all_to_all(value, 'row', 0, 0)  88 us
    all_to_all x2, blocking collectives, exchange(): return lax.all_to_all(value, 'row', 0, 0)  68.4 us
    pallas_call x3, Pallas kernels, outer_product(): call(functools.partial(outer_kernel, pairs, count), (GROUPS * count,), [i...  48.9 us
    all_to_all x9, starting transfers between devices, exchange(): return lax.all_to_all(value, 'row', 0, 0)  38.2 us
    ppermute x2, waiting for transfers between devices, sum_gains(): lax.ppermute(both, 'row', [(i, i ^ bit) for i in range(SLOTS)])  32.2 us
    pallas_call x1, Pallas kernels, attend_back(): call(attend_back_kernel, (blocks,), [resident(q.shape), rows_of(WIDTH, QU...  26.8 us
    pallas_call x1, Pallas kernels, up_back(): call(up_back_kernel, (GROUPS + tokens // TILE,), [LATER_BLOCKS] + [units_...  26.6 us
    pallas_call x1, Pallas kernels, feed_up(): call(up_kernel, (GROUPS,), [resident((tokens, WIDTH))] + weight_rows(2 *...  18.7 us
  transfers between devices with their start and end apart: 25, of which 13 were waited for; matrix products, arithmetic and copies ran while one was open for 8% of the time, Pallas kernels for 33%

profile of v2, /device:TPU:0, one launch (start us, length us, event | category | flops | bytes accessed | tf_op | source)
XLA Modules:
  0.0 552.9 jit_solution(16123613700899581956)
XLA Ops:
  13.5 33.6 %all_to_all.55 = bf16[4,1104,128]{2,1,0:T(8,128)(2,1)S(1)} all-to-all(bf16[4,1104,128]{2,1,0:T(8,128)(2,1)S(1)} %broadcast_in_dim.45), channel_id=1, replica_groups=mesh['dp'=2,'row'=4,'col'=4] {'row'}, dimensions={0} | all-to-all | bytes 2260992 | tf_op jit(solution)/shard_map/all_to_all | solution.py:602
  49.8 34.8 %all_to_all.56 = bf16[4,1312,128]{2,1,0:T(8,128)(2,1)} all-to-all(bf16[4,1312,128]{2,1,0:T(8,128)(2,1)S(1)} %broadcast_in_dim.46), channel_id=1, replica_groups=mesh['dp'=2,'row'=4,'col'=4] {'row'}, dimensions={0} | all-to-all | bytes 2686976 | tf_op jit(solution)/shard_map/all_to_all | solution.py:602
  94.0 52.7 %all-to-all-done.2.xs = bf16[4,1152,256]{2,1,0:T(8,128)(2,1)S(1)} async-done(((bf16[4,1152,256]{2,1,0:T(8,128)(2,1)}), bf16[4,1152,256]{2,1,0:T(8,128)(2,1)S(1)}, u32[]{:S(2)}, u32[]{:S(2)}) %all-to-all-start.2) | async-done | bytes 2359328 | tf_op jit(solution)/shard_map/all_to_all | solution.py:602
  156.8 14.0 %project.1 = (bf16[1152,1024]{1,0:T(8,128)(2,1)}, bf16[1152,1024]{1,0:T(8,128)(2,1)}, bf16[1152,1024]{1,0:T(8,128)(2,1)}, bf16[1152,1024]{1,0:T(8,128)(2,1)}) custom-call(bf16[4,1152,256]{2,1,0:T(8,128)(2,1)} %copy-done.2, f32[1,1024]{1,0:T(1,128)} %bitcast.145, f32[1152,128]{1,0:T(8,128)} %copy.93.cosine.refs_5_, f32[1152,128]{1,0:T(8,128)} %copy.94.sine.refs_6_, ...), custom_call_target="tpu_custom_call" | custom-call | flops 7247757312 | bytes 18087936 | tf_op jit(solution)/shard_map/project/pallas_call | solution.py:168
  178.5 17.2 %attend.1 = (bf16[1024,1024]{1,0:T(8,128)(2,1)}, bf16[8,4,512,256]{3,2,1,0:T(8,128)(2,1)}) custom-call(bf16[1152,1024]{1,0:T(8,128)(2,1)} %get-tuple-element.104.q.refs_0_, bf16[1152,1024]{1,0:T(8,128)(2,1)} %get-tuple-element.105.k.refs_3_, bf16[1152,1024]{1,0:T(8,128)(2,1)} %get-tuple-element.106.v.refs_4_, s32[1024,1]{1,0:T(8,128)} %copy.95.seg_query, ...), custom_call_target="tpu_custom_call" | custom-call | flops 4294967296 | bytes 16777216 | tf_op jit(solution)/shard_map/attend/pallas_call | solution.py:233
  195.7 10.6 %mix.1 = (bf16[1024,1024]{1,0:T(8,128)(2,1)}, bf16[1024,1024]{1,0:T(8,128)(2,1)}) custom-call(bf16[4,1152,256]{2,1,0:T(8,128)(2,1)} %copy-done.2, bf16[1024,1024]{1,0:T(8,128)(2,1)} %get-tuple-element.107.attended.refs_3_, f32[1,1024]{1,0:T(1,128)} %bitcast.142, bf16[8,4,1024,128]{3,2,1,0:T(8,128)(2,1)} %bitcast.96, bf16[8,4,1024,128]{3,2,1,0:T(8,128)(2,1)} %bitcast.97), custom_call_target="tpu_custom_call" | custom-call | flops 2147483648 | bytes 10485760 | tf_op jit(solution)/shard_map/mix/pallas_call | solution.py:353
  206.3 18.7 %feed_up.1 = (bf16[4,1024,656]{2,1,0:T(8,128)(2,1)}, bf16[4,1024,656]{2,1,0:T(8,128)(2,1)}, bf16[4,1024,656]{2,1,0:T(8,128)(2,1)}) custom-call(bf16[1024,1024]{1,0:T(8,128)(2,1)} %get-tuple-element.108.normed.refs_2_, bf16[8,4,1312,128]{3,2,1,0:T(8,128)(2,1)} %bitcast.102, bf16[8,4,1312,128]{3,2,1,0:T(8,128)(2,1)} %bitcast.103), custom_call_target="tpu_custom_call" | custom-call | flops 11005853696 | bytes 28966912 | tf_op jit(solution)/shard_map/feed_up/pallas_call | solution.py:389
  225.1 14.2 %feed_down.1 = (bf16[4,512,256]{2,1,0:T(8,128)(2,1)}, bf16[4,512,256]{2,1,0:T(8,128)(2,1)}) custom-call(bf16[4,1024,656]{2,1,0:T(8,128)(2,1)} %get-tuple-element.119.hidden.refs_0_, bf16[1024,1024]{1,0:T(8,128)(2,1)} %get-tuple-element.110.mixed.refs_3_, bf16[8,4,656,128]{3,2,1,0:T(8,128)(2,1)} %bitcast.106, bf16[8,4,656,128]{3,2,1,0:T(8,128)(2,1)} %bitcast.107), custom_call_target="tpu_custom_call" | custom-call | flops 5502926848 | bytes 14942208 | tf_op jit(solution)/shard_map/feed_down/pallas_call | solution.py:421
  240.6 9.9 %outer_product.3 = bf16[2,4,4,656,128]{4,3,2,1,0:T(8,128)(2,1)} custom-call(bf16[4,1024,656]{2,1,0:T(8,128)(2,1)} %get-tuple-element.119.hidden.refs_0_, bf16[4,1024,256]{2,1,0:T(8,128)(2,1)} %copy-done.3), custom_call_target="tpu_custom_call" | custom-call | flops 5502926848 | bytes 12845056 | tf_op jit(solution)/shard_map/outer_product/pallas_call | solution.py:572
  255.8 16.9 %down_back.1 = (bf16[4,1024,656]{2,1,0:T(8,128)(2,1)}, bf16[4,1024,656]{2,1,0:T(8,128)(2,1)}) custom-call(bf16[4,1024,256]{2,1,0:T(8,128)(2,1)} %copy-done.3, bf16[4,1024,656]{2,1,0:T(8,128)(2,1)} %get-tuple-element.120.slope, bf16[4,1024,656]{2,1,0:T(8,128)(2,1)} %get-tuple-element.121.gelu, bf16[8,4,656,128]{3,2,1,0:T(8,128)(2,1)} %bitcast.108, ...), custom_call_target="tpu_custom_call" | custom-call | flops 5502926848 | bytes 28966912 | tf_op jit(solution)/shard_map/down_back/pallas_call | solution.py:448
  272.7 6.0 %all-to-all-done.5 = bf16[4,512,256]{2,1,0:T(8,128)(2,1)S(1)} async-done(((bf16[4,512,256]{2,1,0:T(8,128)(2,1)}), bf16[4,512,256]{2,1,0:T(8,128)(2,1)S(1)}, u32[]{:S(2)}, u32[]{:S(2)}) %all-to-all-start.5) | async-done | bytes 1048608 | tf_op jit(solution)/shard_map/all_to_all | solution.py:602
  278.7 19.2 %outer_product.4 = bf16[2,4,4,1312,128]{4,3,2,1,0:T(8,128)(2,1)} custom-call(bf16[4,1024,656]{2,1,0:T(8,128)(2,1)} %get-tuple-element.125.refs_0_.refs_1_, bf16[4,1024,656]{2,1,0:T(8,128)(2,1)} %get-tuple-element.124.refs_1_.refs_2_, bf16[1024,1024]{1,0:T(8,128)(2,1)} %get-tuple-element.108.normed.refs_2_), custom_call_target="tpu_custom_call" | custom-call | flops 11005853696 | bytes 23592960 | tf_op jit(solution)/shard_map/outer_product/pallas_call | solution.py:572
  302.8 26.6 %up_back.1 = (bf16[1024,1024]{1,0:T(8,128)(2,1)}, bf16[1024,1024]{1,0:T(8,128)(2,1)}, f32[8,1024]{1,0:T(8,128)}) custom-call(bf16[4,1024,256]{2,1,0:T(8,128)(2,1)} %copy-done.3, bf16[4,1024,656]{2,1,0:T(8,128)(2,1)} %get-tuple-element.125.refs_0_.refs_1_, bf16[4,1024,656]{2,1,0:T(8,128)(2,1)} %get-tuple-element.124.refs_1_.refs_2_, ...), custom_call_target="tpu_custom_call" | custom-call | flops 13153337344 | bytes 29884416 | tf_op jit(solution)/shard_map/up_back/pallas_call | solution.py:488
  329.5 26.8 %attend_back.1 = (bf16[1024,1024]{1,0:T(8,128)(2,1)}, bf16[1024,1024]{1,0:T(8,128)(2,1)}, bf16[1024,1024]{1,0:T(8,128)(2,1)}, f32[256,1024]{1,0:T(8,128)}, f32[256,1024]{1,0:T(8,128)}) custom-call(bf16[1152,1024]{1,0:T(8,128)(2,1)} %get-tuple-element.104.q.refs_0_, bf16[1024,1024]{1,0:T(8,128)(2,1)} %get-tuple-element.127.refs_1_, ...), custom_call_target="tpu_custom_call" | custom-call | flops 8589934592 | bytes 23068672 | tf_op jit(solution)/shard_map/attend_back/pallas_call | solution.py:308
  367.2 5.7 %all-to-all-start.7 = ((bf16[4,656,128]{2,1,0:T(8,128)(2,1)}), bf16[4,656,128]{2,1,0:T(8,128)(2,1)S(1)}, u32[]{:S(2)}, u32[]{:S(2)}) async-start(bf16[4,656,128]{2,1,0:T(8,128)(2,1)} %bitcast.122), calls=%async_computation.8 | async-start | bytes 1343488 | tf_op jit(solution)/shard_map/all_to_all | solution.py:602
  381.2 7.6 %all-to-all-done.7 = bf16[4,656,128]{2,1,0:T(8,128)(2,1)S(1)} async-done(((bf16[4,656,128]{2,1,0:T(8,128)(2,1)}), bf16[4,656,128]{2,1,0:T(8,128)(2,1)S(1)}, u32[]{:S(2)}, u32[]{:S(2)}) %all-to-all-start.7) | async-done | bytes 671776 | tf_op jit(solution)/shard_map/all_to_all | solution.py:602
  388.8 6.7 %reduce-scatter.6.cloned.1.call-done = bf16[1,4,1312,128]{3,2,1,0:T(8,128)(2,1)} async-done(((bf16[8,4,1312,128]{3,2,1,0:T(8,128)(2,1)}), bf16[1,4,1312,128]{3,2,1,0:T(8,128)(2,1)}) %reduce-scatter.6.cloned.1.call-update) | async-done | bytes 1343504 | tf_op jit(solution)/shard_map/reduce_scatter | solution.py:623
  395.5 19.8 %outer_product.5 = bf16[2,4,4,1024,128]{4,3,2,1,0:T(8,128)(2,1)} custom-call(bf16[1024,1024]{1,0:T(8,128)(2,1)} %get-tuple-element.138.refs_0_.gq, bf16[1024,1024]{1,0:T(8,128)(2,1)} %constant_dynamic-update-slice_fusion.refs_1_.gk, bf16[1024,1024]{1,0:T(8,128)(2,1)} %fusion.8.refs_2_.gv, bf16[1024,1024]{1,0:T(8,128)(2,1)} %get-tuple-element.107.attended.refs_3_, ...), custom_call_target="tpu_custom_call" | custom-call | flops 8589934592 | bytes 18874368 | tf_op jit(solution)/shard_map/outer_product/pallas_call | solution.py:572
  419.9 17.6 %unproject.1 = (bf16[4,1024,256]{2,1,0:T(8,128)(2,1)}, f32[8,1024]{1,0:T(8,128)}) custom-call(bf16[4,1152,256]{2,1,0:T(8,128)(2,1)} %copy-done.2, bf16[1024,1024]{1,0:T(8,128)(2,1)} %get-tuple-element.138.refs_0_.gq, bf16[1024,1024]{1,0:T(8,128)(2,1)} %constant_dynamic-update-slice_fusion.refs_1_.gk, bf16[1024,1024]{1,0:T(8,128)(2,1)} %fusion.8.refs_2_.gv, ...), custom_call_target="tpu_custom_call" | custom-call | flops 6442450944 | bytes 18874368 | tf_op jit(solution)/shard_map/unproject/pallas_call | solution.py:525
  437.5 14.5 %all-to-all-done.8 = bf16[4,1312,128]{2,1,0:T(8,128)(2,1)S(1)} async-done(((bf16[4,1312,128]{2,1,0:T(8,128)(2,1)}), bf16[4,1312,128]{2,1,0:T(8,128)(2,1)S(1)}, u32[]{:S(2)}, u32[]{:S(2)}) %all-to-all-start.8) | async-done | bytes 1343520 | tf_op jit(solution)/shard_map/all_to_all | solution.py:602
  467.8 22.5 %collective-permute-done.5 = f32[2,1024]{1,0:T(2,128)S(1)} collective-permute-done((f32[2,1024]{1,0:T(2,128)S(1)}, f32[2,1024]{1,0:T(2,128)S(1)}, u32[]{:S(2)}, u32[]{:S(2)}) %collective-permute-start.5) | collective-permute-done | bytes 8224 | tf_op jit(solution)/shard_map/ppermute | solution.py:642
  494.9 9.8 %collective-permute-done.6 = f32[2,1024]{1,0:T(2,128)S(1)} collective-permute-done((f32[2,1024]{1,0:T(2,128)S(1)}, f32[2,1024]{1,0:T(2,128)S(1)}, u32[]{:S(2)}, u32[]{:S(2)}) %collective-permute-start.6) | collective-permute-done | bytes 8224 | tf_op jit(solution)/shard_map/ppermute | solution.py:642
  519.6 5.2 collective-permute-done.8
  526.2 7.2 %all-to-all-done.10 = bf16[4,1024,128]{2,1,0:T(8,128)(2,1)S(1)} async-done(((bf16[4,1024,128]{2,1,0:T(8,128)(2,1)}), bf16[4,1024,128]{2,1,0:T(8,128)(2,1)S(1)}, u32[]{:S(2)}, u32[]{:S(2)}) %all-to-all-start.10) | async-done | bytes 1048608 | tf_op jit(solution)/shard_map/all_to_all | solution.py:602
  (201 shorter events, 119.8 us)
Async XLA Ops:
  7.2 149.6 %all-gather.7.cloned.1.call-start = ((), (), s32[]{:S(2)}) async-start(), calls=%async_computation.17 | async-start | bytes 9437184 | tf_op jit(solution)/shard_map/all_gather | solution.py:618
  49.2 157.1 %all-gather.9.cloned.1.call-start = ((), (), s32[]{:S(2)}) async-start(), calls=%async_computation.18 | async-start | bytes 12091392 | tf_op jit(solution)/shard_map/all_gather | solution.py:618
  90.3 56.4 %all-to-all-start.2 = ((bf16[4,1152,256]{2,1,0:T(8,128)(2,1)}), bf16[4,1152,256]{2,1,0:T(8,128)(2,1)S(1)}, u32[]{:S(2)}, u32[]{:S(2)}) async-start(bf16[4,1152,256]{2,1,0:T(8,128)(2,1)} %pad_maximum_fusion), calls=%async_computation.2 | async-start | bytes 4718592 | tf_op jit(solution)/shard_map/all_to_all | solution.py:602
  147.7 23.1 %all-to-all-start.3 = ((bf16[4,656,128]{2,1,0:T(8,128)(2,1)}), bf16[4,656,128]{2,1,0:T(8,128)(2,1)S(1)}, u32[]{:S(2)}, u32[]{:S(2)}) async-start(bf16[4,656,128]{2,1,0:T(8,128)(2,1)} %broadcast_in_dim.52), calls=%async_computation.3 | async-start | bytes 1343488 | tf_op jit(solution)/shard_map/all_to_all | solution.py:602
  151.2 73.9 %all-gather.11.cloned.1.call-start = ((), (), s32[]{:S(2)}) async-start(), calls=%async_computation.19 | async-start | bytes 6045696 | tf_op jit(solution)/shard_map/all_gather | solution.py:618
  171.7 67.6 %all-to-all-start.4 = ((bf16[4,1024,256]{2,1,0:T(8,128)(2,1)}), bf16[4,1024,256]{2,1,0:T(8,128)(2,1)S(1)}, u32[]{:S(2)}, u32[]{:S(2)}) async-start(bf16[4,1024,256]{2,1,0:T(8,128)(2,1)} %bitcast.115), calls=%async_computation.4 | async-start | bytes 4194304 | tf_op jit(solution)/shard_map/all_to_all | solution.py:602
  176.7 152.8 %reduce-scatter.4.cloned.1.call-start = ((), (), s32[]{:S(2)}) async-start(), calls=%async_computation.14 | async-start | bytes 6045696 | tf_op jit(solution)/shard_map/reduce_scatter | solution.py:623
  250.6 28.1 %all-to-all-start.5 = ((bf16[4,512,256]{2,1,0:T(8,128)(2,1)}), bf16[4,512,256]{2,1,0:T(8,128)(2,1)S(1)}, u32[]{:S(2)}, u32[]{:S(2)}) async-start(bf16[4,512,256]{2,1,0:T(8,128)(2,1)} %get-tuple-element.115), calls=%async_computation.5 | async-start | bytes 2097152 | tf_op jit(solution)/shard_map/all_to_all | solution.py:602
  255.6 139.9 %reduce-scatter.6.cloned.1.call-start = ((), (), s32[]{:S(2)}) async-start(), calls=%async_computation.15 | async-start | bytes 12091392 | tf_op jit(solution)/shard_map/reduce_scatter | solution.py:623
  298.0 31.5 %all-to-all-start.6 = ((bf16[4,512,256]{2,1,0:T(8,128)(2,1)}), bf16[4,512,256]{2,1,0:T(8,128)(2,1)S(1)}, u32[]{:S(2)}, u32[]{:S(2)}) async-start(bf16[4,512,256]{2,1,0:T(8,128)(2,1)} %get-tuple-element.117), calls=%async_computation.6 | async-start | bytes 2097152 | tf_op jit(solution)/shard_map/all_to_all | solution.py:602
  358.7 14.2 %collective-permute-start = (bf16[64,2048]{1,0:T(8,128)(2,1)}, bf16[64,2048]{1,0:T(8,128)(2,1)S(1)}, u32[]{:S(2)}, u32[]{:S(2)}) collective-permute-start(bf16[64,2048]{1,0:T(8,128)(2,1)} %pad_maximum_fusion.3), channel_id=1, source_target_pairs={{0,4},{4,8},{8,12},{1,5},{5,9},{9,13},{2,6},{6,10},{10,14},{3,7},{... | collective-permute-start | bytes 786440 | tf_op jit(solution)/shard_map/ppermute | solution.py:714
  363.7 9.3 %collective-permute-start.1 = (bf16[64,2048]{1,0:T(8,128)(2,1)}, bf16[64,2048]{1,0:T(8,128)(2,1)S(1)}, u32[]{:S(2)}, u32[]{:S(2)}) collective-permute-start(bf16[64,2048]{1,0:T(8,128)(2,1)} %pad_maximum_fusion.4), channel_id=1, source_target_pairs={{4,0},{8,4},{12,8},{5,1},{9,5},{13,9},{6,2},{10,6},{14,10},{7,3},{... | collective-permute-start | bytes 786440 | tf_op jit(solution)/shard_map/ppermute | solution.py:714
  367.2 21.6 %all-to-all-start.7 = ((bf16[4,656,128]{2,1,0:T(8,128)(2,1)}), bf16[4,656,128]{2,1,0:T(8,128)(2,1)S(1)}, u32[]{:S(2)}, u32[]{:S(2)}) async-start(bf16[4,656,128]{2,1,0:T(8,128)(2,1)} %bitcast.122), calls=%async_computation.8 | async-start | bytes 1343488 | tf_op jit(solution)/shard_map/all_to_all | solution.py:602
  372.9 131.8 %reduce-scatter.8.cloned.1.call-start = ((), (), s32[]{:S(2)}) async-start(), calls=%async_computation.16 | async-start | bytes 9437184 | tf_op jit(solution)/shard_map/reduce_scatter | solution.py:623
  415.3 36.7 %all-to-all-start.8 = ((bf16[4,1312,128]{2,1,0:T(8,128)(2,1)}), bf16[4,1312,128]{2,1,0:T(8,128)(2,1)S(1)}, u32[]{:S(2)}, u32[]{:S(2)}) async-start(bf16[4,1312,128]{2,1,0:T(8,128)(2,1)} %bitcast.36), calls=%async_computation.10 | async-start | bytes 2686976 | tf_op jit(solution)/shard_map/all_to_all | solution.py:602
  453.0 51.6 %all-to-all-start.9 = ((bf16[4,1024,256]{2,1,0:T(8,128)(2,1)}), bf16[4,1024,256]{2,1,0:T(8,128)(2,1)S(1)}, u32[]{:S(2)}, u32[]{:S(2)}) async-start(bf16[4,1024,256]{2,1,0:T(8,128)(2,1)} %get-tuple-element.141), calls=%async_computation.11 | async-start | bytes 4194304 | tf_op jit(solution)/shard_map/all_to_all | solution.py:602
  456.8 3.9 collective-permute-start.2
  460.7 3.9 collective-permute-start.3
  465.8 24.4 %collective-permute-start.5 = (f32[2,1024]{1,0:T(2,128)S(1)}, f32[2,1024]{1,0:T(2,128)S(1)}, u32[]{:S(2)}, u32[]{:S(2)}) collective-permute-start(f32[2,1024]{1,0:T(2,128)S(1)} %add.109), channel_id=1, source_target_pairs={{0,4},{4,0},{8,12},{12,8},{1,5},{5,1},{9,13},{13,9},{2,6},{6,2},{1... | collective-permute-start | bytes 24584 | tf_op jit(solution)/shard_map/ppermute | solution.py:642
  490.2 14.4 %collective-permute-start.6 = (f32[2,1024]{1,0:T(2,128)S(1)}, f32[2,1024]{1,0:T(2,128)S(1)}, u32[]{:S(2)}, u32[]{:S(2)}) collective-permute-start(f32[2,1024]{1,0:T(2,128)S(1)} %add.110), channel_id=1, source_target_pairs={{0,8},{4,12},{8,0},{12,4},{1,9},{5,13},{9,1},{13,5},{2,10},{6,14},... | collective-permute-start | bytes 24584 | tf_op jit(solution)/shard_map/ppermute | solution.py:642
  504.7 28.7 %all-to-all-start.10 = ((bf16[4,1024,128]{2,1,0:T(8,128)(2,1)}), bf16[4,1024,128]{2,1,0:T(8,128)(2,1)S(1)}, u32[]{:S(2)}, u32[]{:S(2)}) async-start(bf16[4,1024,128]{2,1,0:T(8,128)(2,1)} %bitcast.117), calls=%async_computation.13 | async-start | bytes 2097152 | tf_op jit(solution)/shard_map/all_to_all | solution.py:602
  510.1 6.8 %collective-permute-start.9 = (bf16[656,128]{1,0:T(8,128)(2,1)}, bf16[656,128]{1,0:T(8,128)(2,1)}, u32[]{:S(2)}, u32[]{:S(2)}) collective-permute-start(bf16[656,128]{1,0:T(8,128)(2,1)} %reduce_sum.78), channel_id=1, source_target_pairs={{0,16},{16,0},{1,17},{17,1},{2,18},{18,2},{3,19},{19,3},{4,20},{20... | collective-permute-start | bytes 503816 | tf_op jit(solution)/shard_map/ppermute | solution.py:590
  516.2 8.6 %collective-permute-start.8 = (bf16[1312,128]{1,0:T(8,128)(2,1)S(1)}, bf16[1312,128]{1,0:T(8,128)(2,1)S(1)}, u32[]{:S(2)}, u32[]{:S(2)}) collective-permute-start(bf16[1312,128]{1,0:T(8,128)(2,1)S(1)} %reduce_sum.77), channel_id=1, source_target_pairs={{0,16},{16,0},{1,17},{17,1},{2,18},{18,2},{3,19},{19,3},{4,20},{20... | collective-permute-start | bytes 1007624 | tf_op jit(solution)/shard_map/ppermute | solution.py:590
  533.7 7.3 %collective-permute-start.7 = (bf16[1024,128]{1,0:T(8,128)(2,1)S(1)}, bf16[1024,128]{1,0:T(8,128)(2,1)S(1)}, u32[]{:S(2)}, u32[]{:S(2)}) collective-permute-start(bf16[1024,128]{1,0:T(8,128)(2,1)S(1)} %reduce_sum.76), channel_id=1, source_target_pairs={{0,16},{16,0},{1,17},{17,1},{2,18},{18,2},{3,19},{19,3},{4,20},{20... | collective-permute-start | bytes 786440 | tf_op jit(solution)/shard_map/ppermute | solution.py:590
  (24 other events, 256.3 us)
Sparse Core Ops, SparseCore 0:
  49.3 53.4 all-gather.6
  104.8 64.3 all-gather.8
  171.8 43.1 all-gather.10
  250.7 58.5 reduce-scatter.3
  312.6 82.7 reduce-scatter.5
  415.4 71.4 reduce-scatter.7

commit v3 on v2

--- a/solution.py
+++ b/solution.py
@@ -85,22 +85,22 @@
     ]
 
 
-def joined_rows(halves, rows=slice(None)):
-    return jnp.concatenate([w[0, o, rows, :] for o in range(SLOTS) for w in halves], axis=1)
+def joined_rows(halves, p=0, rows=slice(None)):
+    return jnp.concatenate([w[p, o, rows, :] for o in range(SLOTS) for w in halves], axis=1)
 
 
 def at_first(run):
     pl.when(pl.program_id(0) == 0)(run)
 
 
-def add_up(total, part):
+def add_up(total, inner, weight, rows=slice(None)):
     @at_first
     def _():
-        total[...] = part
-
-    @pl.when((pl.program_id(0) > 0) & (pl.program_id(0) < GROUPS))
-    def _():
-        total[...] += part
+        total[...] = nn(inner[0], joined_rows(weight, 0, rows))
+
+    @pl.when(pl.program_id(0) > 0)
+    def _():
+        total[...] += nn(inner[0], joined_rows(weight, 0, rows))
 
 
 def struct(shape, dtype):
@@ -198,61 +198,75 @@
     return total
 
 
-def attend_kernel(q, k, v, seg_query, seg_key, attended, probability):
+def attend_kernel(*refs):
+    q, k, v, bias, xs, gain, low, high = refs[:8]
+    attended, probability, mixed, normed, held = refs[8:]
+
+    @at_first
+    def _():
+        for p in range(GROUPS):
+            held[pl.ds(p * GROUP, GROUP), :] = joined_rows((low, high), p)
+
     span = pl.ds(pl.multiple_of(pl.program_id(0) * QUERY, QUERY), QUERY + 2 * REACH)
     own = inner_rows(QUERY)
-    shape = (QUERY, QUERY + 2 * REACH)
-    offset = (
-        lax.broadcasted_iota(jnp.int32, shape, 1)
-        - lax.broadcasted_iota(jnp.int32, shape, 0)
-        - REACH
-    )
-    allowed = (jnp.abs(offset) <= REACH) & ((seg_query[...] == seg_key[0]) | (offset == 0))
     halves, wholes = head_masks()
+    masked = bias[0]
     for p in range(GROUPS):
         lanes = slice(p * GROUP, (p + 1) * GROUP)
-        stacked = spread(q[own, lanes], halves)
-        scores = nt(stacked, k[span, lanes]) * HEAD**-0.5
+        scores = nt(spread(q[own, lanes], halves), k[span, lanes]) * HEAD**-0.5
         scores = jnp.concatenate(
-            [
-                jnp.where(allowed, scores[h * QUERY : (h + 1) * QUERY], MASKED_SCORE)
-                for h in range(4)
-            ],
-            axis=0,
+            [scores[h * QUERY : (h + 1) * QUERY] + masked for h in range(4)], axis=0
         )
         exponent = jnp.exp(scores - jnp.max(scores, axis=1, keepdims=True))
         weight = (exponent * (1.0 / jnp.sum(exponent, axis=1, keepdims=True))).astype(BF16)
         probability[0, p] = weight
         attended[:, lanes] = collect(nn(weight, v[span, lanes]), wholes).astype(BF16)
-
-
-def attend(q, k, v, seg_query, seg_key):
-    tokens = seg_query.shape[0]
-    blocks = tokens // QUERY
-    span = QUERY + 2 * REACH
+    total = whole_rows(xs, own).astype(F32) + nn(attended[...], held[...])
+    mixed[...] = total.astype(BF16)
+    normed[...] = (norm(total)[0] * gain[...]).astype(BF16)
+
+
+def out_weight():
+    return [
+        pl.BlockSpec(
+            (GROUPS, SLOTS, GROUP, LANES), lambda i, a=a: (a, 0, 3, 0), pipeline_mode=pl.Buffered(1)
+        )
+        for a in range(2)
+    ]
+
+
+def attend(q, k, v, bias, xs, gain, heads):
+    blocks, _, span = bias.shape
+    tokens = blocks * QUERY
     return call(
         attend_kernel,
         (blocks,),
         [resident(q.shape)] * 3
-        + [rows_of(1, QUERY), pl.BlockSpec((1, 1, span), lambda i: (i, 0, 0))],
+        + [pl.BlockSpec((1, QUERY, span), lambda i: (i, 0, 0))]
+        + [resident(xs.shape), resident((1, WIDTH))]
+        + out_weight(),
         [
             rows_of(WIDTH, QUERY),
             pl.BlockSpec((1, GROUPS, 4 * QUERY, span), lambda i: (i, 0, 0, 0)),
+            rows_of(WIDTH, QUERY),
+            rows_of(WIDTH, QUERY),
         ],
         [
             struct((tokens, WIDTH), BF16),
             struct((blocks, GROUPS, 4 * QUERY, span), BF16),
+            struct((tokens, WIDTH), BF16),
+            struct((tokens, WIDTH), BF16),
         ],
-        [],
-        blocks * GROUPS * 2 * 2 * 4 * QUERY * span * GROUP,
-        8 * tokens * WIDTH + blocks * GROUPS * 8 * QUERY * span,
+        [pltpu.VMEM((WIDTH, WIDTH), BF16)],
+        blocks * GROUPS * 2 * 2 * 4 * QUERY * span * GROUP + 2 * tokens * WIDTH * WIDTH,
+        14 * tokens * WIDTH + blocks * GROUPS * 8 * QUERY * span,
         "attend",
-    )(q, k, v, seg_query, seg_key)
+    )(q, k, v, bias, xs, gain, heads, heads)
 
 
 def attend_back_kernel(*refs):
     q, grad, weights, k, v, cosine, sine = refs[:7]
-    gq, gk, gv, edge_k, edge_v, sum_k, sum_v = refs[7:]
+    gq, gk, gv, to_low, to_high, edges, sum_k, sum_v = refs[7:]
     step, steps = pl.program_id(0), pl.num_programs(0)
     tokens = gk.shape[0]
 
@@ -285,9 +299,12 @@
 
     @pl.when(step == steps - 1)
     def _():
-        for edge, total in ((edge_k, sum_k), (edge_v, sum_v)):
-            edge[0 : 2 * REACH, :] = total[0 : 2 * REACH, :]
-            edge[2 * REACH :, :] = total[pl.ds(tokens, 2 * REACH), :]
+        for t, total in ((0, sum_k), (1, sum_v)):
+            lanes = slice(t * WIDTH, (t + 1) * WIDTH)
+            to_low[:, lanes] = total[0:REACH, :].astype(BF16)
+            edges[0, :, lanes] = total[REACH : 2 * REACH, :]
+            edges[1, :, lanes] = total[pl.ds(tokens, REACH), :]
+            to_high[:, lanes] = total[pl.ds(tokens + REACH, REACH), :].astype(BF16)
         for at in range(0, tokens, QUERY):
             own = pl.ds(REACH + at, QUERY)
             c, s = cosine[own, :], sine[own, :]
@@ -304,7 +321,7 @@
     blocks = tokens // QUERY
     span = QUERY + 2 * REACH
     full = resident((tokens, WIDTH))
-    edge = resident((4 * REACH, WIDTH))
+    edge = (REACH, 2 * WIDTH)
     return call(
         attend_back_kernel,
         (blocks,),
@@ -317,8 +334,8 @@
             resident(cosine.shape),
             resident(cosine.shape),
         ],
-        [rows_of(WIDTH, QUERY), full, full, edge, edge],
-        [struct((tokens, WIDTH), BF16)] * 3 + [struct((4 * REACH, WIDTH), F32)] * 2,
+        [rows_of(WIDTH, QUERY), full, full, resident(edge), resident(edge), resident((2,) + edge)],
+        [struct((tokens, WIDTH), BF16)] * 3 + [struct(edge, BF16)] * 2 + [struct((2,) + edge, F32)],
         [pltpu.VMEM(q.shape, F32)] * 2,
         blocks * GROUPS * 2 * 4 * 4 * QUERY * span * GROUP,
         14 * tokens * WIDTH + blocks * GROUPS * 8 * QUERY * span,
@@ -326,17 +343,45 @@
     )(q, grad, weights, k, v, cosine, sine)
 
 
-def mix_kernel(xs, attended, gain, low, high, mixed, normed, total):
-    @pl.when(pl.program_id(0) < GROUPS)
-    def _():
-        add_up(total, nn(attended[...], joined_rows((low, high))))
-
-    @pl.when(pl.program_id(0) >= GROUPS)
-    def _():
-        rows = step_rows()
-        made = whole_rows(xs, between_rows()).astype(F32) + total[rows, :]
-        mixed[...] = made.astype(mixed.dtype)
-        normed[...] = (norm(made)[0] * gain[...]).astype(BF16)
+def edge_kernel(*refs):
+    edges, from_low, from_high, cosine, sine = refs[2:7]
+    gk, gv = refs[7:]
+
+    def finish(came):
+        c, s = cosine[...], sine[...]
+        for p in range(GROUPS):
+            one = slice(p * GROUP, p * GROUP + LANES)
+            two = slice(p * GROUP + LANES, (p + 1) * GROUP)
+            first = edges[0, :, one] + came[:, one].astype(F32)
+            second = edges[0, :, two] + came[:, two].astype(F32)
+            gk[:, one] = (first * c + second * s).astype(BF16)
+            gk[:, two] = (second * c - first * s).astype(BF16)
+        gv[...] = (edges[0, :, WIDTH:] + came[:, WIDTH:].astype(F32)).astype(BF16)
+
+    pl.when(pl.program_id(0) == 0)(lambda: finish(from_low))
+    pl.when(pl.program_id(0) == 1)(lambda: finish(from_high))
+
+
+def add_edges(gk, gv, edges, from_low, from_high, cosine, sine):
+    tokens = gk.shape[0]
+    far = tokens // REACH - 1
+    rows = pl.BlockSpec((REACH, WIDTH), lambda i: (i * far, 0))
+    table = pl.BlockSpec((REACH, LANES), lambda i: (1 + i * far, 0))
+    came = resident(from_low.shape)
+    return pl.pallas_call(
+        edge_kernel,
+        grid=(2,),
+        in_specs=[pl.BlockSpec(memory_space=pl.ANY)] * 2
+        + [pl.BlockSpec((1, REACH, 2 * WIDTH), lambda i: (i, 0, 0)), came, came, table, table],
+        out_specs=[rows] * 2,
+        out_shape=[struct(gk.shape, BF16)] * 2,
+        input_output_aliases={0: 0, 1: 1},
+        compiler_params=pltpu.CompilerParams(
+            vmem_limit_bytes=VMEM, dimension_semantics=("arbitrary",)
+        ),
+        cost_estimate=pl.CostEstimate(flops=1, bytes_accessed=2**21, transcendentals=0),
+        name="add_edges",
+    )(gk, gv, edges, from_low, from_high, cosine, sine)
 
 
 def step_rows():
@@ -348,168 +393,119 @@
     return pl.ds(pl.multiple_of(at, REACH), TILE)
 
 
-def mix(xs, attended, gain, weight):
-    tokens = attended.shape[0]
-    return call(
-        mix_kernel,
-        (GROUPS + tokens // TILE,),
-        [
-            resident(xs.shape),
-            pl.BlockSpec((tokens, GROUP), lambda i: (0, group_of(i))),
-            resident((1, WIDTH)),
-        ]
-        + weight_rows(GROUP, 3),
-        [later_rows(WIDTH)] * 2,
-        [struct((tokens, WIDTH), BF16)] * 2,
-        [pltpu.VMEM((tokens, WIDTH), F32)],
-        2 * tokens * WIDTH * WIDTH,
-        8 * tokens * WIDTH + 2 * WIDTH * WIDTH,
-        "mix",
-    )(xs, attended, gain, weight, weight)
-
-
-def up_kernel(normed, low, high, hidden, slope, gelu):
+def feed_kernel(*refs):
+    normed, mixed, weight = refs[0], refs[1], refs[2:4]
+    hidden, slope, gelu, early, late, total = refs[4:]
     ff = hidden.shape[2]
-    act = nt(normed[...], joined_rows((low, high), slice(0, ff)))
-    gate = nt(normed[...], joined_rows((low, high), slice(ff, 2 * ff)))
-    spread_to = 0.5 * (1.0 + lax.erf(act * math.sqrt(0.5)))
-    curve = act * spread_to
-    density = jnp.exp(act * act * -0.5) * (1.0 / math.sqrt(2.0 * math.pi))
-    slope[0] = (gate * (spread_to + act * density)).astype(BF16)
-    gelu[0] = curve.astype(BF16)
-    hidden[0] = (curve * gate).astype(BF16)
+    half = GROUPS + total.shape[0] // TILE // 2
+    step = pl.program_id(0)
+
+    @pl.when(step < GROUPS)
+    def _():
+        act = nt(normed[...], joined_rows(weight, 0, slice(0, ff)))
+        gate = nt(normed[...], joined_rows(weight, 0, slice(ff, 2 * ff)))
+        spread_to = 0.5 * (1.0 + lax.erf(act * math.sqrt(0.5)))
+        curve = act * spread_to
+        density = jnp.exp(act * act * -0.5) * (1.0 / math.sqrt(2.0 * math.pi))
+        slope[0] = (gate * (spread_to + act * density)).astype(BF16)
+        gelu[0] = curve.astype(BF16)
+        hidden[0] = (curve * gate).astype(BF16)
+        add_up(total, hidden, weight, slice(2 * ff, 3 * ff))
+
+    @pl.when((step >= GROUPS) & (step < half))
+    def _():
+        put_rows(early, mixed[...].astype(F32) + total[step_rows(), :])
+
+    @pl.when(step >= half)
+    def _():
+        put_rows(late, mixed[...].astype(F32) + total[step_rows(), :])
 
 
 def units_of(tokens, ff):
     return pl.BlockSpec((1, tokens, ff), lambda i: (group_of(i), 0, 0))
 
 
-def feed_up(normed, weight):
-    tokens, ff = normed.shape[0], weight.shape[2] // 2
-    return call(
-        up_kernel,
-        (GROUPS,),
-        [resident((tokens, WIDTH))] + weight_rows(2 * ff),
-        [units_of(tokens, ff)] * 3,
-        [struct((GROUPS, tokens, ff), BF16)] * 3,
-        [],
-        2 * tokens * WIDTH * 2 * GROUPS * ff,
-        2 * tokens * WIDTH + 2 * GROUPS * ff * (3 * tokens + 2 * WIDTH),
-        "feed_up",
-    )(normed, weight, weight)
-
-
-def down_kernel(hidden, mixed, low, high, early, late, total):
-    @pl.when(pl.program_id(0) < GROUPS)
-    def _():
-        add_up(total, nn(hidden[0], joined_rows((low, high))))
-
-    half = GROUPS + total.shape[0] // TILE // 2
-
-    @pl.when((pl.program_id(0) >= GROUPS) & (pl.program_id(0) < half))
-    def _():
-        put_rows(early, mixed[...].astype(F32) + total[step_rows(), :])
-
-    @pl.when(pl.program_id(0) >= half)
-    def _():
-        put_rows(late, mixed[...].astype(F32) + total[step_rows(), :])
-
-
-def feed_down(hidden, mixed, weight):
-    _, tokens, ff = hidden.shape
+def feed(normed, mixed, weight):
+    tokens, ff = normed.shape[0], weight.shape[2] // 3
     steps = tokens // TILE // 2
     return call(
-        down_kernel,
+        feed_kernel,
         (GROUPS + tokens // TILE,),
-        [units_of(tokens, ff), later_rows(WIDTH)] + weight_rows(ff),
-        [
+        [resident((tokens, WIDTH)), later_rows(WIDTH)] + weight_rows(3 * ff),
+        [units_of(tokens, ff)] * 3
+        + [
             pl.BlockSpec(
                 (SLOTS, TILE, 256),
                 lambda i, first=first: (0, jnp.clip(i - GROUPS - first, 0, steps - 1), 0),
             )
             for first in (0, steps)
         ],
-        [struct((SLOTS, tokens // 2, 256), BF16)] * 2,
+        [struct((GROUPS, tokens, ff), BF16)] * 3
+        + [struct((SLOTS, tokens // 2, 256), BF16)] * 2,
         [pltpu.VMEM((tokens, WIDTH), F32)],
-        2 * tokens * WIDTH * GROUPS * ff,
-        4 * tokens * WIDTH + 2 * GROUPS * ff * (tokens + WIDTH),
-        "feed_down",
-    )(hidden, mixed, weight, weight)
-
-
-def down_back_kernel(cots, slope, gelu, low, high, g_act, g_gate):
-    g_hidden = nt(whole_rows(cots), joined_rows((low, high)))
-    g_act[0] = (g_hidden * slope[0].astype(F32)).astype(BF16)
-    g_gate[0] = (g_hidden * gelu[0].astype(F32)).astype(BF16)
-
-
-def down_back(cots, slope, gelu, weight):
-    _, tokens, ff = slope.shape
-    return call(
-        down_back_kernel,
-        (GROUPS,),
-        [resident(cots.shape)] + [units_of(tokens, ff)] * 2 + weight_rows(ff),
-        [units_of(tokens, ff)] * 2,
-        [struct((GROUPS, tokens, ff), BF16)] * 2,
-        [],
-        2 * tokens * WIDTH * GROUPS * ff,
-        2 * tokens * WIDTH + 2 * GROUPS * ff * (4 * tokens + WIDTH),
-        "down_back",
-    )(cots, slope, gelu, weight, weight)
-
-
-def up_back_kernel(*refs):
-    cots, g_act, g_gate, mixed, gain, low, high, out_low, out_high = refs[:9]
-    g_branch, g_attended, gain_part, total = refs[9:]
+        2 * tokens * WIDTH * 3 * GROUPS * ff,
+        6 * tokens * WIDTH + 6 * GROUPS * ff * (tokens + WIDTH),
+        "feed",
+    )(normed, mixed, weight, weight)
+
+
+def feed_back_kernel(*refs):
+    cots, slope, gelu, mixed, gain = refs[:5]
+    weight, outward = refs[5:7], refs[7:9]
+    g_act, g_gate, g_branch, g_attended, gain_part, cot, total = refs[9:]
     ff = g_act.shape[2]
 
+    @at_first
+    def _():
+        cot[...] = whole_rows(cots)
+
     @pl.when(pl.program_id(0) < GROUPS)
     def _():
-        part = nn(g_act[0], joined_rows((low, high), slice(0, ff)))
-        add_up(total, part + nn(g_gate[0], joined_rows((low, high), slice(ff, 2 * ff))))
+        g_hidden = nt(cot[...], joined_rows(weight, 0, slice(2 * ff, 3 * ff)))
+        g_act[0] = (g_hidden * slope[0].astype(F32)).astype(BF16)
+        g_gate[0] = (g_hidden * gelu[0].astype(F32)).astype(BF16)
+        add_up(total, g_act, weight, slice(0, ff))
+        total[...] += nn(g_gate[0], joined_rows(weight, 0, slice(ff, 2 * ff)))
 
     @pl.when(pl.program_id(0) >= GROUPS)
     def _():
         gradient = total[step_rows(), :]
         unit, inverse = norm(mixed[...].astype(F32))
         add_gain(gain_part, gradient * unit)
-        made = whole_rows(cots).astype(F32) + norm_back(gradient, unit, inverse, gain[...])
+        made = cot[step_rows(), :].astype(F32) + norm_back(gradient, unit, inverse, gain[...])
         branch = made.astype(BF16)
         g_branch[...] = branch
         for p in range(GROUPS):
-            parts = [ref[p, o] for o in range(SLOTS) for ref in (out_low, out_high)]
-            held = jnp.concatenate(parts, axis=1)
-            g_attended[:, p * GROUP : (p + 1) * GROUP] = nt(branch, held).astype(BF16)
-
-
-def up_back(cots, g_act, g_gate, mixed, gain, up, heads):
-    _, tokens, ff = g_act.shape
-    out_shape = (GROUPS, SLOTS, GROUP, LANES)
+            lanes = slice(p * GROUP, (p + 1) * GROUP)
+            g_attended[:, lanes] = nt(branch, joined_rows(outward, p)).astype(BF16)
+
+
+def feed_back(cots, slope, gelu, mixed, gain, weight, heads):
+    _, tokens, ff = slope.shape
     return call(
-        up_back_kernel,
+        feed_back_kernel,
         (GROUPS + tokens // TILE,),
-        [LATER_BLOCKS]
+        [resident(cots.shape)]
         + [units_of(tokens, ff)] * 2
         + [later_rows(WIDTH), resident((1, WIDTH))]
-        + weight_rows(2 * ff)
-        + [
-            pl.BlockSpec(out_shape, lambda i, a=a: (a, 0, 3, 0), pipeline_mode=pl.Buffered(1))
-            for a in range(2)
-        ],
-        [later_rows(WIDTH)] * 2 + [resident((8, WIDTH))],
-        [struct((tokens, WIDTH), BF16)] * 2 + [struct((8, WIDTH), F32)],
-        [pltpu.VMEM((tokens, WIDTH), F32)],
-        2 * tokens * WIDTH * (2 * GROUPS * ff + WIDTH),
-        8 * tokens * WIDTH + 4 * GROUPS * ff * (tokens + WIDTH),
-        "up_back",
-    )(cots, g_act, g_gate, mixed, gain, up, up, heads, heads)
-
-
-def unproject_kernel(xs, gq, gk, gv, g_branch, gain, low, high, outs, gain_part, total):
+        + weight_rows(3 * ff)
+        + out_weight(),
+        [units_of(tokens, ff)] * 2 + [later_rows(WIDTH)] * 2 + [resident((8, WIDTH))],
+        [struct((GROUPS, tokens, ff), BF16)] * 2
+        + [struct((tokens, WIDTH), BF16)] * 2
+        + [struct((8, WIDTH), F32)],
+        [pltpu.VMEM((tokens, WIDTH), BF16), pltpu.VMEM((tokens, WIDTH), F32)],
+        2 * tokens * WIDTH * (3 * GROUPS * ff + WIDTH),
+        8 * tokens * WIDTH + 6 * GROUPS * ff * (tokens + WIDTH),
+        "feed_back",
+    )(cots, slope, gelu, mixed, gain, weight, weight, heads, heads)
+
+
+def unproject_kernel(xs, gq, gk, gv, g_branch, gain, low, high, outs, gain_part, held, total):
     @pl.when(pl.program_id(0) < GROUPS)
     def _():
-        inner = jnp.concatenate([gq[...], gk[...], gv[...]], axis=1)
-        add_up(total, nn(inner, joined_rows((low, high))))
+        held[0] = jnp.concatenate([gq[...], gk[...], gv[...]], axis=1)
+        add_up(total, held, (low, high))
 
     @pl.when(pl.program_id(0) >= GROUPS)
     def _():
@@ -531,15 +527,15 @@
         + weight_rows(3 * GROUP),
         [LATER_BLOCKS, resident((8, WIDTH))],
         [struct((SLOTS, tokens, 256), BF16), struct((8, WIDTH), F32)],
-        [pltpu.VMEM((tokens, WIDTH), F32)],
+        [pltpu.VMEM((1, tokens, 3 * GROUP), BF16), pltpu.VMEM((tokens, WIDTH), F32)],
         2 * tokens * WIDTH * 3 * WIDTH,
         12 * tokens * WIDTH + 6 * WIDTH * WIDTH,
         "unproject",
     )(xs, gq, gk, gv, g_branch, gain, weight, weight)
 
 
-def outer_kernel(pairs, count, *refs):
-    inner, outer, out = refs[: len(pairs)], refs[len(pairs) : -1], refs[-1]
+def outer_kernel(count, *refs):
+    inner, outer, out = refs[:count], refs[count : 2 * count], refs[-1]
     tokens = inner[0].shape[-2]
 
     def make(left, right):
@@ -554,36 +550,45 @@
                 at = o * 256 + a * LANES
                 out[a, 0, o] = made[:, at : at + LANES].astype(BF16)
 
-    for t, j in enumerate(pairs):
-        pl.when(pl.program_id(0) % count == t)(functools.partial(make, inner[t], outer[j]))
-
-
-def outer_product(pairs, inner, outer):
+    for t in range(count):
+        pl.when(pl.program_id(0) % count == t)(functools.partial(make, inner[t], outer[t]))
+
+
+def outer_product(inner, outer, places, kinds, base=None):
     count = len(inner)
     tokens = inner[0].shape[-2]
     width = inner[0].shape[2] if inner[0].ndim == 3 else GROUP
-    rows = count * width
+    stride = places[-1] - places[0]
 
     def inner_block(value):
         if value.ndim == 3:
             return pl.BlockSpec((1, tokens, width), lambda i: (i // count, 0, 0))
         return pl.BlockSpec((tokens, GROUP), lambda i: (0, i // count))
 
-    return call(
-        functools.partial(outer_kernel, pairs, count),
-        (GROUPS * count,),
-        [inner_block(value) for value in inner] + [resident(value.shape) for value in outer],
-        [
-            pl.BlockSpec(
-                (2, 1, SLOTS, width, LANES), lambda i: (0, i // count, 0, i % count, 0)
-            )
-        ],
-        [struct((2, GROUPS, SLOTS, rows, LANES), BF16)],
-        [],
-        2 * tokens * GROUPS * rows * WIDTH,
-        8 * rows * (tokens + WIDTH) + 2 * tokens * WIDTH,
-        "outer_product",
-    )(*inner, *outer)[0]
+    more = [] if base is None else [base]
+    moved = 8 * count * width * (tokens + WIDTH) + 2 * tokens * WIDTH
+    return pl.pallas_call(
+        functools.partial(outer_kernel, count),
+        grid=(GROUPS * count,),
+        in_specs=[inner_block(value) for value in inner]
+        + [resident(value.shape) for value in outer]
+        + [pl.BlockSpec(memory_space=pl.ANY) for _ in more],
+        out_specs=pl.BlockSpec(
+            (2, 1, SLOTS, width, LANES),
+            lambda i: (0, i // count, 0, places[0] + i % count * stride, 0),
+        ),
+        out_shape=struct((2, GROUPS, SLOTS, kinds * width, LANES), BF16),
+        input_output_aliases={2 * count: 0} if more else {},
+        compiler_params=pltpu.CompilerParams(
+            vmem_limit_bytes=VMEM, dimension_semantics=("arbitrary",)
+        ),
+        cost_estimate=pl.CostEstimate(
+            flops=2 * tokens * GROUPS * count * width * WIDTH,
+            bytes_accessed=moved,
+            transcendentals=0,
+        ),
+        name="outer_product",
+    )(*inner, *outer, *more)
 
 
 def over_dp(value):
@@ -627,11 +632,30 @@
     half = jnp.sum(parts.astype(F32), axis=0).astype(BF16)
     other = over_dp(half)
     first = lax.axis_index("dp") == 0
-    return jnp.where(
-        first,
-        jnp.concatenate([half, other], axis=1),
-        jnp.concatenate([other, half], axis=1),
-    ).astype(F32)
+    return jnp.where(first, half, other), jnp.where(first, other, half)
+
+
+def finish_kernel(kinds, width, low, high, *outs):
+    for t, (kind, out) in enumerate(zip(kinds, outs, strict=True)):
+        rows = slice(t * width, (t + 1) * width)
+        value = jnp.concatenate([low[rows, :], high[rows, :]], axis=1).astype(F32)
+        if kind not in "qkv":
+            out[...] = value
+            continue
+        if kind in "qk":
+            cuts = [value[at * 32 : (at + 1) * 32] for at in (0, 4, 1, 5, 2, 6, 3, 7)]
+            value = jnp.concatenate(cuts, axis=0)
+        out[...] = value.T
+
+
+def finish(halves, kinds, width):
+    return pl.pallas_call(
+        functools.partial(finish_kernel, kinds, width),
+        out_shape=[struct((256, width) if kind in "qkv" else (width, 256), F32) for kind in kinds],
+        compiler_params=pltpu.CompilerParams(vmem_limit_bytes=VMEM),
+        cost_estimate=pl.CostEstimate(flops=1, bytes_accessed=2**21, transcendentals=0),
+        name="finish",
+    )(*halves)
 
 
 def sum_gains(parts):
@@ -671,14 +695,21 @@
     before = jnp.sum((segments[None, :] < ids[:, None]).astype(jnp.int32), axis=1)
     begin = jnp.sum(jnp.where(near[:, None] == ids[None, :], before[None, :], 0), axis=1)
     where_in = (index - begin).astype(F32)
-    frequency = ROPE_THETA ** (-(jnp.arange(32, dtype=F32) * 2.0) / HEAD)
+    frequency = ROPE_THETA ** (-((jnp.arange(LANES) % 32).astype(F32) * 2.0) / HEAD)
     angles = where_in[:, None] * frequency[None, :]
-    cosine, sine = jnp.tile(jnp.cos(angles), (1, 4)), jnp.tile(jnp.sin(angles), (1, 4))
     code = jnp.pad(jnp.where(valid == 1, segments, -1), pads, constant_values=-1)
     code = lax.dynamic_slice_in_dim(code, first, tokens + 2 * REACH, 0)
     span = QUERY + 2 * REACH
     keys = jnp.stack([code[i : i + span] for i in range(0, tokens, QUERY)])[:, None, :]
-    return cosine, sine, near[REACH:-REACH, None], keys
+    queries = near[REACH:-REACH].reshape(-1, QUERY, 1)
+    shape = (tokens // QUERY, QUERY, span)
+    offset = (
+        lax.broadcasted_iota(jnp.int32, shape, 2)
+        - lax.broadcasted_iota(jnp.int32, shape, 1)
+        - REACH
+    )
+    allowed = (jnp.abs(offset) <= REACH) & ((queries == keys) | (offset == 0))
+    return jnp.cos(angles), jnp.sin(angles), jnp.where(allowed, 0.0, MASKED_SCORE).astype(F32)
 
 
 def body(
@@ -727,20 +758,22 @@
             ],
             axis=0,
         )
-        up_half = jnp.concatenate([own_half(w_act.T), own_half(w_gate.T)], axis=0)
+        feed_half = jnp.concatenate(
+            [own_half(w_act.T), own_half(w_gate.T), own_half(w_down)], axis=0
+        )
         padded = jnp.pad(tokens_in, ((REACH, REACH), (0, 0)))
         spans = [padded[j * tokens : (j + 1) * tokens + 2 * REACH] for j in range(rows)]
         heads_own = gather_rows(heads_half)
         heads_w = gather_groups(heads_own[:, :WIDTH])
-        up_own = gather_rows(after(up_half, heads_own))
-        up_w = gather_groups(up_own)
+        feed_own = gather_rows(after(feed_half, heads_own))
+        feed_w = gather_groups(feed_own)
         last = WIDTH + marks.shape[0]
         marks = heads_own[:, WIDTH:last].reshape(rows, 2, length)
         marks = lax.dynamic_index_in_dim(marks, sequence, 0, False).astype(jnp.int32)
         gain_slots = heads_own[:, last : last + 4].reshape(SLOTS, 2, 256)
         tables = positions_and_masks(*marks, first, tokens)
-        xs = exchange(after(jnp.stack(spans), up_own, *tables))
-        down_own = gather_rows(after(own_half(w_down), xs))
+        xs = exchange(after(jnp.stack(spans), feed_own))
+        cots = exchange(after(cotangent.reshape(rows, tokens, 256), xs))
     else:
         xs = exchange(tokens_in.reshape(rows, tokens, 256))
         below, above = shift(xs[:, -REACH:], upward), shift(xs[:, :REACH], downward)
@@ -766,83 +799,55 @@
             full(w_value, False),
             full(w_out, True),
         )
-        up_w = joined(full(w_act, False), full(w_gate, False))
-        down_w = joined(full(w_down, True))
+        feed_w = joined(full(w_act, False), full(w_gate, False), full(w_down, True))
     gain_rows = gain_slots.swapaxes(0, 1).reshape(2, 1, WIDTH).astype(F32)
-    cosine, sine, seg_query, seg_key = tables
+    cosine, sine, bias = tables
 
     q, k, v, normed_attn = project(xs, gain_rows[0], cosine, sine, heads_w)
-    if own_slice:
-        down_own = after(down_own, q)
-        down_w = gather_groups(down_own)
-        cots = exchange(after(cotangent.reshape(rows, tokens, 256), down_own))
-    attended, weights = attend(q, k, v, seg_query, seg_key)
-    mixed, normed_ffn = mix(xs, attended, gain_rows[1], heads_w)
-    hidden, slope, gelu = feed_up(normed_ffn, up_w)
-    early, late = feed_down(hidden, mixed, down_w)
-    hidden = after(hidden, early)
+    attended, weights, mixed, normed_ffn = attend(q, k, v, bias, xs, gain_rows[1], heads_w)
+    hidden, slope, gelu, early, late = feed(normed_ffn, mixed, feed_w)
     early = exchange(after(early, cots))
-    late = exchange(after(late, early))
-    layer_out = jnp.concatenate([early, late], axis=1)
-    down_parts = outer_product((0,), [hidden], [cots])
-    g_act, g_gate = down_back(cots, after(slope, down_parts), gelu, down_w)
-    up_parts = outer_product((0, 0), [after(g_act, early), g_gate], [normed_ffn])
-    g_branch, g_attended, gain_part_ffn = up_back(
-        cots, after(g_act, up_parts), g_gate, mixed, gain_rows[1], up_w, heads_w
+    down_parts = outer_product([hidden], [cots], (0,), 1)
+    g_act, g_gate, g_branch, g_attended, gain_part_ffn = feed_back(
+        cots, after(slope, down_parts), gelu, mixed, gain_rows[1], feed_w, heads_w
     )
+    up_parts = outer_product([after(g_act, early), g_gate], [normed_ffn] * 2, (0, 1), 2)
     if own_slice:
         down_own, up_own = reduce_groups(down_parts), reduce_groups(up_parts)
-        down_sum = exchange(after(down_own, late))
-        g_attended = after(g_attended, late, down_own)
-    gq, gk, gv, edge_k, edge_v = attend_back(q, g_attended, weights, k, v, cosine, sine)
-    to_low = jnp.concatenate([edge_k[:REACH], edge_v[:REACH]], axis=1).astype(BF16)
-    to_high = jnp.concatenate([edge_k[-REACH:], edge_v[-REACH:]], axis=1).astype(BF16)
-    from_high = shift(to_low, downward).astype(F32)
-    from_low = shift(to_high, upward).astype(F32)
-
-    def turned(value, c, s):
-        cut = value.reshape(-1, GROUPS, 2, LANES)
-        first, second = cut[:, :, 0], cut[:, :, 1]
-        c, s = c[:, None], s[:, None]
-        back = jnp.stack([first * c + second * s, second * c - first * s], axis=2)
-        return back.reshape(value.shape).astype(BF16)
-
-    near_k = edge_k[REACH : 2 * REACH] + from_low[:, :WIDTH]
-    near_v = edge_v[REACH : 2 * REACH] + from_low[:, WIDTH:]
-    last_k = edge_k[2 * REACH : 3 * REACH] + from_high[:, :WIDTH]
-    last_v = edge_v[2 * REACH : 3 * REACH] + from_high[:, WIDTH:]
-    gk = gk.at[:REACH].set(turned(near_k, cosine[REACH : 2 * REACH], sine[REACH : 2 * REACH]))
-    gk = gk.at[-REACH:].set(
-        turned(last_k, cosine[-2 * REACH : -REACH], sine[-2 * REACH : -REACH])
+        g_attended = after(g_attended, up_parts, down_own)
+    gq, gk, gv, to_low, to_high, edges = attend_back(
+        q, g_attended, weights, k, v, cosine, sine
     )
-    gv = gv.at[:REACH].set(near_v.astype(BF16))
-    gv = gv.at[-REACH:].set(last_v.astype(BF16))
-
+    from_low, from_high = shift(to_high, upward), shift(to_low, downward)
     if own_slice:
-        gq = after(gq, down_sum, up_own)
-    heads_parts = outer_product(
-        (0, 0, 0, 1), [gq, gk, gv, attended], [normed_attn, g_branch]
-    )
+        rest = down_own.reshape(rows, -1, 256)
+        late, rest = jnp.split(
+            exchange(jnp.concatenate([after(late, early), rest], axis=1)), [tokens // 2], axis=1
+        )
+        down_sum = rest.reshape(down_own.shape)
+        gq = after(gq, late, down_sum)
+    else:
+        late = exchange(late)
+    layer_out = jnp.concatenate([early, late], axis=1)
+    heads_parts = outer_product([gq, attended], [normed_attn, g_branch], (0, 3), 4)
+    from_low = after(from_low, heads_parts)
+    gk, gv = add_edges(gk, gv, edges, from_low, from_high, cosine, sine)
+    heads_parts = outer_product([gk, gv], [normed_attn] * 2, (1, 2), 4, heads_parts)
     grad_slots, gain_part_attn = unproject(
         xs, after(gq, heads_parts), gk, gv, g_branch, gain_rows[0], heads_w
     )
 
     gain_parts = jnp.stack([jnp.sum(gain_part_attn, axis=0), jnp.sum(gain_part_ffn, axis=0)])
     if own_slice:
-        up_sum = exchange(after(up_own, down_sum))
-        token_gradient = exchange(after(grad_slots, up_sum))
+        token_gradient = exchange(after(grad_slots, down_sum))
+        up_sum = exchange(after(up_own, token_gradient))
         gain_grads = sum_gains(gain_parts)
-        heads_sum = exchange(after(reduce_groups(heads_parts), token_gradient, gain_grads))
-        down_sum, up_sum, heads_sum = (sum_rows(v) for v in (down_sum, up_sum, heads_sum))
+        heads_sum = exchange(after(reduce_groups(heads_parts), up_sum, gain_grads))
         ff = w_act.shape[1]
         grads = (
-            join_heads(heads_sum[:GROUP]).T,
-            join_heads(heads_sum[GROUP : 2 * GROUP]).T,
-            heads_sum[2 * GROUP : 3 * GROUP].T,
-            heads_sum[3 * GROUP :],
-            up_sum[:ff].T,
-            up_sum[ff:].T,
-            down_sum,
+            *finish(sum_rows(heads_sum), "qkvo", GROUP),
+            *(value.T for value in finish(sum_rows(up_sum), "ag", ff)),
+            *finish(sum_rows(down_sum), "d", ff),
         )
     else:
 

time: 561 us -> 532 us (0.948)
  blocking collectives: 68.4 us -> 134 us
  waiting for transfers between devices: 142 us -> 89 us
  local copies, waits for them, and re-layouts: 32.6 us -> 11.9 us
  starting transfers between devices: 57.5 us -> 46 us
    all_to_all x2 -> x3, blocking collectives: 68.4 us -> 134 us  [exchange(): return lax.all_to_all(value, 'row', 0, 0)]
    all_to_all x9 -> x6, waiting for transfers between devices: 88 us -> 65.7 us  [exchange(): return lax.all_to_all(value, 'row', 0, 0)]
    ppermute x2, waiting for transfers between devices: 32.2 us -> 14.3 us  [sum_gains(): lax.ppermute(both, 'row', [(i, i ^ bit) for i in range(SLOTS)])]
    all_to_all x9 -> x6, starting transfers between devices: 38.2 us -> 26.8 us  [exchange(): return lax.all_to_all(value, 'row', 0, 0)]
    reduce_scatter x3, waiting for transfers between devices: 6.77 us -> 0.03 us  [reduce_groups(): lax.psum_scatter(parts, ('dp', 'col'), scatter_dimension=0, tiled=False)]
    ppermute x4, waiting for transfers between devices: 11.1 us -> 5.34 us  [over_dp(): return lax.ppermute(value, 'dp', [(0, 1), (1, 0)])]
    pallas_call x9 -> x11, Pallas kernels: 153 us -> 153 us  [the longest x4 54.6 us: outer_product(): pl.pallas_call(functools.partial(outer_kernel, count), grid=(GROUPS * cou...]
  transfers between devices with their start and end apart: 25 -> 21, of which waited for: 13 -> 9; matrix products, arithmetic and copies ran while one was open for 8% -> 4% of each run, Pallas kernels for 33% -> 38%
where the time goes in v3:
time: 532 us; the launch traced here: 527 us
  Pallas kernels  211 us (40%)
  blocking collectives  134 us (25%)
  waiting for transfers between devices  89 us (17%)
  starting transfers between devices  46 us (9%)
  other arithmetic  21.2 us (4%)
  between operations  14.7 us (3%)
  local copies, waits for them, and re-layouts  11.9 us (2%)
    all_to_all x3, blocking collectives, exchange(): return lax.all_to_all(value, 'row', 0, 0)  134 us
    all_to_all x6, waiting for transfers between devices, exchange(): return lax.all_to_all(value, 'row', 0, 0)  65.7 us
    pallas_call x4, Pallas kernels, outer_product(): pl.pallas_call(functools.partial(outer_kernel, count), grid=(GROUPS * cou...  54.6 us
    pallas_call x1, Pallas kernels, feed_back(): call(feed_back_kernel, (GROUPS + tokens // TILE,), [resident(cots.shape)]...  36.4 us
    pallas_call x1, Pallas kernels, feed(): call(feed_kernel, (GROUPS + tokens // TILE,), [resident((tokens, WIDTH)),...  30.1 us
    pallas_call x1, Pallas kernels, attend_back(): call(attend_back_kernel, (blocks,), [resident(q.shape), rows_of(WIDTH, QU...  28.1 us
    all_to_all x6, starting transfers between devices, exchange(): return lax.all_to_all(value, 'row', 0, 0)  26.8 us
    pallas_call x1, Pallas kernels, attend(): call(attend_kernel, (blocks,), [resident(q.shape)] * 3 + [pl.BlockSpec((1...  23.3 us
  transfers between devices with their start and end apart: 21, of which 9 were waited for; matrix products, arithmetic and copies ran while one was open for 4% of the time, Pallas kernels for 38%

profile of v3, /device:TPU:0, one launch (start us, length us, event | category | flops | bytes accessed | tf_op | source)
XLA Modules:
  0.0 527.0 jit_solution(17030289360792989473)
XLA Ops:
  13.5 33.6 %all_to_all.45 = bf16[4,1104,128]{2,1,0:T(8,128)(2,1)S(1)} all-to-all(bf16[4,1104,128]{2,1,0:T(8,128)(2,1)S(1)} %broadcast_in_dim.41), channel_id=1, replica_groups=mesh['dp'=2,'row'=4,'col'=4] {'row'}, dimensions={0} | all-to-all | bytes 2260992 | tf_op jit(solution)/shard_map/all_to_all | solution.py:607
  49.9 49.3 %all_to_all.46 = bf16[4,1968,128]{2,1,0:T(8,128)(2,1)} all-to-all(bf16[4,1968,128]{2,1,0:T(8,128)(2,1)S(1)} %broadcast_in_dim.42), channel_id=1, replica_groups=mesh['dp'=2,'row'=4,'col'=4] {'row'}, dimensions={0} | all-to-all | bytes 4030464 | tf_op jit(solution)/shard_map/all_to_all | solution.py:607
  110.8 46.7 %all-to-all-done.2.xs.refs_4_ = bf16[4,1152,256]{2,1,0:T(8,128)(2,1)S(1)} async-done(((bf16[4,1152,256]{2,1,0:T(8,128)(2,1)}), bf16[4,1152,256]{2,1,0:T(8,128)(2,1)S(1)}, u32[]{:S(2)}, u32[]{:S(2)}) %all-to-all-start.2) | async-done | bytes 2359328 | tf_op jit(solution)/shard_map/all_to_all | solution.py:607
  157.6 4.5 all-to-all-start.3
  163.4 14.1 %project.1 = (bf16[1152,1024]{1,0:T(8,128)(2,1)}, bf16[1152,1024]{1,0:T(8,128)(2,1)}, bf16[1152,1024]{1,0:T(8,128)(2,1)}, bf16[1152,1024]{1,0:T(8,128)(2,1)}) custom-call(bf16[4,1152,256]{2,1,0:T(8,128)(2,1)} %copy-done.2, f32[1,1024]{1,0:T(1,128)} %bitcast.96, f32[1152,128]{1,0:T(8,128)} %get-tuple-element.128.cosine.refs_5_, ...), custom_call_target="tpu_custom_call" | custom-call | flops 7247757312 | bytes 18087936 | tf_op jit(solution)/shard_map/project/pallas_call | solution.py:168
  177.5 23.3 %attend.1 = (bf16[1024,1024]{1,0:T(8,128)(2,1)}, bf16[8,4,512,256]{3,2,1,0:T(8,128)(2,1)}, bf16[1024,1024]{1,0:T(8,128)(2,1)}, bf16[1024,1024]{1,0:T(8,128)(2,1)}) custom-call(bf16[1152,1024]{1,0:T(8,128)(2,1)} %get-tuple-element.61.refs_0_, bf16[1152,1024]{1,0:T(8,128)(2,1)} %get-tuple-element.62.refs_1_.refs_3_, ...), custom_call_target="tpu_custom_call" | custom-call | flops 6442450944 | bytes 23068672 | tf_op jit(solution)/shard_map/attend/pallas_call | solution.py:241
  200.8 30.1 %feed.1 = (bf16[4,1024,656]{2,1,0:T(8,128)(2,1)}, bf16[4,1024,656]{2,1,0:T(8,128)(2,1)}, bf16[4,1024,656]{2,1,0:T(8,128)(2,1)}, bf16[4,512,256]{2,1,0:T(8,128)(2,1)}, bf16[4,512,256]{2,1,0:T(8,128)(2,1)}) custom-call(bf16[1024,1024]{1,0:T(8,128)(2,1)} %get-tuple-element.64.refs_0_.refs_2_.refs_3_, bf16[1024,1024]{1,0:T(8,128)(2,1)} %get-tuple-element.65.refs_1_.refs_3_, ...), custom_call_target="tpu_custom_call" | custom-call | flops 16508780544 | bytes 38535168 | tf_op jit(solution)/shard_map/feed/pallas_call | solution.py:431
  230.9 9.9 %outer_product.4 = bf16[2,4,4,656,128]{4,3,2,1,0:T(8,128)(2,1)} custom-call(bf16[4,1024,656]{2,1,0:T(8,128)(2,1)} %get-tuple-element.71.refs_0_, bf16[4,1024,256]{2,1,0:T(8,128)(2,1)} %all-to-all-done.3.refs_1_.refs_0_), custom_call_target="tpu_custom_call" | custom-call | flops 5502926848 | bytes 12845056 | tf_op jit(solution)/shard_map/outer_product/pallas_call | solution.py:570
  240.8 5.0 all-to-all-start.4
  246.0 36.4 %feed_back.1 = (bf16[4,1024,656]{2,1,0:T(8,128)(2,1)}, bf16[4,1024,656]{2,1,0:T(8,128)(2,1)}, bf16[1024,1024]{1,0:T(8,128)(2,1)}, bf16[1024,1024]{1,0:T(8,128)(2,1)}, f32[8,1024]{1,0:T(8,128)}) custom-call(bf16[4,1024,256]{2,1,0:T(8,128)(2,1)} %all-to-all-done.3.refs_1_.refs_0_, bf16[4,1024,656]{2,1,0:T(8,128)(2,1)} %get-tuple-element.73.refs_1_, ...), custom_call_target="tpu_custom_call" | custom-call | flops 18656264192 | bytes 40632320 | tf_op jit(solution)/shard_map/feed_back/pallas_call | solution.py:485
  282.5 20.7 %outer_product.5 = bf16[2,4,4,1312,128]{4,3,2,1,0:T(8,128)(2,1)} custom-call(bf16[4,1024,656]{2,1,0:T(8,128)(2,1)} %get-tuple-element.77.refs_0_, bf16[4,1024,656]{2,1,0:T(8,128)(2,1)} %get-tuple-element.78.refs_1_, bf16[1024,1024]{1,0:T(8,128)(2,1)} %get-tuple-element.64.refs_0_.refs_2_.refs_3_, bf16[1024,1024]{1,0:T(8,128)(2,1)} %get-tuple-element.64.refs_0_.refs_2_.refs_3_), custom_call_target="tpu_custom_call" | custom-call | flops 11005853696 | bytes 23592960 | tf_op jit(solution)/shard_map/outer_product/pallas_call | solution.py:570
  305.9 4.9 all-to-all-start.5
  311.1 28.1 %attend_back.1 = (bf16[1024,1024]{1,0:T(8,128)(2,1)}, bf16[1024,1024]{1,0:T(8,128)(2,1)}, bf16[1024,1024]{1,0:T(8,128)(2,1)}, bf16[64,2048]{1,0:T(8,128)(2,1)}, ...) custom-call(bf16[1152,1024]{1,0:T(8,128)(2,1)} %get-tuple-element.61.refs_0_, ...), custom_call_target="tpu_custom_call" | custom-call | flops 8589934592 | bytes 23068672 | tf_op jit(solution)/shard_map/attend_back/pallas_call | solution.py:325
  344.5 4.8 all-to-all-done.5
  349.5 12.1 %outer_product.6.refs_4_ = bf16[2,4,4,1024,128]{4,3,2,1,0:T(8,128)(2,1)} custom-call(bf16[1024,1024]{1,0:T(8,128)(2,1)} %get-tuple-element.94.refs_0_.gq, bf16[1024,1024]{1,0:T(8,128)(2,1)} %get-tuple-element.87.refs_1_, bf16[1152,1024]{1,0:T(8,128)(2,1)} %get-tuple-element.88.refs_2_.refs_3_, bf16[1024,1024]{1,0:T(8,128)(2,1)} %get-tuple-element.89.refs_3_.g_branch), custom_call_target="tpu_custom_call" | custom-call | flops 4294967296 | bytes 10485760 | tf_op jit(solution)/shard_map/outer_product/pallas_call | solution.py:570
  364.6 11.9 %outer_product.7 = bf16[2,4,4,1024,128]{4,3,2,1,0:T(8,128)(2,1)} custom-call(bf16[1024,1024]{1,0:T(8,128)(2,1)} %get-tuple-element.92.refs_0_.gk, bf16[1024,1024]{1,0:T(8,128)(2,1)} %get-tuple-element.93.refs_1_.gv, bf16[1152,1024]{1,0:T(8,128)(2,1)} %get-tuple-element.88.refs_2_.refs_3_, ...), custom_call_target="tpu_custom_call", output_to_operand_aliasing={{}: (4, {})} | custom-call | flops 4294967296 | bytes 10485760 | tf_op jit(solution)/shard_map/outer_product/pallas_call | solution.py:570
  376.5 15.8 %unproject.1 = (bf16[4,1024,256]{2,1,0:T(8,128)(2,1)}, f32[8,1024]{1,0:T(8,128)}) custom-call(bf16[4,1152,256]{2,1,0:T(8,128)(2,1)} %copy-done.2, bf16[1024,1024]{1,0:T(8,128)(2,1)} %get-tuple-element.94.refs_0_.gq, bf16[1024,1024]{1,0:T(8,128)(2,1)} %get-tuple-element.92.refs_0_.gk, bf16[1024,1024]{1,0:T(8,128)(2,1)} %get-tuple-element.93.refs_1_.gv, ...), custom_call_target="tpu_custom_call" | custom-call | flops 6442450944 | bytes 18874368 | tf_op jit(solution)/shard_map/unproject/pallas_call | solution.py:521
  392.3 50.6 %all_to_all.47 = bf16[4,1024,256]{2,1,0:T(8,128)(2,1)S(1)} all-to-all(bf16[4,1024,256]{2,1,0:T(8,128)(2,1)} %get-tuple-element.96), channel_id=1, replica_groups=mesh['dp'=2,'row'=4,'col'=4] {'row'}, dimensions={0} | all-to-all | bytes 4194304 | tf_op jit(solution)/shard_map/all_to_all | solution.py:607
  443.0 4.4 all-to-all-start.7
  458.5 9.8 %collective-permute-done.5 = f32[2,1024]{1,0:T(2,128)S(1)} collective-permute-done((f32[2,1024]{1,0:T(2,128)S(1)}, f32[2,1024]{1,0:T(2,128)S(1)}, u32[]{:S(2)}, u32[]{:S(2)}) %collective-permute-start.5) | collective-permute-done | bytes 8224 | tf_op jit(solution)/shard_map/ppermute | solution.py:666
  468.2 4.7 collective-permute-start.6
  474.1 4.5 collective-permute-done.6
  478.7 4.3 all-to-all-start.8
  494.2 14.1 %all-to-all-done.8 = bf16[4,1024,128]{2,1,0:T(8,128)(2,1)} async-done(((bf16[4,1024,128]{2,1,0:T(8,128)(2,1)}), bf16[4,1024,128]{2,1,0:T(8,128)(2,1)}, u32[]{:S(2)}, u32[]{:S(2)}) %all-to-all-start.8) | async-done | bytes 1048608 | tf_op jit(solution)/shard_map/all_to_all | solution.py:607
  (139 shorter events, 68.7 us)
Async XLA Ops:
  7.2 42.1 %copy-start = (bf16[656,256]{1,0:T(8,128)(2,1)S(1)}, bf16[656,256]{1,0:T(8,128)(2,1)}, u32[]{:S(2)}) copy-start(bf16[656,256]{1,0:T(8,128)(2,1)} %param.20) | copy-start | bytes 1007620
  7.2 156.2 %all-gather.5.cloned.1.call-start = ((), (), s32[]{:S(2)}) async-start(), calls=%async_computation.15 | async-start | bytes 9437184 | tf_op jit(solution)/shard_map/all_gather | solution.py:623
  49.2 151.6 %all-gather.7.cloned.1.call-start = ((), (), s32[]{:S(2)}) async-start(), calls=%async_computation.16 | async-start | bytes 18137088 | tf_op jit(solution)/shard_map/all_gather | solution.py:623
  49.8 49.3 %copy-start.4 = (bf16[4096,256]{1,0:T(8,128)(2,1)S(1)}, bf16[4096,256]{1,0:T(8,128)(2,1)}, u32[]{:S(2)}) copy-start(bf16[4096,256]{1,0:T(8,128)(2,1)} %param.13) | copy-start | bytes 6291460
  101.1 56.5 %all-to-all-start.2 = ((bf16[4,1152,256]{2,1,0:T(8,128)(2,1)}), bf16[4,1152,256]{2,1,0:T(8,128)(2,1)S(1)}, u32[]{:S(2)}, u32[]{:S(2)}) async-start(bf16[4,1152,256]{2,1,0:T(8,128)(2,1)} %pad_maximum_fusion), calls=%async_computation.2 | async-start | bytes 4718592 | tf_op jit(solution)/shard_map/all_to_all | solution.py:607
  157.6 73.3 %all-to-all-start.3 = ((bf16[4,1024,256]{2,1,0:T(8,128)(2,1)}), bf16[4,1024,256]{2,1,0:T(8,128)(2,1)}, u32[]{:S(2)}, u32[]{:S(2)}) async-start(bf16[4,1024,256]{2,1,0:T(8,128)(2,1)} %bitcast.76), calls=%async_computation.3 | async-start | bytes 4194304 | tf_op jit(solution)/shard_map/all_to_all | solution.py:607
  162.0 141.2 %reduce-scatter.4.cloned.1.call-start = ((), (), s32[]{:S(2)}) async-start(), calls=%async_computation.12 | async-start | bytes 6045696 | tf_op jit(solution)/shard_map/reduce_scatter | solution.py:628
  240.8 41.6 %all-to-all-start.4 = ((bf16[4,512,256]{2,1,0:T(8,128)(2,1)}), bf16[4,512,256]{2,1,0:T(8,128)(2,1)S(1)}, u32[]{:S(2)}, u32[]{:S(2)}) async-start(bf16[4,512,256]{2,1,0:T(8,128)(2,1)} %get-tuple-element.68), calls=%async_computation.4 | async-start | bytes 2097152 | tf_op jit(solution)/shard_map/all_to_all | solution.py:607
  245.8 197.1 %reduce-scatter.8.cloned.1.call-start = ((), (), s32[]{:S(2)}) async-start(), calls=%async_computation.14 | async-start | bytes 12091392 | tf_op jit(solution)/shard_map/reduce_scatter | solution.py:628
  305.9 43.5 %all-to-all-start.5 = ((bf16[4,840,256]{2,1,0:T(8,128)(2,1)}), bf16[4,840,256]{2,1,0:T(8,128)(2,1)S(1)}, u32[]{:S(2)}, u32[]{:S(2)}) async-start(bf16[4,840,256]{2,1,0:T(8,128)(2,1)} %pad_maximum_fusion.2), calls=%async_computation.6 | async-start | bytes 3440640 | tf_op jit(solution)/shard_map/all_to_all | solution.py:607
  310.8 167.8 %reduce-scatter.6.cloned.1.call-start = ((), (), s32[]{:S(2)}) async-start(), calls=%async_computation.13 | async-start | bytes 9437184 | tf_op jit(solution)/shard_map/reduce_scatter | solution.py:628
  339.2 22.4 %collective-permute-start = (bf16[64,2048]{1,0:T(8,128)(2,1)}, bf16[64,2048]{1,0:T(8,128)(2,1)S(1)}, u32[]{:S(2)}, u32[]{:S(2)}) collective-permute-start(bf16[64,2048]{1,0:T(8,128)(2,1)} %get-tuple-element.86), channel_id=1, source_target_pairs={{0,4},{4,8},{8,12},{1,5},{5,9},{9,13},{2,6},{6,10},{10,14},{3,7},{... | collective-permute-start | bytes 786440 | tf_op jit(solution)/shard_map/ppermute | solution.py:745
  343.2 18.3 %collective-permute-start.1 = (bf16[64,2048]{1,0:T(8,128)(2,1)}, bf16[64,2048]{1,0:T(8,128)(2,1)S(1)}, u32[]{:S(2)}, u32[]{:S(2)}) collective-permute-start(bf16[64,2048]{1,0:T(8,128)(2,1)} %get-tuple-element.91), channel_id=1, source_target_pairs={{4,0},{8,4},{12,8},{5,1},{9,5},{13,9},{6,2},{10,6},{14,10},{7,3},{... | collective-permute-start | bytes 786440 | tf_op jit(solution)/shard_map/ppermute | solution.py:745
  443.0 40.0 %slice-start = ((bf16[4,840,256]{2,1,0:T(8,128)(2,1)}), bf16[4,512,256]{2,1,0:T(8,128)(2,1)S(1)}, s32[]{:S(2)}) async-start(bf16[4,840,256]{2,1,0:T(8,128)(2,1)} %copy-done.3), calls=%async_computation.17 | async-start | bytes 2097152 | tf_op jit(solution)/shard_map/split | solution.py:824
  443.0 35.7 %all-to-all-start.7 = ((bf16[4,1312,128]{2,1,0:T(8,128)(2,1)}), bf16[4,1312,128]{2,1,0:T(8,128)(2,1)}, u32[]{:S(2)}, u32[]{:S(2)}) async-start(bf16[4,1312,128]{2,1,0:T(8,128)(2,1)} %bitcast.78), calls=%async_computation.10 | async-start | bytes 2686976 | tf_op jit(solution)/shard_map/all_to_all | solution.py:607
  447.5 3.8 collective-permute-start.2
  451.3 3.9 collective-permute-start.3
  455.2 1.2 collective-permute-start.4
  456.4 11.8 %collective-permute-start.5 = (f32[2,1024]{1,0:T(2,128)S(1)}, f32[2,1024]{1,0:T(2,128)S(1)}, u32[]{:S(2)}, u32[]{:S(2)}) collective-permute-start(f32[2,1024]{1,0:T(2,128)S(1)} %add.87), channel_id=1, source_target_pairs={{0,4},{4,0},{8,12},{12,8},{1,5},{5,1},{9,13},{13,9},{2,6},{6,2},{1... | collective-permute-start | bytes 24584 | tf_op jit(solution)/shard_map/ppermute | solution.py:666
  468.2 10.4 %collective-permute-start.6 = (f32[2,1024]{1,0:T(2,128)S(1)}, f32[2,1024]{1,0:T(2,128)S(1)}, u32[]{:S(2)}, u32[]{:S(2)}) collective-permute-start(f32[2,1024]{1,0:T(2,128)S(1)} %add.88), channel_id=1, source_target_pairs={{0,8},{4,12},{8,0},{12,4},{1,9},{5,13},{9,1},{13,5},{2,10},{6,14},... | collective-permute-start | bytes 24584 | tf_op jit(solution)/shard_map/ppermute | solution.py:666
  473.0 13.2 %collective-permute-start.9 = (bf16[656,128]{1,0:T(8,128)(2,1)S(1)}, bf16[656,128]{1,0:T(8,128)(2,1)S(1)}, u32[]{:S(2)}, u32[]{:S(2)}) collective-permute-start(bf16[656,128]{1,0:T(8,128)(2,1)S(1)} %reduce_sum.81), channel_id=1, source_target_pairs={{0,16},{16,0},{1,17},{17,1},{2,18},{18,2},{3,19},{19,3},{4,20},{20... | collective-permute-start | bytes 503816 | tf_op jit(solution)/shard_map/ppermute | solution.py:595
  478.7 29.6 %all-to-all-start.8 = ((bf16[4,1024,128]{2,1,0:T(8,128)(2,1)}), bf16[4,1024,128]{2,1,0:T(8,128)(2,1)}, u32[]{:S(2)}, u32[]{:S(2)}) async-start(bf16[4,1024,128]{2,1,0:T(8,128)(2,1)} %bitcast.79), calls=%async_computation.11 | async-start | bytes 2097152 | tf_op jit(solution)/shard_map/all_to_all | solution.py:607
  490.5 20.4 %collective-permute-start.8 = (bf16[1312,128]{1,0:T(8,128)(2,1)S(1)}, bf16[1312,128]{1,0:T(8,128)(2,1)S(1)}, u32[]{:S(2)}, u32[]{:S(2)}) collective-permute-start(bf16[1312,128]{1,0:T(8,128)(2,1)S(1)} %reduce_sum.79), channel_id=1, source_target_pairs={{0,16},{16,0},{1,17},{17,1},{2,18},{18,2},{3,19},{19,3},{4,20},{20... | collective-permute-start | bytes 1007624 | tf_op jit(solution)/shard_map/ppermute | solution.py:595
  509.8 7.3 %collective-permute-start.7 = (bf16[1024,128]{1,0:T(8,128)(2,1)S(1)}, bf16[1024,128]{1,0:T(8,128)(2,1)S(1)}, u32[]{:S(2)}, u32[]{:S(2)}) collective-permute-start(bf16[1024,128]{1,0:T(8,128)(2,1)S(1)} %reduce_sum.78), channel_id=1, source_target_pairs={{0,16},{16,0},{1,17},{17,1},{2,18},{18,2},{3,19},{19,3},{4,20},{20... | collective-permute-start | bytes 786440 | tf_op jit(solution)/shard_map/ppermute | solution.py:595
  (13 other events, 86.2 us)
Sparse Core Ops, SparseCore 0:
  49.3 53.4 all-gather.4
  104.7 87.0 all-gather.6
  241.0 58.6 reduce-scatter.3
  303.3 83.8 reduce-scatter.7
  390.9 71.3 reduce-scatter.5

commit v4 on v3

--- a/solution.py
+++ b/solution.py
@@ -111,10 +111,6 @@
     return jnp.concatenate([slots[o, rows, :] for o in range(SLOTS)], axis=1)
 
 
-def inner_rows(tile):
-    return pl.ds(pl.multiple_of(pl.program_id(0) * tile + REACH, REACH), tile)
-
-
 def put_rows(slots, total):
     for o in range(SLOTS):
         slots[o] = total[:, o * 256 : (o + 1) * 256].astype(slots.dtype)
@@ -155,9 +151,9 @@
 
     made = nt(rows[...], joined_rows((low, high)))
     c, s = cosine[...], sine[...]
-    for t, out in ((0, q), (1, k)):
-        first = made[:, t * GROUP : t * GROUP + LANES]
-        second = made[:, t * GROUP + LANES : (t + 1) * GROUP]
+    for t, out, scale in ((0, q, HEAD**-0.5), (1, k, 1.0)):
+        first = made[:, t * GROUP : t * GROUP + LANES] * scale
+        second = made[:, t * GROUP + LANES : (t + 1) * GROUP] * scale
         out[:, :LANES] = (first * c - second * s).astype(BF16)
         out[:, LANES:] = (second * c + first * s).astype(BF16)
     v[...] = made[:, 2 * GROUP :].astype(BF16)
@@ -198,30 +194,49 @@
     return total
 
 
+def pair(refs, lanes=slice(None)):
+    return jnp.concatenate([ref[:, lanes] for ref in refs], axis=0)
+
+
+def pair_of(shape):
+    lead = len(shape) - 2
+    return [
+        pl.BlockSpec(
+            shape[:lead] + (QUERY, shape[-1]),
+            lambda i, more=more: (0,) * lead + (i + more, 0),
+        )
+        for more in range(2)
+    ]
+
+
+MIDDLE = slice(REACH, REACH + QUERY)
+
+
 def attend_kernel(*refs):
-    q, k, v, bias, xs, gain, low, high = refs[:8]
-    attended, probability, mixed, normed, held = refs[8:]
+    q, k, v, xs = (refs[2 * t : 2 * t + 2] for t in range(4))
+    bias, gain, low, high = refs[8:12]
+    attended, probability, mixed, normed, held = refs[12:]
 
     @at_first
     def _():
         for p in range(GROUPS):
             held[pl.ds(p * GROUP, GROUP), :] = joined_rows((low, high), p)
 
-    span = pl.ds(pl.multiple_of(pl.program_id(0) * QUERY, QUERY), QUERY + 2 * REACH)
-    own = inner_rows(QUERY)
     halves, wholes = head_masks()
     masked = bias[0]
     for p in range(GROUPS):
         lanes = slice(p * GROUP, (p + 1) * GROUP)
-        scores = nt(spread(q[own, lanes], halves), k[span, lanes]) * HEAD**-0.5
-        scores = jnp.concatenate(
-            [scores[h * QUERY : (h + 1) * QUERY] + masked for h in range(4)], axis=0
-        )
-        exponent = jnp.exp(scores - jnp.max(scores, axis=1, keepdims=True))
-        weight = (exponent * (1.0 / jnp.sum(exponent, axis=1, keepdims=True))).astype(BF16)
-        probability[0, p] = weight
-        attended[:, lanes] = collect(nn(weight, v[span, lanes]), wholes).astype(BF16)
-    total = whole_rows(xs, own).astype(F32) + nn(attended[...], held[...])
+        scores = nt(spread(pair(q, lanes)[MIDDLE], halves), pair(k, lanes))
+        for h in range(4):
+            rows = slice(h * QUERY, (h + 1) * QUERY)
+            score = scores[rows] + masked
+            exponent = jnp.exp(score - jnp.max(score, axis=1, keepdims=True))
+            share = 1.0 / jnp.sum(exponent, axis=1, keepdims=True)
+            probability[0, p, rows, :] = (exponent * share).astype(BF16)
+        made = collect(nn(probability[0, p], pair(v, lanes)), wholes)
+        attended[:, lanes] = made.astype(BF16)
+    values = [jnp.concatenate([ref[o] for ref in xs], axis=0)[MIDDLE] for o in range(SLOTS)]
+    total = jnp.concatenate(values, axis=1).astype(F32) + nn(attended[...], held[...])
     mixed[...] = total.astype(BF16)
     normed[...] = (norm(total)[0] * gain[...]).astype(BF16)
 
@@ -241,9 +256,9 @@
     return call(
         attend_kernel,
         (blocks,),
-        [resident(q.shape)] * 3
-        + [pl.BlockSpec((1, QUERY, span), lambda i: (i, 0, 0))]
-        + [resident(xs.shape), resident((1, WIDTH))]
+        pair_of((QUERY, WIDTH)) * 3
+        + pair_of((SLOTS, QUERY, 256))
+        + [pl.BlockSpec((1, QUERY, span), lambda i: (i, 0, 0)), resident((1, WIDTH))]
         + out_weight(),
         [
             rows_of(WIDTH, QUERY),
@@ -261,86 +276,111 @@
         blocks * GROUPS * 2 * 2 * 4 * QUERY * span * GROUP + 2 * tokens * WIDTH * WIDTH,
         14 * tokens * WIDTH + blocks * GROUPS * 8 * QUERY * span,
         "attend",
-    )(q, k, v, bias, xs, gain, heads, heads)
+    )(q, q, k, k, v, v, xs, xs, bias, gain, heads, heads)
 
 
 def attend_back_kernel(*refs):
-    q, grad, weights, k, v, cosine, sine = refs[:7]
-    gq, gk, gv, to_low, to_high, edges, sum_k, sum_v = refs[7:]
-    step, steps = pl.program_id(0), pl.num_programs(0)
-    tokens = gk.shape[0]
+    q, k, v, table_c, table_s = (refs[2 * t : 2 * t + 2] for t in range(5))
+    grad, weights = refs[10:12]
+    gq, gk, gv, to_low, to_high, edges, sum_k, sum_v = refs[12:]
+    step, last = pl.program_id(0), pl.num_programs(0) - 1
 
     @at_first
     def _():
         sum_k[...] = jnp.zeros_like(sum_k)
         sum_v[...] = jnp.zeros_like(sum_v)
 
-    start = pl.multiple_of(step * QUERY, QUERY)
-    span = pl.ds(start, QUERY + 2 * REACH)
-    halves, wholes = head_masks()
-    own = inner_rows(QUERY)
-    c, s = cosine[own, :], sine[own, :]
+    @pl.when(step < last)
+    def _():
+        halves, wholes = head_masks()
+        c, s = pair(table_c)[MIDDLE], pair(table_s)[MIDDLE]
+        for p in range(GROUPS):
+            lanes = slice(p * GROUP, (p + 1) * GROUP)
+            queries = spread(pair(q, lanes)[MIDDLE], halves)
+            grads = spread(grad[:, lanes], wholes)
+            d_weights = nt(grads, pair(v, lanes))
+            parts = []
+            for h in range(4):
+                rows = slice(h * QUERY, (h + 1) * QUERY)
+                wide, d_weight = weights[0, p, rows, :].astype(F32), d_weights[rows]
+                mean = jnp.sum(wide * d_weight, axis=1, keepdims=True)
+                parts.append((wide * (d_weight - mean)).astype(BF16))
+            g_score = jnp.concatenate(parts, axis=0)
+            made = collect(nn(g_score, pair(k, lanes)), halves) * HEAD**-0.5
+            first, second = made[:, :LANES], made[:, LANES:]
+            gq[:, p * GROUP : p * GROUP + LANES] = (first * c + second * s).astype(BF16)
+            gq[:, p * GROUP + LANES : (p + 1) * GROUP] = (second * c - first * s).astype(BF16)
+            for total, made in (
+                (sum_k, tn(g_score, queries)),
+                (sum_v, tn(weights[0, p], grads)),
+            ):
+                total[0:QUERY, lanes] = total[QUERY:, lanes] + made[0:QUERY]
+                total[QUERY:, lanes] = made[QUERY:]
+
+    @pl.when(step == last)
+    def _():
+        for total in (sum_k, sum_v):
+            total[0:QUERY, :] = total[QUERY:, :]
+
+    c, s = table_c[0][...], table_s[0][...]
     for p in range(GROUPS):
-        lanes = slice(p * GROUP, (p + 1) * GROUP)
-        queries = spread(q[own, lanes], halves)
-        grads = spread(grad[:, lanes], wholes)
-        block_k, block_v = k[span, lanes], v[span, lanes]
-        weight = weights[0, p]
-        wide = weight.astype(F32)
-        d_weight = nt(grads, block_v)
-        mean = jnp.sum(wide * d_weight, axis=1, keepdims=True)
-        g_score = (wide * (d_weight - mean)).astype(BF16)
-        made = collect(nn(g_score, block_k), halves) * HEAD**-0.5
-        first, second = made[:, :LANES], made[:, LANES:]
-        gq[:, p * GROUP : p * GROUP + LANES] = (first * c + second * s).astype(BF16)
-        gq[:, p * GROUP + LANES : (p + 1) * GROUP] = (second * c - first * s).astype(BF16)
-        sum_k[span, lanes] += tn(g_score, queries) * HEAD**-0.5
-        sum_v[span, lanes] += tn(weight, grads)
-
-    @pl.when(step == steps - 1)
+        one, two = slice(p * GROUP, p * GROUP + LANES), slice(p * GROUP + LANES, (p + 1) * GROUP)
+        first, second = sum_k[0:QUERY, one], sum_k[0:QUERY, two]
+        gk[:, one] = (first * c + second * s).astype(BF16)
+        gk[:, two] = (second * c - first * s).astype(BF16)
+    gv[...] = sum_v[0:QUERY, :].astype(BF16)
+
+    @at_first
     def _():
         for t, total in ((0, sum_k), (1, sum_v)):
             lanes = slice(t * WIDTH, (t + 1) * WIDTH)
             to_low[:, lanes] = total[0:REACH, :].astype(BF16)
-            edges[0, :, lanes] = total[REACH : 2 * REACH, :]
-            edges[1, :, lanes] = total[pl.ds(tokens, REACH), :]
-            to_high[:, lanes] = total[pl.ds(tokens + REACH, REACH), :].astype(BF16)
-        for at in range(0, tokens, QUERY):
-            own = pl.ds(REACH + at, QUERY)
-            c, s = cosine[own, :], sine[own, :]
-            for p in range(GROUPS):
-                one, two = p * GROUP, p * GROUP + LANES
-                first, second = sum_k[own, pl.ds(one, LANES)], sum_k[own, pl.ds(two, LANES)]
-                gk[pl.ds(at, QUERY), pl.ds(one, LANES)] = (first * c + second * s).astype(BF16)
-                gk[pl.ds(at, QUERY), pl.ds(two, LANES)] = (second * c - first * s).astype(BF16)
-            gv[pl.ds(at, QUERY), :] = sum_v[own, :].astype(BF16)
+            edges[0, :, lanes] = total[REACH:QUERY, :]
+
+    @pl.when(step == last)
+    def _():
+        for t, total in ((0, sum_k), (1, sum_v)):
+            lanes = slice(t * WIDTH, (t + 1) * WIDTH)
+            edges[1, :, lanes] = total[0:REACH, :]
+            to_high[:, lanes] = total[REACH:QUERY, :].astype(BF16)
 
 
 def attend_back(q, grad, weights, k, v, cosine, sine):
     tokens = grad.shape[0]
     blocks = tokens // QUERY
     span = QUERY + 2 * REACH
-    full = resident((tokens, WIDTH))
     edge = (REACH, 2 * WIDTH)
+
+    def own(i):
+        return jnp.minimum(i, blocks - 1)
+
+    def pairs(width):
+        return [
+            pl.BlockSpec((QUERY, width), lambda i: (i, 0)),
+            pl.BlockSpec((QUERY, width), lambda i: (own(i) + 1, 0)),
+        ]
+
     return call(
         attend_back_kernel,
-        (blocks,),
-        [
-            resident(q.shape),
-            rows_of(WIDTH, QUERY),
-            pl.BlockSpec((1, GROUPS, 4 * QUERY, span), lambda i: (i, 0, 0, 0)),
-            resident(q.shape),
-            resident(q.shape),
-            resident(cosine.shape),
-            resident(cosine.shape),
+        (blocks + 1,),
+        pairs(WIDTH) * 3
+        + pairs(LANES) * 2
+        + [
+            pl.BlockSpec((QUERY, WIDTH), lambda i: (own(i), 0)),
+            pl.BlockSpec((1, GROUPS, 4 * QUERY, span), lambda i: (own(i), 0, 0, 0)),
         ],
-        [rows_of(WIDTH, QUERY), full, full, resident(edge), resident(edge), resident((2,) + edge)],
-        [struct((tokens, WIDTH), BF16)] * 3 + [struct(edge, BF16)] * 2 + [struct((2,) + edge, F32)],
-        [pltpu.VMEM(q.shape, F32)] * 2,
+        [pl.BlockSpec((QUERY, WIDTH), lambda i: (own(i), 0))]
+        + [rows_of(WIDTH, QUERY)] * 2
+        + [resident(edge), resident(edge), resident((2,) + edge)],
+        [struct((tokens, WIDTH), BF16)]
+        + [struct(q.shape, BF16)] * 2
+        + [struct(edge, BF16)] * 2
+        + [struct((2,) + edge, F32)],
+        [pltpu.VMEM((span, WIDTH), F32)] * 2,
         blocks * GROUPS * 2 * 4 * 4 * QUERY * span * GROUP,
         14 * tokens * WIDTH + blocks * GROUPS * 8 * QUERY * span,
         "attend_back",
-    )(q, grad, weights, k, v, cosine, sine)
+    )(q, q, k, k, v, v, cosine, cosine, sine, sine, grad, weights)
 
 
 def edge_kernel(*refs):
@@ -363,9 +403,8 @@
 
 
 def add_edges(gk, gv, edges, from_low, from_high, cosine, sine):
-    tokens = gk.shape[0]
-    far = tokens // REACH - 1
-    rows = pl.BlockSpec((REACH, WIDTH), lambda i: (i * far, 0))
+    far = gk.shape[0] // REACH - 3
+    rows = pl.BlockSpec((REACH, WIDTH), lambda i: (1 + i * far, 0))
     table = pl.BlockSpec((REACH, LANES), lambda i: (1 + i * far, 0))
     came = resident(from_low.shape)
     return pl.pallas_call(
@@ -397,7 +436,7 @@
     normed, mixed, weight = refs[0], refs[1], refs[2:4]
     hidden, slope, gelu, early, late, total = refs[4:]
     ff = hidden.shape[2]
-    half = GROUPS + total.shape[0] // TILE // 2
+    half = GROUPS + total.shape[0] // TILE - 1
     step = pl.program_id(0)
 
     @pl.when(step < GROUPS)
@@ -427,7 +466,7 @@
 
 def feed(normed, mixed, weight):
     tokens, ff = normed.shape[0], weight.shape[2] // 3
-    steps = tokens // TILE // 2
+    last = tokens // TILE - 1
     return call(
         feed_kernel,
         (GROUPS + tokens // TILE,),
@@ -435,13 +474,12 @@
         [units_of(tokens, ff)] * 3
         + [
             pl.BlockSpec(
-                (SLOTS, TILE, 256),
-                lambda i, first=first: (0, jnp.clip(i - GROUPS - first, 0, steps - 1), 0),
-            )
-            for first in (0, steps)
+                (SLOTS, TILE, 256), lambda i: (0, jnp.clip(i - GROUPS, 0, last - 1), 0)
+            ),
+            resident((SLOTS, TILE, 256)),
         ],
         [struct((GROUPS, tokens, ff), BF16)] * 3
-        + [struct((SLOTS, tokens // 2, 256), BF16)] * 2,
+        + [struct((SLOTS, tokens - TILE, 256), BF16), struct((SLOTS, TILE, 256), BF16)],
         [pltpu.VMEM((tokens, WIDTH), F32)],
         2 * tokens * WIDTH * 3 * GROUPS * ff,
         6 * tokens * WIDTH + 6 * GROUPS * ff * (tokens + WIDTH),
@@ -501,10 +539,12 @@
     )(cots, slope, gelu, mixed, gain, weight, weight, heads, heads)
 
 
-def unproject_kernel(xs, gq, gk, gv, g_branch, gain, low, high, outs, gain_part, held, total):
+def unproject_kernel(*refs):
+    xs, gq, gk, gv, g_branch, gain, low, high, early, late, gain_part, held, total = refs
     @pl.when(pl.program_id(0) < GROUPS)
     def _():
-        held[0] = jnp.concatenate([gq[...], gk[...], gv[...]], axis=1)
+        own = pl.ds(REACH, gq.shape[0])
+        held[0] = jnp.concatenate([gq[...], gk[own, :], gv[own, :]], axis=1)
         add_up(total, held, (low, high))
 
     @pl.when(pl.program_id(0) >= GROUPS)
@@ -512,8 +552,9 @@
         gradient = total[step_rows(), :]
         unit, inverse = norm(whole_rows(xs, between_rows()).astype(F32))
         add_gain(gain_part, gradient * unit)
-        back = norm_back(gradient, unit, inverse, gain[...])
-        put_rows(outs, g_branch[...].astype(F32) + back)
+        made = g_branch[...].astype(F32) + norm_back(gradient, unit, inverse, gain[...])
+        pl.when(pl.program_id(0) == GROUPS)(lambda: put_rows(early, made))
+        pl.when(pl.program_id(0) > GROUPS)(lambda: put_rows(late, made))
 
 
 def unproject(xs, gq, gk, gv, g_branch, gain, weight):
@@ -522,11 +563,22 @@
         unproject_kernel,
         (GROUPS + tokens // TILE,),
         [resident(xs.shape)]
-        + [pl.BlockSpec((tokens, GROUP), lambda i: (0, group_of(i)))] * 3
+        + [
+            pl.BlockSpec((value.shape[0], GROUP), lambda i: (0, group_of(i)))
+            for value in (gq, gk, gv)
+        ]
         + [later_rows(WIDTH), resident((1, WIDTH))]
         + weight_rows(3 * GROUP),
-        [LATER_BLOCKS, resident((8, WIDTH))],
-        [struct((SLOTS, tokens, 256), BF16), struct((8, WIDTH), F32)],
+        [
+            resident((SLOTS, TILE, 256)),
+            pl.BlockSpec((SLOTS, TILE, 256), lambda i: (0, jnp.maximum(i - GROUPS - 1, 0), 0)),
+            resident((8, WIDTH)),
+        ],
+        [
+            struct((SLOTS, TILE, 256), BF16),
+            struct((SLOTS, tokens - TILE, 256), BF16),
+            struct((8, WIDTH), F32),
+        ],
         [pltpu.VMEM((1, tokens, 3 * GROUP), BF16), pltpu.VMEM((tokens, WIDTH), F32)],
         2 * tokens * WIDTH * 3 * WIDTH,
         12 * tokens * WIDTH + 6 * WIDTH * WIDTH,
@@ -534,16 +586,15 @@
     )(xs, gq, gk, gv, g_branch, gain, weight, weight)
 
 
-def outer_kernel(count, *refs):
+def outer_kernel(count, tokens, *refs):
     inner, outer, out = refs[:count], refs[count : 2 * count], refs[-1]
-    tokens = inner[0].shape[-2]
+
+    def own_rows(value):
+        return value[pl.ds((value.shape[0] - tokens) // 2, tokens), :]
 
     def make(left, right):
-        left = left[0] if len(left.shape) == 3 else left[...]
-        if len(right.shape) == 3:
-            right = whole_rows(right)
-        else:
-            right = right[pl.ds((right.shape[0] - tokens) // 2, tokens), :]
+        left = left[0] if len(left.shape) == 3 else own_rows(left)
+        right = whole_rows(right) if len(right.shape) == 3 else own_rows(right)
         made = tn(left, right)
         for a in range(2):
             for o in range(SLOTS):
@@ -554,21 +605,20 @@
         pl.when(pl.program_id(0) % count == t)(functools.partial(make, inner[t], outer[t]))
 
 
-def outer_product(inner, outer, places, kinds, base=None):
+def outer_product(tokens, inner, outer, places, kinds, base=None):
     count = len(inner)
-    tokens = inner[0].shape[-2]
     width = inner[0].shape[2] if inner[0].ndim == 3 else GROUP
     stride = places[-1] - places[0]
 
     def inner_block(value):
         if value.ndim == 3:
             return pl.BlockSpec((1, tokens, width), lambda i: (i // count, 0, 0))
-        return pl.BlockSpec((tokens, GROUP), lambda i: (0, i // count))
+        return pl.BlockSpec((value.shape[0], GROUP), lambda i: (0, i // count))
 
     more = [] if base is None else [base]
     moved = 8 * count * width * (tokens + WIDTH) + 2 * tokens * WIDTH
     return pl.pallas_call(
-        functools.partial(outer_kernel, count),
+        functools.partial(outer_kernel, count, tokens),
         grid=(GROUPS * count,),
         in_specs=[inner_block(value) for value in inner]
         + [resident(value.shape) for value in outer]
@@ -807,11 +857,11 @@
     attended, weights, mixed, normed_ffn = attend(q, k, v, bias, xs, gain_rows[1], heads_w)
     hidden, slope, gelu, early, late = feed(normed_ffn, mixed, feed_w)
     early = exchange(after(early, cots))
-    down_parts = outer_product([hidden], [cots], (0,), 1)
+    down_parts = outer_product(tokens, [hidden], [cots], (0,), 1)
     g_act, g_gate, g_branch, g_attended, gain_part_ffn = feed_back(
         cots, after(slope, down_parts), gelu, mixed, gain_rows[1], feed_w, heads_w
     )
-    up_parts = outer_product([after(g_act, early), g_gate], [normed_ffn] * 2, (0, 1), 2)
+    up_parts = outer_product(tokens, [after(g_act, early), g_gate], [normed_ffn] * 2, (0, 1), 2)
     if own_slice:
         down_own, up_own = reduce_groups(down_parts), reduce_groups(up_parts)
         g_attended = after(g_attended, up_parts, down_own)
@@ -822,25 +872,27 @@
     if own_slice:
         rest = down_own.reshape(rows, -1, 256)
         late, rest = jnp.split(
-            exchange(jnp.concatenate([after(late, early), rest], axis=1)), [tokens // 2], axis=1
+            exchange(jnp.concatenate([after(late, early), rest], axis=1)), [TILE], axis=1
         )
         down_sum = rest.reshape(down_own.shape)
-        gq = after(gq, late, down_sum)
     else:
         late = exchange(late)
     layer_out = jnp.concatenate([early, late], axis=1)
-    heads_parts = outer_product([gq, attended], [normed_attn, g_branch], (0, 3), 4)
-    from_low = after(from_low, heads_parts)
     gk, gv = add_edges(gk, gv, edges, from_low, from_high, cosine, sine)
-    heads_parts = outer_product([gk, gv], [normed_attn] * 2, (1, 2), 4, heads_parts)
-    grad_slots, gain_part_attn = unproject(
-        xs, after(gq, heads_parts), gk, gv, g_branch, gain_rows[0], heads_w
+    first_tokens, other_tokens, gain_part_attn = unproject(
+        xs, gq, gk, gv, g_branch, gain_rows[0], heads_w
     )
+    attended = after(attended, first_tokens, *([late, down_sum] if own_slice else []))
+    heads_parts = outer_product(tokens, [gq, attended], [normed_attn, g_branch], (0, 3), 4)
+    first_tokens = exchange(after(first_tokens, late))
+    gk = after(gk, heads_parts, first_tokens)
+    heads_parts = outer_product(tokens, [gk, gv], [normed_attn] * 2, (1, 2), 4, heads_parts)
+    other_tokens = exchange(after(other_tokens, first_tokens))
+    token_gradient = jnp.concatenate([first_tokens, other_tokens], axis=1)
 
     gain_parts = jnp.stack([jnp.sum(gain_part_attn, axis=0), jnp.sum(gain_part_ffn, axis=0)])
     if own_slice:
-        token_gradient = exchange(after(grad_slots, down_sum))
-        up_sum = exchange(after(up_own, token_gradient))
+        up_sum = exchange(after(up_own, other_tokens))
         gain_grads = sum_gains(gain_parts)
         heads_sum = exchange(after(reduce_groups(heads_parts), up_sum, gain_grads))
         ff = w_act.shape[1]
@@ -858,7 +910,6 @@
             value = lax.psum_scatter(value, second, scatter_dimension=1, tiled=True)
             return lax.psum(value, "dp").astype(F32)
 
-        token_gradient = exchange(grad_slots)
         (down_whole,) = whole_of(down_parts, 1)
         act_whole, gate_whole = whole_of(up_parts, 2)
         query_whole, key_whole, value_whole, out_whole = whole_of(heads_parts, 4)

time: 532 us -> 521 us (0.979)
  blocking collectives: 134 us -> 121 us
  Pallas kernels: 211 us -> 203 us
    all_to_all x3, blocking collectives: 134 us -> 121 us  [exchange(): return lax.all_to_all(value, 'row', 0, 0)]
    pallas_call x6, Pallas kernels: 106 us -> 97.9 us  [the longest x4 53.5 us: outer_product(): pl.pallas_call(functools.partial(outer_kernel, count, tokens), grid=(GROU...]
    ppermute x2, waiting for transfers between devices: 0.01 us -> 6.92 us  [shift(): lax.ppermute(value, ('row', 'col'), [(place_of[i], place_of[j]) for i, j...]
    all_to_all x6 -> x7, waiting for transfers between devices: 65.7 us -> 60.1 us  [exchange(): return lax.all_to_all(value, 'row', 0, 0)]
    all_to_all x6 -> x7, starting transfers between devices: 26.8 us -> 31 us  [exchange(): return lax.all_to_all(value, 'row', 0, 0)]
  transfers between devices with their start and end apart: 21 -> 22, of which waited for: 9 -> 10; matrix products, arithmetic and copies ran while one was open for 4% -> 5% of each run, Pallas kernels for 38% -> 37%
where the time goes in v4:
time: 521 us; the launch traced here: 516 us
  Pallas kernels  203 us (39%)
  blocking collectives  121 us (23%)
  waiting for transfers between devices  90.9 us (17%)
  starting transfers between devices  49.4 us (9%)
  other arithmetic  23.5 us (5%)
  between operations  14.7 us (3%)
  local copies, waits for them, and re-layouts  13.9 us (3%)
    all_to_all x3, blocking collectives, exchange(): return lax.all_to_all(value, 'row', 0, 0)  121 us
    all_to_all x7, waiting for transfers between devices, exchange(): return lax.all_to_all(value, 'row', 0, 0)  60.1 us
    pallas_call x4, Pallas kernels, outer_product(): pl.pallas_call(functools.partial(outer_kernel, count, tokens), grid=(GROU...  53.5 us
    pallas_call x1, Pallas kernels, feed_back(): call(feed_back_kernel, (GROUPS + tokens // TILE,), [resident(cots.shape)]...  36.3 us
    all_to_all x7, starting transfers between devices, exchange(): return lax.all_to_all(value, 'row', 0, 0)  31 us
    pallas_call x1, Pallas kernels, feed(): call(feed_kernel, (GROUPS + tokens // TILE,), [resident((tokens, WIDTH)),...  30.2 us
    pallas_call x1, Pallas kernels, attend_back(): call(attend_back_kernel, (blocks + 1,), pairs(WIDTH) * 3 + pairs(LANES) *...  23.5 us
    pallas_call x1, Pallas kernels, attend(): call(attend_kernel, (blocks,), pair_of((QUERY, WIDTH)) * 3 + pair_of((SLO...  20.9 us
  transfers between devices with their start and end apart: 22, of which 10 were waited for; matrix products, arithmetic and copies ran while one was open for 5% of the time, Pallas kernels for 37%

profile of v4, /device:TPU:0, one launch (start us, length us, event | category | flops | bytes accessed | tf_op | source)
XLA Modules:
  0.0 516.1 jit_solution(655215917132038493)
XLA Ops:
  13.6 33.7 %all_to_all.50 = bf16[4,1104,128]{2,1,0:T(8,128)(2,1)S(1)} all-to-all(bf16[4,1104,128]{2,1,0:T(8,128)(2,1)S(1)} %broadcast_in_dim.41), channel_id=1, replica_groups=mesh['dp'=2,'row'=4,'col'=4] {'row'}, dimensions={0} | all-to-all | bytes 2260992 | tf_op jit(solution)/shard_map/all_to_all | solution.py:657
  49.9 49.3 %all_to_all.51 = bf16[4,1968,128]{2,1,0:T(8,128)(2,1)} all-to-all(bf16[4,1968,128]{2,1,0:T(8,128)(2,1)S(1)} %broadcast_in_dim.42), channel_id=1, replica_groups=mesh['dp'=2,'row'=4,'col'=4] {'row'}, dimensions={0} | all-to-all | bytes 4030464 | tf_op jit(solution)/shard_map/all_to_all | solution.py:657
  110.9 46.7 %all-to-all-done.2.xs.refs_6_.refs_7_.refs_0_ = bf16[4,1152,256]{2,1,0:T(8,128)(2,1)S(1)} async-done(((bf16[4,1152,256]{2,1,0:T(8,128)(2,1)}), bf16[4,1152,256]{2,1,0:T(8,128)(2,1)S(1)}, u32[]{:S(2)}, u32[]{:S(2)}) %all-to-all-start.2) | async-done | bytes 2359328 | tf_op jit(solution)/shard_map/all_to_all | solution.py:657
  157.6 4.5 all-to-all-start.3
  163.6 13.9 %project.1 = (bf16[1152,1024]{1,0:T(8,128)(2,1)}, bf16[1152,1024]{1,0:T(8,128)(2,1)}, bf16[1152,1024]{1,0:T(8,128)(2,1)}, bf16[1152,1024]{1,0:T(8,128)(2,1)}) custom-call(bf16[4,1152,256]{2,1,0:T(8,128)(2,1)} %copy-done.2, f32[1,1024]{1,0:T(1,128)} %bitcast.96, f32[1152,128]{1,0:T(8,128)} %get-tuple-element.128.cosine.refs_6_.refs_7_.refs_5_, ...), custom_call_target="tpu_custom_call" | custom-call | flops 7247757312 | bytes 18087936 | tf_op jit(solution)/shard_map/project/pallas_call | solution.py:164
  177.5 20.9 %attend.1 = (bf16[1024,1024]{1,0:T(8,128)(2,1)}, bf16[8,4,512,256]{3,2,1,0:T(8,128)(2,1)}, bf16[1024,1024]{1,0:T(8,128)(2,1)}, bf16[1024,1024]{1,0:T(8,128)(2,1)}) custom-call(bf16[1152,1024]{1,0:T(8,128)(2,1)} %get-tuple-element.62.refs_0_.refs_1_, bf16[1152,1024]{1,0:T(8,128)(2,1)} %get-tuple-element.62.refs_0_.refs_1_, ...), custom_call_target="tpu_custom_call" | custom-call | flops 6442450944 | bytes 23068672 | tf_op jit(solution)/shard_map/attend/pallas_call | solution.py:256
  198.4 30.2 %feed.1 = (bf16[4,1024,656]{2,1,0:T(8,128)(2,1)}, bf16[4,1024,656]{2,1,0:T(8,128)(2,1)}, bf16[4,1024,656]{2,1,0:T(8,128)(2,1)}, bf16[4,768,256]{2,1,0:T(8,128)(2,1)}, bf16[4,256,256]{2,1,0:T(8,128)(2,1)}) custom-call(bf16[1024,1024]{1,0:T(8,128)(2,1)} %get-tuple-element.65.refs_0_.refs_2_.refs_3_, bf16[1024,1024]{1,0:T(8,128)(2,1)} %get-tuple-element.66.refs_1_.refs_3_, ...), custom_call_target="tpu_custom_call" | custom-call | flops 16508780544 | bytes 38535168 | tf_op jit(solution)/shard_map/feed/pallas_call | solution.py:470
  228.7 9.9 %outer_product.4 = bf16[2,4,4,656,128]{4,3,2,1,0:T(8,128)(2,1)} custom-call(bf16[4,1024,656]{2,1,0:T(8,128)(2,1)} %get-tuple-element.72.refs_0_, bf16[4,1024,256]{2,1,0:T(8,128)(2,1)} %all-to-all-done.3.refs_1_.refs_0_), custom_call_target="tpu_custom_call" | custom-call | flops 5502926848 | bytes 12845056 | tf_op jit(solution)/shard_map/outer_product/pallas_call | solution.py:620
  238.6 5.2 %all-to-all-start.4 = ((bf16[4,768,256]{2,1,0:T(8,128)(2,1)}), bf16[4,768,256]{2,1,0:T(8,128)(2,1)S(1)}, u32[]{:S(2)}, u32[]{:S(2)}) async-start(bf16[4,768,256]{2,1,0:T(8,128)(2,1)} %get-tuple-element.69), calls=%async_computation.4 | async-start | bytes 3145728 | tf_op jit(solution)/shard_map/all_to_all | solution.py:657
  243.8 36.3 %feed_back.1 = (bf16[4,1024,656]{2,1,0:T(8,128)(2,1)}, bf16[4,1024,656]{2,1,0:T(8,128)(2,1)}, bf16[1024,1024]{1,0:T(8,128)(2,1)}, bf16[1024,1024]{1,0:T(8,128)(2,1)}, f32[8,1024]{1,0:T(8,128)}) custom-call(bf16[4,1024,256]{2,1,0:T(8,128)(2,1)} %all-to-all-done.3.refs_1_.refs_0_, bf16[4,1024,656]{2,1,0:T(8,128)(2,1)} %get-tuple-element.74.refs_1_, ...), custom_call_target="tpu_custom_call" | custom-call | flops 18656264192 | bytes 40632320 | tf_op jit(solution)/shard_map/feed_back/pallas_call | solution.py:523
  280.1 20.0 %outer_product.5 = bf16[2,4,4,1312,128]{4,3,2,1,0:T(8,128)(2,1)} custom-call(bf16[4,1024,656]{2,1,0:T(8,128)(2,1)} %get-tuple-element.78.refs_0_, bf16[4,1024,656]{2,1,0:T(8,128)(2,1)} %get-tuple-element.79.refs_1_, bf16[1024,1024]{1,0:T(8,128)(2,1)} %get-tuple-element.65.refs_0_.refs_2_.refs_3_, bf16[1024,1024]{1,0:T(8,128)(2,1)} %get-tuple-element.65.refs_0_.refs_2_.refs_3_), custom_call_target="tpu_custom_call" | custom-call | flops 11005853696 | bytes 23592960 | tf_op jit(solution)/shard_map/outer_product/pallas_call | solution.py:620
  302.7 5.6 %all-to-all-start.5 = ((bf16[4,584,256]{2,1,0:T(8,128)(2,1)}), bf16[4,584,256]{2,1,0:T(8,128)(2,1)S(1)}, u32[]{:S(2)}, u32[]{:S(2)}) async-start(bf16[4,584,256]{2,1,0:T(8,128)(2,1)} %pad_maximum_fusion.3), calls=%async_computation.6 | async-start | bytes 2392064 | tf_op jit(solution)/shard_map/all_to_all | solution.py:657
  308.3 23.5 %attend_back.1 = (bf16[1024,1024]{1,0:T(8,128)(2,1)}, bf16[1152,1024]{1,0:T(8,128)(2,1)}, bf16[1152,1024]{1,0:T(8,128)(2,1)}, bf16[64,2048]{1,0:T(8,128)(2,1)}, ...) custom-call(bf16[1152,1024]{1,0:T(8,128)(2,1)} %get-tuple-element.62.refs_0_.refs_1_, ...), custom_call_target="tpu_custom_call" | custom-call | flops 8589934592 | bytes 23068672 | tf_op jit(solution)/shard_map/attend_back/pallas_call | solution.py:363
  339.9 4.3 collective-permute-done.1.refs_4_
  347.1 16.4 %unproject.1 = (bf16[4,256,256]{2,1,0:T(8,128)(2,1)}, bf16[4,768,256]{2,1,0:T(8,128)(2,1)}, f32[8,1024]{1,0:T(8,128)}) custom-call(bf16[4,1152,256]{2,1,0:T(8,128)(2,1)} %copy-done.2, bf16[1024,1024]{1,0:T(8,128)(2,1)} %get-tuple-element.82.refs_1_.refs_0_, bf16[1152,1024]{1,0:T(8,128)(2,1)} %get-tuple-element.98.refs_2_.refs_0_, ...), custom_call_target="tpu_custom_call" | custom-call | flops 6442450944 | bytes 18874368 | tf_op jit(solution)/shard_map/unproject/pallas_call | solution.py:562
  364.4 4.2 all-to-all-start.6
  368.7 11.6 %outer_product.6.refs_4_ = bf16[2,4,4,1024,128]{4,3,2,1,0:T(8,128)(2,1)} custom-call(bf16[1024,1024]{1,0:T(8,128)(2,1)} %get-tuple-element.82.refs_1_.refs_0_, bf16[1024,1024]{1,0:T(8,128)(2,1)} %get-tuple-element.96.refs_1_, bf16[1152,1024]{1,0:T(8,128)(2,1)} %get-tuple-element.97.refs_2_.refs_3_, bf16[1024,1024]{1,0:T(8,128)(2,1)} %get-tuple-element.90.refs_4_.refs_3_), custom_call_target="tpu_custom_call" | custom-call | flops 4294967296 | bytes 10485760 | tf_op jit(solution)/shard_map/outer_product/pallas_call | solution.py:620
  380.3 12.0 %outer_product.7 = bf16[2,4,4,1024,128]{4,3,2,1,0:T(8,128)(2,1)} custom-call(bf16[1152,1024]{1,0:T(8,128)(2,1)} %get-tuple-element.98.refs_2_.refs_0_, bf16[1152,1024]{1,0:T(8,128)(2,1)} %get-tuple-element.89.refs_3_.refs_1_, bf16[1152,1024]{1,0:T(8,128)(2,1)} %get-tuple-element.97.refs_2_.refs_3_, ...), custom_call_target="tpu_custom_call", output_to_operand_aliasing={{}: (4, {})} | custom-call | flops 4294967296 | bytes 10485760 | tf_op jit(solution)/shard_map/outer_product/pallas_call | solution.py:620
  393.6 37.6 %all_to_all.52 = bf16[4,768,256]{2,1,0:T(8,128)(2,1)} all-to-all(bf16[4,768,256]{2,1,0:T(8,128)(2,1)S(1)} %copy-done.7), channel_id=1, replica_groups=mesh['dp'=2,'row'=4,'col'=4] {'row'}, dimensions={0} | all-to-all | bytes 3145728 | tf_op jit(solution)/shard_map/all_to_all | solution.py:657
  445.8 8.6 %collective-permute-done.5 = f32[2,1024]{1,0:T(2,128)S(1)} collective-permute-done((f32[2,1024]{1,0:T(2,128)S(1)}, f32[2,1024]{1,0:T(2,128)S(1)}, u32[]{:S(2)}, u32[]{:S(2)}) %collective-permute-start.5) | collective-permute-done | bytes 8224 | tf_op jit(solution)/shard_map/ppermute | solution.py:716
  454.4 4.6 collective-permute-start.6
  459.1 5.8 %collective-permute-done.6 = f32[2,1024]{1,0:T(2,128)S(1)} collective-permute-done((f32[2,1024]{1,0:T(2,128)S(1)}, f32[2,1024]{1,0:T(2,128)S(1)}, u32[]{:S(2)}, u32[]{:S(2)}) %collective-permute-start.6) | collective-permute-done | bytes 8224 | tf_op jit(solution)/shard_map/ppermute | solution.py:716
  468.2 4.2 all-to-all-start.9
  484.1 13.4 %all-to-all-done.9 = bf16[4,1024,128]{2,1,0:T(8,128)(2,1)} async-done(((bf16[4,1024,128]{2,1,0:T(8,128)(2,1)}), bf16[4,1024,128]{2,1,0:T(8,128)(2,1)}, u32[]{:S(2)}, u32[]{:S(2)}) %all-to-all-start.9) | async-done | bytes 1048608 | tf_op jit(solution)/shard_map/all_to_all | solution.py:657
  (143 shorter events, 79.0 us)
Async XLA Ops:
  7.2 42.3 %copy-start = (bf16[656,256]{1,0:T(8,128)(2,1)S(1)}, bf16[656,256]{1,0:T(8,128)(2,1)}, u32[]{:S(2)}) copy-start(bf16[656,256]{1,0:T(8,128)(2,1)} %param.20) | copy-start | bytes 1007620
  7.2 156.4 %all-gather.5.cloned.1.call-start = ((), (), s32[]{:S(2)}) async-start(), calls=%async_computation.16 | async-start | bytes 9437184 | tf_op jit(solution)/shard_map/all_gather | solution.py:673
  49.4 149.0 %all-gather.7.cloned.1.call-start = ((), (), s32[]{:S(2)}) async-start(), calls=%async_computation.17 | async-start | bytes 18137088 | tf_op jit(solution)/shard_map/all_gather | solution.py:673
  49.9 49.3 %copy-start.4 = (bf16[4096,256]{1,0:T(8,128)(2,1)S(1)}, bf16[4096,256]{1,0:T(8,128)(2,1)}, u32[]{:S(2)}) copy-start(bf16[4096,256]{1,0:T(8,128)(2,1)} %param.13) | copy-start | bytes 6291460
  101.1 56.5 %all-to-all-start.2 = ((bf16[4,1152,256]{2,1,0:T(8,128)(2,1)}), bf16[4,1152,256]{2,1,0:T(8,128)(2,1)S(1)}, u32[]{:S(2)}, u32[]{:S(2)}) async-start(bf16[4,1152,256]{2,1,0:T(8,128)(2,1)} %pad_maximum_fusion), calls=%async_computation.2 | async-start | bytes 4718592 | tf_op jit(solution)/shard_map/all_to_all | solution.py:657
  157.6 71.0 %all-to-all-start.3 = ((bf16[4,1024,256]{2,1,0:T(8,128)(2,1)}), bf16[4,1024,256]{2,1,0:T(8,128)(2,1)}, u32[]{:S(2)}, u32[]{:S(2)}) async-start(bf16[4,1024,256]{2,1,0:T(8,128)(2,1)} %bitcast.76), calls=%async_computation.3 | async-start | bytes 4194304 | tf_op jit(solution)/shard_map/all_to_all | solution.py:657
  162.1 138.1 %reduce-scatter.4.cloned.1.call-start = ((), (), s32[]{:S(2)}) async-start(), calls=%async_computation.13 | async-start | bytes 6045696 | tf_op jit(solution)/shard_map/reduce_scatter | solution.py:678
  238.6 41.5 %all-to-all-start.4 = ((bf16[4,768,256]{2,1,0:T(8,128)(2,1)}), bf16[4,768,256]{2,1,0:T(8,128)(2,1)S(1)}, u32[]{:S(2)}, u32[]{:S(2)}) async-start(bf16[4,768,256]{2,1,0:T(8,128)(2,1)} %get-tuple-element.69), calls=%async_computation.4 | async-start | bytes 3145728 | tf_op jit(solution)/shard_map/all_to_all | solution.py:657
  243.8 187.4 %reduce-scatter.8.cloned.1.call-start = ((), (), s32[]{:S(2)}) async-start(), calls=%async_computation.15 | async-start | bytes 12091392 | tf_op jit(solution)/shard_map/reduce_scatter | solution.py:678
  302.7 60.8 %all-to-all-start.5 = ((bf16[4,584,256]{2,1,0:T(8,128)(2,1)}), bf16[4,584,256]{2,1,0:T(8,128)(2,1)S(1)}, u32[]{:S(2)}, u32[]{:S(2)}) async-start(bf16[4,584,256]{2,1,0:T(8,128)(2,1)} %pad_maximum_fusion.3), calls=%async_computation.6 | async-start | bytes 2392064 | tf_op jit(solution)/shard_map/all_to_all | solution.py:657
  331.8 8.1 %collective-permute-start = (bf16[64,2048]{1,0:T(8,128)(2,1)}, bf16[64,2048]{1,0:T(8,128)(2,1)S(1)}, u32[]{:S(2)}, u32[]{:S(2)}) collective-permute-start(bf16[64,2048]{1,0:T(8,128)(2,1)} %get-tuple-element.86), channel_id=1, source_target_pairs={{0,4},{4,8},{8,12},{1,5},{5,9},{9,13},{2,6},{6,10},{10,14},{3,7},{... | collective-permute-start | bytes 786440 | tf_op jit(solution)/shard_map/ppermute | solution.py:795
  335.8 8.5 %collective-permute-start.1 = (bf16[64,2048]{1,0:T(8,128)(2,1)}, bf16[64,2048]{1,0:T(8,128)(2,1)S(1)}, u32[]{:S(2)}, u32[]{:S(2)}) collective-permute-start(bf16[64,2048]{1,0:T(8,128)(2,1)} %get-tuple-element.87), channel_id=1, source_target_pairs={{4,0},{8,4},{12,8},{5,1},{9,5},{13,9},{6,2},{10,6},{14,10},{7,3},{... | collective-permute-start | bytes 786440 | tf_op jit(solution)/shard_map/ppermute | solution.py:795
  364.4 15.8 %all-to-all-start.6 = ((bf16[4,256,256]{2,1,0:T(8,128)(2,1)}), bf16[4,256,256]{2,1,0:T(8,128)(2,1)}, u32[]{:S(2)}, u32[]{:S(2)}) async-start(bf16[4,256,256]{2,1,0:T(8,128)(2,1)} %get-tuple-element.92), calls=%async_computation.7 | async-start | bytes 1048576 | tf_op jit(solution)/shard_map/all_to_all | solution.py:657
  368.6 99.6 %reduce-scatter.6.cloned.1.call-start = ((), (), s32[]{:S(2)}) async-start(), calls=%async_computation.14 | async-start | bytes 9437184 | tf_op jit(solution)/shard_map/reduce_scatter | solution.py:678
  431.2 37.0 %all-to-all-start.8 = ((bf16[4,1312,128]{2,1,0:T(8,128)(2,1)}), bf16[4,1312,128]{2,1,0:T(8,128)(2,1)S(1)}, u32[]{:S(2)}, u32[]{:S(2)}) async-start(bf16[4,1312,128]{2,1,0:T(8,128)(2,1)} %bitcast.78), calls=%async_computation.11 | async-start | bytes 2686976 | tf_op jit(solution)/shard_map/all_to_all | solution.py:657
  434.8 3.9 collective-permute-start.2
  438.7 3.9 collective-permute-start.3
  442.6 1.2 collective-permute-start.4
  443.8 10.6 %collective-permute-start.5 = (f32[2,1024]{1,0:T(2,128)S(1)}, f32[2,1024]{1,0:T(2,128)S(1)}, u32[]{:S(2)}, u32[]{:S(2)}) collective-permute-start(f32[2,1024]{1,0:T(2,128)S(1)} %add.87), channel_id=1, source_target_pairs={{0,4},{4,0},{8,12},{12,8},{1,5},{5,1},{9,13},{13,9},{2,6},{6,2},{1... | collective-permute-start | bytes 24584 | tf_op jit(solution)/shard_map/ppermute | solution.py:716
  454.4 10.4 %collective-permute-start.6 = (f32[2,1024]{1,0:T(2,128)S(1)}, f32[2,1024]{1,0:T(2,128)S(1)}, u32[]{:S(2)}, u32[]{:S(2)}) collective-permute-start(f32[2,1024]{1,0:T(2,128)S(1)} %add.88), channel_id=1, source_target_pairs={{0,8},{4,12},{8,0},{12,4},{1,9},{5,13},{9,1},{13,5},{2,10},{6,14},... | collective-permute-start | bytes 24584 | tf_op jit(solution)/shard_map/ppermute | solution.py:716
  466.1 8.9 %collective-permute-start.9 = (bf16[656,128]{1,0:T(8,128)(2,1)S(1)}, bf16[656,128]{1,0:T(8,128)(2,1)S(1)}, u32[]{:S(2)}, u32[]{:S(2)}) collective-permute-start(bf16[656,128]{1,0:T(8,128)(2,1)S(1)} %reduce_sum.81), channel_id=1, source_target_pairs={{0,16},{16,0},{1,17},{17,1},{2,18},{18,2},{3,19},{19,3},{4,20},{20... | collective-permute-start | bytes 503816 | tf_op jit(solution)/shard_map/ppermute | solution.py:645
  468.2 29.2 %all-to-all-start.9 = ((bf16[4,1024,128]{2,1,0:T(8,128)(2,1)}), bf16[4,1024,128]{2,1,0:T(8,128)(2,1)}, u32[]{:S(2)}, u32[]{:S(2)}) async-start(bf16[4,1024,128]{2,1,0:T(8,128)(2,1)} %bitcast.79), calls=%async_computation.12 | async-start | bytes 2097152 | tf_op jit(solution)/shard_map/all_to_all | solution.py:657
  481.0 18.6 %collective-permute-start.8 = (bf16[1312,128]{1,0:T(8,128)(2,1)S(1)}, bf16[1312,128]{1,0:T(8,128)(2,1)S(1)}, u32[]{:S(2)}, u32[]{:S(2)}) collective-permute-start(bf16[1312,128]{1,0:T(8,128)(2,1)S(1)} %reduce_sum.79), channel_id=1, source_target_pairs={{0,16},{16,0},{1,17},{17,1},{2,18},{18,2},{3,19},{19,3},{4,20},{20... | collective-permute-start | bytes 1007624 | tf_op jit(solution)/shard_map/ppermute | solution.py:645
  498.9 7.3 %collective-permute-start.7 = (bf16[1024,128]{1,0:T(8,128)(2,1)S(1)}, bf16[1024,128]{1,0:T(8,128)(2,1)S(1)}, u32[]{:S(2)}, u32[]{:S(2)}) collective-permute-start(bf16[1024,128]{1,0:T(8,128)(2,1)S(1)} %reduce_sum.78), channel_id=1, source_target_pairs={{0,16},{16,0},{1,17},{17,1},{2,18},{18,2},{3,19},{19,3},{4,20},{20... | collective-permute-start | bytes 786440 | tf_op jit(solution)/shard_map/ppermute | solution.py:645
  (14 other events, 224.0 us)
Sparse Core Ops, SparseCore 0:
  49.6 53.4 all-gather.4
  105.0 87.0 all-gather.6
  238.7 58.8 reduce-scatter.3
  301.0 84.3 reduce-scatter.7
  392.4 73.0 reduce-scatter.5

commit v5 on v4

--- a/solution.py
+++ b/solution.py
@@ -540,7 +540,7 @@
 
 
 def unproject_kernel(*refs):
-    xs, gq, gk, gv, g_branch, gain, low, high, early, late, gain_part, held, total = refs
+    xs, gq, gk, gv, g_branch, gain, low, high, outs, gain_part, held, total = refs
     @pl.when(pl.program_id(0) < GROUPS)
     def _():
         own = pl.ds(REACH, gq.shape[0])
@@ -553,8 +553,7 @@
         unit, inverse = norm(whole_rows(xs, between_rows()).astype(F32))
         add_gain(gain_part, gradient * unit)
         made = g_branch[...].astype(F32) + norm_back(gradient, unit, inverse, gain[...])
-        pl.when(pl.program_id(0) == GROUPS)(lambda: put_rows(early, made))
-        pl.when(pl.program_id(0) > GROUPS)(lambda: put_rows(late, made))
+        put_rows(outs, made)
 
 
 def unproject(xs, gq, gk, gv, g_branch, gain, weight):
@@ -569,16 +568,8 @@
         ]
         + [later_rows(WIDTH), resident((1, WIDTH))]
         + weight_rows(3 * GROUP),
-        [
-            resident((SLOTS, TILE, 256)),
-            pl.BlockSpec((SLOTS, TILE, 256), lambda i: (0, jnp.maximum(i - GROUPS - 1, 0), 0)),
-            resident((8, WIDTH)),
-        ],
-        [
-            struct((SLOTS, TILE, 256), BF16),
-            struct((SLOTS, tokens - TILE, 256), BF16),
-            struct((8, WIDTH), F32),
-        ],
+        [LATER_BLOCKS, resident((8, WIDTH))],
+        [struct((SLOTS, tokens, 256), BF16), struct((8, WIDTH), F32)],
         [pltpu.VMEM((1, tokens, 3 * GROUP), BF16), pltpu.VMEM((tokens, WIDTH), F32)],
         2 * tokens * WIDTH * 3 * WIDTH,
         12 * tokens * WIDTH + 6 * WIDTH * WIDTH,
@@ -596,10 +587,13 @@
         left = left[0] if len(left.shape) == 3 else own_rows(left)
         right = whole_rows(right) if len(right.shape) == 3 else own_rows(right)
         made = tn(left, right)
-        for a in range(2):
-            for o in range(SLOTS):
-                at = o * 256 + a * LANES
-                out[a, 0, o] = made[:, at : at + LANES].astype(BF16)
+        many, width = out.shape[1], out.shape[3]
+        for j in range(many):
+            rows = slice(j * width, (j + 1) * width)
+            for a in range(2):
+                for o in range(SLOTS):
+                    at = o * 256 + a * LANES
+                    out[a, j, o] = made[rows, at : at + LANES].astype(BF16)
 
     for t in range(count):
         pl.when(pl.program_id(0) % count == t)(functools.partial(make, inner[t], outer[t]))
@@ -609,22 +603,23 @@
     count = len(inner)
     width = inner[0].shape[2] if inner[0].ndim == 3 else GROUP
     stride = places[-1] - places[0]
+    many = 1 if inner[0].ndim == 3 else 2
 
     def inner_block(value):
         if value.ndim == 3:
             return pl.BlockSpec((1, tokens, width), lambda i: (i // count, 0, 0))
-        return pl.BlockSpec((value.shape[0], GROUP), lambda i: (0, i // count))
+        return pl.BlockSpec((value.shape[0], many * GROUP), lambda i: (0, i // count))
 
     more = [] if base is None else [base]
     moved = 8 * count * width * (tokens + WIDTH) + 2 * tokens * WIDTH
     return pl.pallas_call(
         functools.partial(outer_kernel, count, tokens),
-        grid=(GROUPS * count,),
+        grid=(GROUPS // many * count,),
         in_specs=[inner_block(value) for value in inner]
         + [resident(value.shape) for value in outer]
         + [pl.BlockSpec(memory_space=pl.ANY) for _ in more],
         out_specs=pl.BlockSpec(
-            (2, 1, SLOTS, width, LANES),
+            (2, many, SLOTS, width, LANES),
             lambda i: (0, i // count, 0, places[0] + i % count * stride, 0),
         ),
         out_shape=struct((2, GROUPS, SLOTS, kinds * width, LANES), BF16),
@@ -878,21 +873,22 @@
     else:
         late = exchange(late)
     layer_out = jnp.concatenate([early, late], axis=1)
+    heads_parts = outer_product(tokens, [gq, attended], [normed_attn, g_branch], (0, 3), 4)
+    from_low = after(from_low, heads_parts)
+    if own_slice:
+        from_low = after(from_low, late, down_sum)
     gk, gv = add_edges(gk, gv, edges, from_low, from_high, cosine, sine)
-    first_tokens, other_tokens, gain_part_attn = unproject(
+    grad_slots, gain_part_attn = unproject(
         xs, gq, gk, gv, g_branch, gain_rows[0], heads_w
     )
-    attended = after(attended, first_tokens, *([late, down_sum] if own_slice else []))
-    heads_parts = outer_product(tokens, [gq, attended], [normed_attn, g_branch], (0, 3), 4)
-    first_tokens = exchange(after(first_tokens, late))
-    gk = after(gk, heads_parts, first_tokens)
-    heads_parts = outer_product(tokens, [gk, gv], [normed_attn] * 2, (1, 2), 4, heads_parts)
-    other_tokens = exchange(after(other_tokens, first_tokens))
-    token_gradient = jnp.concatenate([first_tokens, other_tokens], axis=1)
+    heads_parts = outer_product(
+        tokens, [after(gk, grad_slots), gv], [normed_attn] * 2, (1, 2), 4, heads_parts
+    )
+    token_gradient = exchange(after(grad_slots, late))
 
     gain_parts = jnp.stack([jnp.sum(gain_part_attn, axis=0), jnp.sum(gain_part_ffn, axis=0)])
     if own_slice:
-        up_sum = exchange(after(up_own, other_tokens))
+        up_sum = exchange(after(up_own, token_gradient))
         gain_grads = sum_gains(gain_parts)
         heads_sum = exchange(after(reduce_groups(heads_parts), up_sum, gain_grads))
         ff = w_act.shape[1]

time: 521 us -> 517 us (level)
  blocking collectives: 121 us -> 133 us
  waiting for transfers between devices: 90.9 us -> 82.5 us
    all_to_all x3, blocking collectives: 121 us -> 133 us  [exchange(): return lax.all_to_all(value, 'row', 0, 0)]
    ppermute x2, waiting for transfers between devices: 6.92 us -> 0.01 us  [shift(): lax.ppermute(value, ('row', 'col'), [(place_of[i], place_of[j]) for i, j...]
    all_to_all x7 -> x6, starting transfers between devices: 31 us -> 27.9 us  [exchange(): return lax.all_to_all(value, 'row', 0, 0)]
    all_to_all x7 -> x6, waiting for transfers between devices: 60.1 us -> 61.2 us  [exchange(): return lax.all_to_all(value, 'row', 0, 0)]
  transfers between devices with their start and end apart: 22 -> 21, of which waited for: 10 -> 8; matrix products, arithmetic and copies ran while one was open for 5% -> 5% of each run, Pallas kernels for 37% -> 37%
where the time goes in v5:
time: 517 us; the launch traced here: 512 us
  Pallas kernels  200 us (39%)
  blocking collectives  133 us (26%)
  waiting for transfers between devices  82.5 us (16%)
  starting transfers between devices  47.1 us (9%)
  other arithmetic  22.3 us (4%)
  between operations  14.7 us (3%)
  local copies, waits for them, and re-layouts  11.6 us (2%)
    all_to_all x3, blocking collectives, exchange(): return lax.all_to_all(value, 'row', 0, 0)  133 us
    all_to_all x6, waiting for transfers between devices, exchange(): return lax.all_to_all(value, 'row', 0, 0)  61.2 us
    pallas_call x4, Pallas kernels, outer_product(): pl.pallas_call(functools.partial(outer_kernel, count, tokens), grid=(GROU...  51.5 us
    pallas_call x1, Pallas kernels, feed_back(): call(feed_back_kernel, (GROUPS + tokens // TILE,), [resident(cots.shape)]...  36.3 us
    pallas_call x1, Pallas kernels, feed(): call(feed_kernel, (GROUPS + tokens // TILE,), [resident((tokens, WIDTH)),...  30.2 us
    all_to_all x6, starting transfers between devices, exchange(): return lax.all_to_all(value, 'row', 0, 0)  27.9 us
    pallas_call x1, Pallas kernels, attend_back(): call(attend_back_kernel, (blocks + 1,), pairs(WIDTH) * 3 + pairs(LANES) *...  23.5 us
    pallas_call x1, Pallas kernels, attend(): call(attend_kernel, (blocks,), pair_of((QUERY, WIDTH)) * 3 + pair_of((SLO...  20.9 us
  transfers between devices with their start and end apart: 21, of which 8 were waited for; matrix products, arithmetic and copies ran while one was open for 5% of the time, Pallas kernels for 37%

profile of v5, /device:TPU:0, one launch (start us, length us, event | category | flops | bytes accessed | tf_op | source)
XLA Modules:
  0.0 511.9 jit_solution(11494285241250135942)
XLA Ops:
  13.6 33.7 %all_to_all.45 = bf16[4,1104,128]{2,1,0:T(8,128)(2,1)S(1)} all-to-all(bf16[4,1104,128]{2,1,0:T(8,128)(2,1)S(1)} %broadcast_in_dim.41), channel_id=1, replica_groups=mesh['dp'=2,'row'=4,'col'=4] {'row'}, dimensions={0} | all-to-all | bytes 2260992 | tf_op jit(solution)/shard_map/all_to_all | solution.py:652
  49.8 49.3 %all_to_all.46 = bf16[4,1968,128]{2,1,0:T(8,128)(2,1)} all-to-all(bf16[4,1968,128]{2,1,0:T(8,128)(2,1)S(1)} %broadcast_in_dim.42), channel_id=1, replica_groups=mesh['dp'=2,'row'=4,'col'=4] {'row'}, dimensions={0} | all-to-all | bytes 4030464 | tf_op jit(solution)/shard_map/all_to_all | solution.py:652
  101.0 3.8 all-to-all-start.2
  110.8 46.7 %all-to-all-done.2.xs.refs_6_.refs_7_.refs_0_ = bf16[4,1152,256]{2,1,0:T(8,128)(2,1)S(1)} async-done(((bf16[4,1152,256]{2,1,0:T(8,128)(2,1)}), bf16[4,1152,256]{2,1,0:T(8,128)(2,1)S(1)}, u32[]{:S(2)}, u32[]{:S(2)}) %all-to-all-start.2) | async-done | bytes 2359328 | tf_op jit(solution)/shard_map/all_to_all | solution.py:652
  157.5 4.5 all-to-all-start.3
  163.5 13.9 %project.1 = (bf16[1152,1024]{1,0:T(8,128)(2,1)}, bf16[1152,1024]{1,0:T(8,128)(2,1)}, bf16[1152,1024]{1,0:T(8,128)(2,1)}, bf16[1152,1024]{1,0:T(8,128)(2,1)}) custom-call(bf16[4,1152,256]{2,1,0:T(8,128)(2,1)} %copy-done.2, f32[1,1024]{1,0:T(1,128)} %bitcast.96, f32[1152,128]{1,0:T(8,128)} %get-tuple-element.126.cosine.refs_6_.refs_7_.refs_5_, ...), custom_call_target="tpu_custom_call" | custom-call | flops 7247757312 | bytes 18087936 | tf_op jit(solution)/shard_map/project/pallas_call | solution.py:164
  177.5 20.9 %attend.1 = (bf16[1024,1024]{1,0:T(8,128)(2,1)}, bf16[8,4,512,256]{3,2,1,0:T(8,128)(2,1)}, bf16[1024,1024]{1,0:T(8,128)(2,1)}, bf16[1024,1024]{1,0:T(8,128)(2,1)}) custom-call(bf16[1152,1024]{1,0:T(8,128)(2,1)} %get-tuple-element.61.refs_0_.refs_1_, bf16[1152,1024]{1,0:T(8,128)(2,1)} %get-tuple-element.61.refs_0_.refs_1_, ...), custom_call_target="tpu_custom_call" | custom-call | flops 6442450944 | bytes 23068672 | tf_op jit(solution)/shard_map/attend/pallas_call | solution.py:256
  198.4 30.2 %feed.1 = (bf16[4,1024,656]{2,1,0:T(8,128)(2,1)}, bf16[4,1024,656]{2,1,0:T(8,128)(2,1)}, bf16[4,1024,656]{2,1,0:T(8,128)(2,1)}, bf16[4,768,256]{2,1,0:T(8,128)(2,1)}, bf16[4,256,256]{2,1,0:T(8,128)(2,1)}) custom-call(bf16[1024,1024]{1,0:T(8,128)(2,1)} %get-tuple-element.64.refs_0_.refs_2_.refs_3_, bf16[1024,1024]{1,0:T(8,128)(2,1)} %get-tuple-element.65.refs_1_.refs_3_, ...), custom_call_target="tpu_custom_call" | custom-call | flops 16508780544 | bytes 38535168 | tf_op jit(solution)/shard_map/feed/pallas_call | solution.py:470
  228.6 9.9 %outer_product.4 = bf16[2,4,4,656,128]{4,3,2,1,0:T(8,128)(2,1)} custom-call(bf16[4,1024,656]{2,1,0:T(8,128)(2,1)} %get-tuple-element.71.refs_0_, bf16[4,1024,256]{2,1,0:T(8,128)(2,1)} %all-to-all-done.3.refs_1_.refs_0_), custom_call_target="tpu_custom_call" | custom-call | flops 5502926848 | bytes 12845056 | tf_op jit(solution)/shard_map/outer_product/pallas_call | solution.py:615
  238.5 5.2 %all-to-all-start.4 = ((bf16[4,768,256]{2,1,0:T(8,128)(2,1)}), bf16[4,768,256]{2,1,0:T(8,128)(2,1)S(1)}, u32[]{:S(2)}, u32[]{:S(2)}) async-start(bf16[4,768,256]{2,1,0:T(8,128)(2,1)} %get-tuple-element.68), calls=%async_computation.4 | async-start | bytes 3145728 | tf_op jit(solution)/shard_map/all_to_all | solution.py:652
  243.8 36.3 %feed_back.1 = (bf16[4,1024,656]{2,1,0:T(8,128)(2,1)}, bf16[4,1024,656]{2,1,0:T(8,128)(2,1)}, bf16[1024,1024]{1,0:T(8,128)(2,1)}, bf16[1024,1024]{1,0:T(8,128)(2,1)}, f32[8,1024]{1,0:T(8,128)}) custom-call(bf16[4,1024,256]{2,1,0:T(8,128)(2,1)} %all-to-all-done.3.refs_1_.refs_0_, bf16[4,1024,656]{2,1,0:T(8,128)(2,1)} %get-tuple-element.73.refs_1_, ...), custom_call_target="tpu_custom_call" | custom-call | flops 18656264192 | bytes 40632320 | tf_op jit(solution)/shard_map/feed_back/pallas_call | solution.py:523
  280.1 21.1 %outer_product.5 = bf16[2,4,4,1312,128]{4,3,2,1,0:T(8,128)(2,1)} custom-call(bf16[4,1024,656]{2,1,0:T(8,128)(2,1)} %get-tuple-element.77.refs_0_, bf16[4,1024,656]{2,1,0:T(8,128)(2,1)} %get-tuple-element.78.refs_1_, bf16[1024,1024]{1,0:T(8,128)(2,1)} %get-tuple-element.64.refs_0_.refs_2_.refs_3_, bf16[1024,1024]{1,0:T(8,128)(2,1)} %get-tuple-element.64.refs_0_.refs_2_.refs_3_), custom_call_target="tpu_custom_call" | custom-call | flops 11005853696 | bytes 23592960 | tf_op jit(solution)/shard_map/outer_product/pallas_call | solution.py:615
  303.7 5.0 all-to-all-start.5
  308.7 23.5 %attend_back.1 = (bf16[1024,1024]{1,0:T(8,128)(2,1)}, bf16[1152,1024]{1,0:T(8,128)(2,1)}, bf16[1152,1024]{1,0:T(8,128)(2,1)}, bf16[64,2048]{1,0:T(8,128)(2,1)}, ...) custom-call(bf16[1152,1024]{1,0:T(8,128)(2,1)} %get-tuple-element.61.refs_0_.refs_1_, ...), custom_call_target="tpu_custom_call" | custom-call | flops 8589934592 | bytes 23068672 | tf_op jit(solution)/shard_map/attend_back/pallas_call | solution.py:363
  332.2 4.3 collective-permute-start
  338.0 10.4 %outer_product.6.refs_4_ = bf16[2,4,4,1024,128]{4,3,2,1,0:T(8,128)(2,1)} custom-call(bf16[1024,1024]{1,0:T(8,128)(2,1)} %get-tuple-element.81.refs_0_.refs_1_, bf16[1024,1024]{1,0:T(8,128)(2,1)} %get-tuple-element.86.refs_1_, bf16[1152,1024]{1,0:T(8,128)(2,1)} %get-tuple-element.87.refs_2_.refs_3_, bf16[1024,1024]{1,0:T(8,128)(2,1)} %get-tuple-element.88.refs_3_.refs_4_), custom_call_target="tpu_custom_call" | custom-call | flops 4294967296 | bytes 10485760 | tf_op jit(solution)/shard_map/outer_product/pallas_call | solution.py:615
  351.4 15.8 %unproject.1 = (bf16[4,1024,256]{2,1,0:T(8,128)(2,1)}, f32[8,1024]{1,0:T(8,128)}) custom-call(bf16[4,1152,256]{2,1,0:T(8,128)(2,1)} %copy-done.2, bf16[1024,1024]{1,0:T(8,128)(2,1)} %get-tuple-element.81.refs_0_.refs_1_, bf16[1152,1024]{1,0:T(8,128)(2,1)} %get-tuple-element.96.refs_2_.refs_0_, bf16[1152,1024]{1,0:T(8,128)(2,1)} %get-tuple-element.93.refs_3_.refs_1_, ...), custom_call_target="tpu_custom_call" | custom-call | flops 6442450944 | bytes 18874368 | tf_op jit(solution)/shard_map/unproject/pallas_call | solution.py:561
  367.3 10.1 %outer_product.7 = bf16[2,4,4,1024,128]{4,3,2,1,0:T(8,128)(2,1)} custom-call(bf16[1152,1024]{1,0:T(8,128)(2,1)} %get-tuple-element.96.refs_2_.refs_0_, bf16[1152,1024]{1,0:T(8,128)(2,1)} %get-tuple-element.93.refs_3_.refs_1_, bf16[1152,1024]{1,0:T(8,128)(2,1)} %get-tuple-element.87.refs_2_.refs_3_, ...), custom_call_target="tpu_custom_call", output_to_operand_aliasing={{}: (4, {})} | custom-call | flops 4294967296 | bytes 10485760 | tf_op jit(solution)/shard_map/outer_product/pallas_call | solution.py:615
  377.4 50.1 %all_to_all.47 = bf16[4,1024,256]{2,1,0:T(8,128)(2,1)S(1)} all-to-all(bf16[4,1024,256]{2,1,0:T(8,128)(2,1)} %get-tuple-element.95), channel_id=1, replica_groups=mesh['dp'=2,'row'=4,'col'=4] {'row'}, dimensions={0} | all-to-all | bytes 4194304 | tf_op jit(solution)/shard_map/all_to_all | solution.py:652
  427.5 4.4 all-to-all-start.7
  442.8 9.2 %collective-permute-done.5 = f32[2,1024]{1,0:T(2,128)S(1)} collective-permute-done((f32[2,1024]{1,0:T(2,128)S(1)}, f32[2,1024]{1,0:T(2,128)S(1)}, u32[]{:S(2)}, u32[]{:S(2)}) %collective-permute-start.5) | collective-permute-done | bytes 8224 | tf_op jit(solution)/shard_map/ppermute | solution.py:711
  452.1 4.6 collective-permute-start.6
  462.5 5.1 all-to-all-start.8
  478.7 14.4 %all-to-all-done.8 = bf16[4,1024,128]{2,1,0:T(8,128)(2,1)} async-done(((bf16[4,1024,128]{2,1,0:T(8,128)(2,1)}), bf16[4,1024,128]{2,1,0:T(8,128)(2,1)}, u32[]{:S(2)}, u32[]{:S(2)}) %all-to-all-start.8) | async-done | bytes 1048608 | tf_op jit(solution)/shard_map/all_to_all | solution.py:652
  (139 shorter events, 64.7 us)
Async XLA Ops:
  7.2 42.2 %copy-start = (bf16[656,256]{1,0:T(8,128)(2,1)S(1)}, bf16[656,256]{1,0:T(8,128)(2,1)}, u32[]{:S(2)}) copy-start(bf16[656,256]{1,0:T(8,128)(2,1)} %param.20) | copy-start | bytes 1007620
  7.2 156.3 %all-gather.5.cloned.1.call-start = ((), (), s32[]{:S(2)}) async-start(), calls=%async_computation.15 | async-start | bytes 9437184 | tf_op jit(solution)/shard_map/all_gather | solution.py:668
  13.5 35.9 %copy-start.10 = (bf16[256,656]{0,1:T(8,128)(2,1)S(1)}, bf16[256,656]{0,1:T(8,128)(2,1)}, u32[]{:S(2)}) copy-start(bf16[256,656]{0,1:T(8,128)(2,1)} %param.19) | copy-start | bytes 1007620
  49.3 149.0 %all-gather.7.cloned.1.call-start = ((), (), s32[]{:S(2)}) async-start(), calls=%async_computation.16 | async-start | bytes 18137088 | tf_op jit(solution)/shard_map/all_gather | solution.py:668
  49.8 49.3 %copy-start.4 = (bf16[4096,256]{1,0:T(8,128)(2,1)S(1)}, bf16[4096,256]{1,0:T(8,128)(2,1)}, u32[]{:S(2)}) copy-start(bf16[4096,256]{1,0:T(8,128)(2,1)} %param.13) | copy-start | bytes 6291460
  101.0 56.5 %all-to-all-start.2 = ((bf16[4,1152,256]{2,1,0:T(8,128)(2,1)}), bf16[4,1152,256]{2,1,0:T(8,128)(2,1)S(1)}, u32[]{:S(2)}, u32[]{:S(2)}) async-start(bf16[4,1152,256]{2,1,0:T(8,128)(2,1)} %pad_maximum_fusion), calls=%async_computation.2 | async-start | bytes 4718592 | tf_op jit(solution)/shard_map/all_to_all | solution.py:652
  157.5 71.1 %all-to-all-start.3 = ((bf16[4,1024,256]{2,1,0:T(8,128)(2,1)}), bf16[4,1024,256]{2,1,0:T(8,128)(2,1)}, u32[]{:S(2)}, u32[]{:S(2)}) async-start(bf16[4,1024,256]{2,1,0:T(8,128)(2,1)} %bitcast.76), calls=%async_computation.3 | async-start | bytes 4194304 | tf_op jit(solution)/shard_map/all_to_all | solution.py:652
  162.0 139.2 %reduce-scatter.4.cloned.1.call-start = ((), (), s32[]{:S(2)}) async-start(), calls=%async_computation.12 | async-start | bytes 6045696 | tf_op jit(solution)/shard_map/reduce_scatter | solution.py:673
  238.5 41.5 %all-to-all-start.4 = ((bf16[4,768,256]{2,1,0:T(8,128)(2,1)}), bf16[4,768,256]{2,1,0:T(8,128)(2,1)S(1)}, u32[]{:S(2)}, u32[]{:S(2)}) async-start(bf16[4,768,256]{2,1,0:T(8,128)(2,1)} %get-tuple-element.68), calls=%async_computation.4 | async-start | bytes 3145728 | tf_op jit(solution)/shard_map/all_to_all | solution.py:652
  243.8 183.7 %reduce-scatter.8.cloned.1.call-start = ((), (), s32[]{:S(2)}) async-start(), calls=%async_computation.14 | async-start | bytes 12091392 | tf_op jit(solution)/shard_map/reduce_scatter | solution.py:673
  303.7 44.7 %all-to-all-start.5 = ((bf16[4,584,256]{2,1,0:T(8,128)(2,1)}), bf16[4,584,256]{2,1,0:T(8,128)(2,1)S(1)}, u32[]{:S(2)}, u32[]{:S(2)}) async-start(bf16[4,584,256]{2,1,0:T(8,128)(2,1)} %pad_maximum_fusion.2), calls=%async_computation.6 | async-start | bytes 2392064 | tf_op jit(solution)/shard_map/all_to_all | solution.py:652
  308.7 153.8 %reduce-scatter.6.cloned.1.call-start = ((), (), s32[]{:S(2)}) async-start(), calls=%async_computation.13 | async-start | bytes 9437184 | tf_op jit(solution)/shard_map/reduce_scatter | solution.py:673
  332.2 16.2 %collective-permute-start = (bf16[64,2048]{1,0:T(8,128)(2,1)}, bf16[64,2048]{1,0:T(8,128)(2,1)S(1)}, u32[]{:S(2)}, u32[]{:S(2)}) collective-permute-start(bf16[64,2048]{1,0:T(8,128)(2,1)} %get-tuple-element.85), channel_id=1, source_target_pairs={{0,4},{4,8},{8,12},{1,5},{5,9},{9,13},{2,6},{6,10},{10,14},{3,7},{... | collective-permute-start | bytes 786440 | tf_op jit(solution)/shard_map/ppermute | solution.py:790
  336.5 12.0 %collective-permute-start.1 = (bf16[64,2048]{1,0:T(8,128)(2,1)}, bf16[64,2048]{1,0:T(8,128)(2,1)S(1)}, u32[]{:S(2)}, u32[]{:S(2)}) collective-permute-start(bf16[64,2048]{1,0:T(8,128)(2,1)} %get-tuple-element.91), channel_id=1, source_target_pairs={{4,0},{8,4},{12,8},{5,1},{9,5},{13,9},{6,2},{10,6},{14,10},{7,3},{... | collective-permute-start | bytes 786440 | tf_op jit(solution)/shard_map/ppermute | solution.py:790
  427.5 35.0 %all-to-all-start.7 = ((bf16[4,1312,128]{2,1,0:T(8,128)(2,1)}), bf16[4,1312,128]{2,1,0:T(8,128)(2,1)}, u32[]{:S(2)}, u32[]{:S(2)}) async-start(bf16[4,1312,128]{2,1,0:T(8,128)(2,1)} %bitcast.78), calls=%async_computation.10 | async-start | bytes 2686976 | tf_op jit(solution)/shard_map/all_to_all | solution.py:652
  432.0 3.9 collective-permute-start.2
  435.9 3.7 collective-permute-start.3
  439.6 1.2 collective-permute-start.4
  440.9 11.2 %collective-permute-start.5 = (f32[2,1024]{1,0:T(2,128)S(1)}, f32[2,1024]{1,0:T(2,128)S(1)}, u32[]{:S(2)}, u32[]{:S(2)}) collective-permute-start(f32[2,1024]{1,0:T(2,128)S(1)} %add.87), channel_id=1, source_target_pairs={{0,4},{4,0},{8,12},{12,8},{1,5},{5,1},{9,13},{13,9},{2,6},{6,2},{1... | collective-permute-start | bytes 24584 | tf_op jit(solution)/shard_map/ppermute | solution.py:711
  452.1 10.4 %collective-permute-start.6 = (f32[2,1024]{1,0:T(2,128)S(1)}, f32[2,1024]{1,0:T(2,128)S(1)}, u32[]{:S(2)}, u32[]{:S(2)}) collective-permute-start(f32[2,1024]{1,0:T(2,128)S(1)} %add.88), channel_id=1, source_target_pairs={{0,8},{4,12},{8,0},{12,4},{1,9},{5,13},{9,1},{13,5},{2,10},{6,14},... | collective-permute-start | bytes 24584 | tf_op jit(solution)/shard_map/ppermute | solution.py:711
  458.0 13.1 %collective-permute-start.9 = (bf16[656,128]{1,0:T(8,128)(2,1)S(1)}, bf16[656,128]{1,0:T(8,128)(2,1)S(1)}, u32[]{:S(2)}, u32[]{:S(2)}) collective-permute-start(bf16[656,128]{1,0:T(8,128)(2,1)S(1)} %reduce_sum.81), channel_id=1, source_target_pairs={{0,16},{16,0},{1,17},{17,1},{2,18},{18,2},{3,19},{19,3},{4,20},{20... | collective-permute-start | bytes 503816 | tf_op jit(solution)/shard_map/ppermute | solution.py:640
  462.5 30.7 %all-to-all-start.8 = ((bf16[4,1024,128]{2,1,0:T(8,128)(2,1)}), bf16[4,1024,128]{2,1,0:T(8,128)(2,1)}, u32[]{:S(2)}, u32[]{:S(2)}) async-start(bf16[4,1024,128]{2,1,0:T(8,128)(2,1)} %bitcast.79), calls=%async_computation.11 | async-start | bytes 2097152 | tf_op jit(solution)/shard_map/all_to_all | solution.py:652
  475.4 20.0 %collective-permute-start.8 = (bf16[1312,128]{1,0:T(8,128)(2,1)S(1)}, bf16[1312,128]{1,0:T(8,128)(2,1)S(1)}, u32[]{:S(2)}, u32[]{:S(2)}) collective-permute-start(bf16[1312,128]{1,0:T(8,128)(2,1)S(1)} %reduce_sum.79), channel_id=1, source_target_pairs={{0,16},{16,0},{1,17},{17,1},{2,18},{18,2},{3,19},{19,3},{4,20},{20... | collective-permute-start | bytes 1007624 | tf_op jit(solution)/shard_map/ppermute | solution.py:640
  494.7 7.3 %collective-permute-start.7 = (bf16[1024,128]{1,0:T(8,128)(2,1)S(1)}, bf16[1024,128]{1,0:T(8,128)(2,1)S(1)}, u32[]{:S(2)}, u32[]{:S(2)}) collective-permute-start(bf16[1024,128]{1,0:T(8,128)(2,1)S(1)} %reduce_sum.78), channel_id=1, source_target_pairs={{0,16},{16,0},{1,17},{17,1},{2,18},{18,2},{3,19},{19,3},{4,20},{20... | collective-permute-start | bytes 786440 | tf_op jit(solution)/shard_map/ppermute | solution.py:640
  (13 other events, 147.0 us)
Sparse Core Ops, SparseCore 0:
  49.5 53.4 all-gather.4
  104.9 87.0 all-gather.6
  238.7 58.8 reduce-scatter.3
  301.3 83.8 reduce-scatter.7
  388.9 72.1 reduce-scatter.5

commit v6 on v5

--- a/solution.py
+++ b/solution.py
@@ -675,15 +675,17 @@
 
 def sum_rows(parts):
     half = jnp.sum(parts.astype(F32), axis=0).astype(BF16)
-    other = over_dp(half)
-    first = lax.axis_index("dp") == 0
-    return jnp.where(first, half, other), jnp.where(first, other, half)
-
-
-def finish_kernel(kinds, width, low, high, *outs):
+    return lax.axis_index("dp").reshape(1), half, over_dp(half)
+
+
+def finish_kernel(kinds, width, which, mine, other, *outs):
+    low_is_mine = jnp.full((width, LANES), which[0]) == 0
     for t, (kind, out) in enumerate(zip(kinds, outs, strict=True)):
         rows = slice(t * width, (t + 1) * width)
-        value = jnp.concatenate([low[rows, :], high[rows, :]], axis=1).astype(F32)
+        one, two = mine[rows, :].astype(F32), other[rows, :].astype(F32)
+        value = jnp.concatenate(
+            [jnp.where(low_is_mine, one, two), jnp.where(low_is_mine, two, one)], axis=1
+        )
         if kind not in "qkv":
             out[...] = value
             continue
@@ -696,6 +698,9 @@
 def finish(halves, kinds, width):
     return pl.pallas_call(
         functools.partial(finish_kernel, kinds, width),
+        in_specs=[
+            pl.BlockSpec(memory_space=space) for space in (pltpu.SMEM, pltpu.VMEM, pltpu.VMEM)
+        ],
         out_shape=[struct((256, width) if kind in "qkv" else (width, 256), F32) for kind in kinds],
         compiler_params=pltpu.CompilerParams(vmem_limit_bytes=VMEM),
         cost_estimate=pl.CostEstimate(flops=1, bytes_accessed=2**21, transcendentals=0),
@@ -810,14 +815,15 @@
         spans = [padded[j * tokens : (j + 1) * tokens + 2 * REACH] for j in range(rows)]
         heads_own = gather_rows(heads_half)
         heads_w = gather_groups(heads_own[:, :WIDTH])
-        feed_own = gather_rows(after(feed_half, heads_own))
+        spans = jnp.stack(spans)
+        feed_own = gather_rows(after(feed_half, heads_own, spans))
         feed_w = gather_groups(feed_own)
         last = WIDTH + marks.shape[0]
         marks = heads_own[:, WIDTH:last].reshape(rows, 2, length)
         marks = lax.dynamic_index_in_dim(marks, sequence, 0, False).astype(jnp.int32)
         gain_slots = heads_own[:, last : last + 4].reshape(SLOTS, 2, 256)
         tables = positions_and_masks(*marks, first, tokens)
-        xs = exchange(after(jnp.stack(spans), feed_own))
+        xs = exchange(after(spans, feed_own))
         cots = exchange(after(cotangent.reshape(rows, tokens, 256), xs))
     else:
         xs = exchange(tokens_in.reshape(rows, tokens, 256))

time: 517 us -> 516 us (level)
  transfers between devices with their start and end apart: 21 -> 21, of which waited for: 8 -> 9; matrix products, arithmetic and copies ran while one was open for 5% -> 4% of each run, Pallas kernels for 37% -> 37%
where the time goes in v6:
time: 516 us; the launch traced here: 511 us
  Pallas kernels  200 us (39%)
  blocking collectives  133 us (26%)
  waiting for transfers between devices  79.7 us (15%)
  starting transfers between devices  49.7 us (10%)
  other arithmetic  19.8 us (4%)
  between operations  14.8 us (3%)
  local copies, waits for them, and re-layouts  14.4 us (3%)
    all_to_all x3, blocking collectives, exchange(): return lax.all_to_all(value, 'row', 0, 0)  133 us
    all_to_all x6, waiting for transfers between devices, exchange(): return lax.all_to_all(value, 'row', 0, 0)  59.1 us
    pallas_call x4, Pallas kernels, outer_product(): pl.pallas_call(functools.partial(outer_kernel, count, tokens), grid=(GROU...  50.7 us
    pallas_call x1, Pallas kernels, feed_back(): call(feed_back_kernel, (GROUPS + tokens // TILE,), [resident(cots.shape)]...  36.5 us
    pallas_call x1, Pallas kernels, feed(): call(feed_kernel, (GROUPS + tokens // TILE,), [resident((tokens, WIDTH)),...  30.2 us
    all_to_all x6, starting transfers between devices, exchange(): return lax.all_to_all(value, 'row', 0, 0)  27.5 us
    pallas_call x1, Pallas kernels, attend_back(): call(attend_back_kernel, (blocks + 1,), pairs(WIDTH) * 3 + pairs(LANES) *...  23.5 us
    pallas_call x1, Pallas kernels, attend(): call(attend_kernel, (blocks,), pair_of((QUERY, WIDTH)) * 3 + pair_of((SLO...  20.9 us
  transfers between devices with their start and end apart: 21, of which 9 were waited for; matrix products, arithmetic and copies ran while one was open for 4% of the time, Pallas kernels for 37%

profile of v6, /device:TPU:0, one launch (start us, length us, event | category | flops | bytes accessed | tf_op | source)
XLA Modules:
  0.0 511.3 jit_solution(9090528583489369991)
XLA Ops:
  13.6 33.7 %all_to_all.45 = bf16[4,1104,128]{2,1,0:T(8,128)(2,1)S(1)} all-to-all(bf16[4,1104,128]{2,1,0:T(8,128)(2,1)S(1)} %broadcast_in_dim.41), channel_id=1, replica_groups=mesh['dp'=2,'row'=4,'col'=4] {'row'}, dimensions={0} | all-to-all | bytes 2260992 | tf_op jit(solution)/shard_map/all_to_all | solution.py:652
  52.4 49.1 %all_to_all.46 = bf16[4,1968,128]{2,1,0:T(8,128)(2,1)} all-to-all(bf16[4,1968,128]{2,1,0:T(8,128)(2,1)S(1)} %broadcast_in_dim.42), channel_id=1, replica_groups=mesh['dp'=2,'row'=4,'col'=4] {'row'}, dimensions={0} | all-to-all | bytes 4030464 | tf_op jit(solution)/shard_map/all_to_all | solution.py:652
  111.3 46.7 %all-to-all-done.2.xs.refs_6_.refs_7_.refs_0_ = bf16[4,1152,256]{2,1,0:T(8,128)(2,1)S(1)} async-done(((bf16[4,1152,256]{2,1,0:T(8,128)(2,1)}), bf16[4,1152,256]{2,1,0:T(8,128)(2,1)S(1)}, u32[]{:S(2)}, u32[]{:S(2)}) %all-to-all-start.2) | async-done | bytes 2359328 | tf_op jit(solution)/shard_map/all_to_all | solution.py:652
  158.1 4.4 all-to-all-start.3
  164.1 13.9 %project.1 = (bf16[1152,1024]{1,0:T(8,128)(2,1)}, bf16[1152,1024]{1,0:T(8,128)(2,1)}, bf16[1152,1024]{1,0:T(8,128)(2,1)}, bf16[1152,1024]{1,0:T(8,128)(2,1)}) custom-call(bf16[4,1152,256]{2,1,0:T(8,128)(2,1)} %copy-done.2, f32[1,1024]{1,0:T(1,128)} %bitcast.97, f32[1152,128]{1,0:T(8,128)} %get-tuple-element.120.cosine.refs_6_.refs_7_.refs_5_, ...), custom_call_target="tpu_custom_call" | custom-call | flops 7247757312 | bytes 18087936 | tf_op jit(solution)/shard_map/project/pallas_call | solution.py:164
  178.0 20.9 %attend.1 = (bf16[1024,1024]{1,0:T(8,128)(2,1)}, bf16[8,4,512,256]{3,2,1,0:T(8,128)(2,1)}, bf16[1024,1024]{1,0:T(8,128)(2,1)}, bf16[1024,1024]{1,0:T(8,128)(2,1)}) custom-call(bf16[1152,1024]{1,0:T(8,128)(2,1)} %get-tuple-element.61.refs_0_.refs_1_, bf16[1152,1024]{1,0:T(8,128)(2,1)} %get-tuple-element.61.refs_0_.refs_1_, ...), custom_call_target="tpu_custom_call" | custom-call | flops 6442450944 | bytes 23068672 | tf_op jit(solution)/shard_map/attend/pallas_call | solution.py:256
  198.9 30.2 %feed.1 = (bf16[4,1024,656]{2,1,0:T(8,128)(2,1)}, bf16[4,1024,656]{2,1,0:T(8,128)(2,1)}, bf16[4,1024,656]{2,1,0:T(8,128)(2,1)}, bf16[4,768,256]{2,1,0:T(8,128)(2,1)}, bf16[4,256,256]{2,1,0:T(8,128)(2,1)}) custom-call(bf16[1024,1024]{1,0:T(8,128)(2,1)} %get-tuple-element.64.refs_0_.refs_2_.refs_3_, bf16[1024,1024]{1,0:T(8,128)(2,1)} %get-tuple-element.65.refs_1_.refs_3_, ...), custom_call_target="tpu_custom_call" | custom-call | flops 16508780544 | bytes 38535168 | tf_op jit(solution)/shard_map/feed/pallas_call | solution.py:470
  229.2 9.9 %outer_product.4 = bf16[2,4,4,656,128]{4,3,2,1,0:T(8,128)(2,1)} custom-call(bf16[4,1024,656]{2,1,0:T(8,128)(2,1)} %get-tuple-element.71.refs_0_, bf16[4,1024,256]{2,1,0:T(8,128)(2,1)} %all-to-all-done.3.refs_1_.refs_0_), custom_call_target="tpu_custom_call" | custom-call | flops 5502926848 | bytes 12845056 | tf_op jit(solution)/shard_map/outer_product/pallas_call | solution.py:615
  239.1 5.5 %all-to-all-start.4 = ((bf16[4,768,256]{2,1,0:T(8,128)(2,1)}), bf16[4,768,256]{2,1,0:T(8,128)(2,1)S(1)}, u32[]{:S(2)}, u32[]{:S(2)}) async-start(bf16[4,768,256]{2,1,0:T(8,128)(2,1)} %get-tuple-element.68), calls=%async_computation.4 | async-start | bytes 3145728 | tf_op jit(solution)/shard_map/all_to_all | solution.py:652
  244.5 36.5 %feed_back.1 = (bf16[4,1024,656]{2,1,0:T(8,128)(2,1)}, bf16[4,1024,656]{2,1,0:T(8,128)(2,1)}, bf16[1024,1024]{1,0:T(8,128)(2,1)}, bf16[1024,1024]{1,0:T(8,128)(2,1)}, f32[8,1024]{1,0:T(8,128)}) custom-call(bf16[4,1024,256]{2,1,0:T(8,128)(2,1)} %all-to-all-done.3.refs_1_.refs_0_, bf16[4,1024,656]{2,1,0:T(8,128)(2,1)} %get-tuple-element.73.refs_1_, ...), custom_call_target="tpu_custom_call" | custom-call | flops 18656264192 | bytes 40632320 | tf_op jit(solution)/shard_map/feed_back/pallas_call | solution.py:523
  281.0 20.3 %outer_product.5 = bf16[2,4,4,1312,128]{4,3,2,1,0:T(8,128)(2,1)} custom-call(bf16[4,1024,656]{2,1,0:T(8,128)(2,1)} %get-tuple-element.77.refs_0_, bf16[4,1024,656]{2,1,0:T(8,128)(2,1)} %get-tuple-element.78.refs_1_, bf16[1024,1024]{1,0:T(8,128)(2,1)} %get-tuple-element.64.refs_0_.refs_2_.refs_3_, bf16[1024,1024]{1,0:T(8,128)(2,1)} %get-tuple-element.64.refs_0_.refs_2_.refs_3_), custom_call_target="tpu_custom_call" | custom-call | flops 11005853696 | bytes 23592960 | tf_op jit(solution)/shard_map/outer_product/pallas_call | solution.py:615
  303.9 5.1 %all-to-all-start.5 = ((bf16[4,584,256]{2,1,0:T(8,128)(2,1)}), bf16[4,584,256]{2,1,0:T(8,128)(2,1)S(1)}, u32[]{:S(2)}, u32[]{:S(2)}) async-start(bf16[4,584,256]{2,1,0:T(8,128)(2,1)} %pad_maximum_fusion.2), calls=%async_computation.6 | async-start | bytes 2392064 | tf_op jit(solution)/shard_map/all_to_all | solution.py:652
  309.0 23.5 %attend_back.1 = (bf16[1024,1024]{1,0:T(8,128)(2,1)}, bf16[1152,1024]{1,0:T(8,128)(2,1)}, bf16[1152,1024]{1,0:T(8,128)(2,1)}, bf16[64,2048]{1,0:T(8,128)(2,1)}, ...) custom-call(bf16[1152,1024]{1,0:T(8,128)(2,1)} %get-tuple-element.61.refs_0_.refs_1_, ...), custom_call_target="tpu_custom_call" | custom-call | flops 8589934592 | bytes 23068672 | tf_op jit(solution)/shard_map/attend_back/pallas_call | solution.py:363
  332.5 4.2 collective-permute-start
  338.3 10.1 %outer_product.6.refs_4_ = bf16[2,4,4,1024,128]{4,3,2,1,0:T(8,128)(2,1)} custom-call(bf16[1024,1024]{1,0:T(8,128)(2,1)} %get-tuple-element.81.refs_0_.refs_1_, bf16[1024,1024]{1,0:T(8,128)(2,1)} %get-tuple-element.86.refs_1_, bf16[1152,1024]{1,0:T(8,128)(2,1)} %get-tuple-element.87.refs_2_.refs_3_, bf16[1024,1024]{1,0:T(8,128)(2,1)} %get-tuple-element.88.refs_3_.refs_4_), custom_call_target="tpu_custom_call" | custom-call | flops 4294967296 | bytes 10485760 | tf_op jit(solution)/shard_map/outer_product/pallas_call | solution.py:615
  351.5 15.8 %unproject.1 = (bf16[4,1024,256]{2,1,0:T(8,128)(2,1)}, f32[8,1024]{1,0:T(8,128)}) custom-call(bf16[4,1152,256]{2,1,0:T(8,128)(2,1)} %copy-done.2, bf16[1024,1024]{1,0:T(8,128)(2,1)} %get-tuple-element.81.refs_0_.refs_1_, bf16[1152,1024]{1,0:T(8,128)(2,1)} %get-tuple-element.96.refs_2_.refs_0_, bf16[1152,1024]{1,0:T(8,128)(2,1)} %get-tuple-element.93.refs_3_.refs_1_, ...), custom_call_target="tpu_custom_call" | custom-call | flops 6442450944 | bytes 18874368 | tf_op jit(solution)/shard_map/unproject/pallas_call | solution.py:561
  367.3 10.3 %outer_product.7 = bf16[2,4,4,1024,128]{4,3,2,1,0:T(8,128)(2,1)} custom-call(bf16[1152,1024]{1,0:T(8,128)(2,1)} %get-tuple-element.96.refs_2_.refs_0_, bf16[1152,1024]{1,0:T(8,128)(2,1)} %get-tuple-element.93.refs_3_.refs_1_, bf16[1152,1024]{1,0:T(8,128)(2,1)} %get-tuple-element.87.refs_2_.refs_3_, ...), custom_call_target="tpu_custom_call", output_to_operand_aliasing={{}: (4, {})} | custom-call | flops 4294967296 | bytes 10485760 | tf_op jit(solution)/shard_map/outer_product/pallas_call | solution.py:615
  377.7 50.2 %all_to_all.47 = bf16[4,1024,256]{2,1,0:T(8,128)(2,1)S(1)} all-to-all(bf16[4,1024,256]{2,1,0:T(8,128)(2,1)} %get-tuple-element.95), channel_id=1, replica_groups=mesh['dp'=2,'row'=4,'col'=4] {'row'}, dimensions={0} | all-to-all | bytes 4194304 | tf_op jit(solution)/shard_map/all_to_all | solution.py:652
  427.8 4.4 all-to-all-start.7
  443.2 9.2 %collective-permute-done.5 = f32[2,1024]{1,0:T(2,128)S(1)} collective-permute-done((f32[2,1024]{1,0:T(2,128)S(1)}, f32[2,1024]{1,0:T(2,128)S(1)}, u32[]{:S(2)}, u32[]{:S(2)}) %collective-permute-start.5) | collective-permute-done | bytes 8224 | tf_op jit(solution)/shard_map/ppermute | solution.py:716
  452.4 4.6 collective-permute-start.6
  457.0 5.8 %collective-permute-done.6 = f32[2,1024]{1,0:T(2,128)S(1)} collective-permute-done((f32[2,1024]{1,0:T(2,128)S(1)}, f32[2,1024]{1,0:T(2,128)S(1)}, u32[]{:S(2)}, u32[]{:S(2)}) %collective-permute-start.6) | collective-permute-done | bytes 8224 | tf_op jit(solution)/shard_map/ppermute | solution.py:716
  462.8 4.2 all-to-all-start.8
  480.0 12.4 %all-to-all-done.8 = bf16[4,1024,128]{2,1,0:T(8,128)(2,1)} async-done(((bf16[4,1024,128]{2,1,0:T(8,128)(2,1)}), bf16[4,1024,128]{2,1,0:T(8,128)(2,1)}, u32[]{:S(2)}, u32[]{:S(2)}) %all-to-all-start.8) | async-done | bytes 1048608 | tf_op jit(solution)/shard_map/all_to_all | solution.py:652
  (148 shorter events, 65.4 us)
Async XLA Ops:
  7.2 42.2 %copy-start = (bf16[656,256]{1,0:T(8,128)(2,1)S(1)}, bf16[656,256]{1,0:T(8,128)(2,1)}, u32[]{:S(2)}) copy-start(bf16[656,256]{1,0:T(8,128)(2,1)} %param.20) | copy-start | bytes 1007620
  7.2 156.9 %all-gather.5.cloned.1.call-start = ((), (), s32[]{:S(2)}) async-start(), calls=%async_computation.15 | async-start | bytes 9437184 | tf_op jit(solution)/shard_map/all_gather | solution.py:668
  13.5 35.9 %copy-start.16 = (bf16[256,656]{0,1:T(8,128)(2,1)S(1)}, bf16[256,656]{0,1:T(8,128)(2,1)}, u32[]{:S(2)}) copy-start(bf16[256,656]{0,1:T(8,128)(2,1)} %param.19) | copy-start | bytes 1007620
  49.4 149.6 %all-gather.7.cloned.1.call-start = ((), (), s32[]{:S(2)}) async-start(), calls=%async_computation.16 | async-start | bytes 18137088 | tf_op jit(solution)/shard_map/all_gather | solution.py:668
  101.6 56.5 %all-to-all-start.2 = ((bf16[4,1152,256]{2,1,0:T(8,128)(2,1)}), bf16[4,1152,256]{2,1,0:T(8,128)(2,1)S(1)}, u32[]{:S(2)}, u32[]{:S(2)}) async-start(bf16[4,1152,256]{2,1,0:T(8,128)(2,1)} %pad_maximum_fusion), calls=%async_computation.2 | async-start | bytes 4718592 | tf_op jit(solution)/shard_map/all_to_all | solution.py:652
  158.1 71.1 %all-to-all-start.3 = ((bf16[4,1024,256]{2,1,0:T(8,128)(2,1)}), bf16[4,1024,256]{2,1,0:T(8,128)(2,1)}, u32[]{:S(2)}, u32[]{:S(2)}) async-start(bf16[4,1024,256]{2,1,0:T(8,128)(2,1)} %bitcast.77), calls=%async_computation.3 | async-start | bytes 4194304 | tf_op jit(solution)/shard_map/all_to_all | solution.py:652
  162.5 138.8 %reduce-scatter.4.cloned.1.call-start = ((), (), s32[]{:S(2)}) async-start(), calls=%async_computation.12 | async-start | bytes 6045696 | tf_op jit(solution)/shard_map/reduce_scatter | solution.py:673
  239.1 41.9 %all-to-all-start.4 = ((bf16[4,768,256]{2,1,0:T(8,128)(2,1)}), bf16[4,768,256]{2,1,0:T(8,128)(2,1)S(1)}, u32[]{:S(2)}, u32[]{:S(2)}) async-start(bf16[4,768,256]{2,1,0:T(8,128)(2,1)} %get-tuple-element.68), calls=%async_computation.4 | async-start | bytes 3145728 | tf_op jit(solution)/shard_map/all_to_all | solution.py:652
  244.5 183.3 %reduce-scatter.8.cloned.1.call-start = ((), (), s32[]{:S(2)}) async-start(), calls=%async_computation.14 | async-start | bytes 12091392 | tf_op jit(solution)/shard_map/reduce_scatter | solution.py:673
  303.9 44.5 %all-to-all-start.5 = ((bf16[4,584,256]{2,1,0:T(8,128)(2,1)}), bf16[4,584,256]{2,1,0:T(8,128)(2,1)S(1)}, u32[]{:S(2)}, u32[]{:S(2)}) async-start(bf16[4,584,256]{2,1,0:T(8,128)(2,1)} %pad_maximum_fusion.2), calls=%async_computation.6 | async-start | bytes 2392064 | tf_op jit(solution)/shard_map/all_to_all | solution.py:652
  309.0 153.8 %reduce-scatter.6.cloned.1.call-start = ((), (), s32[]{:S(2)}) async-start(), calls=%async_computation.13 | async-start | bytes 9437184 | tf_op jit(solution)/shard_map/reduce_scatter | solution.py:673
  332.5 15.9 %collective-permute-start = (bf16[64,2048]{1,0:T(8,128)(2,1)}, bf16[64,2048]{1,0:T(8,128)(2,1)S(1)}, u32[]{:S(2)}, u32[]{:S(2)}) collective-permute-start(bf16[64,2048]{1,0:T(8,128)(2,1)} %get-tuple-element.85), channel_id=1, source_target_pairs={{0,4},{4,8},{8,12},{1,5},{5,9},{9,13},{2,6},{6,10},{10,14},{3,7},{... | collective-permute-start | bytes 786440 | tf_op jit(solution)/shard_map/ppermute | solution.py:795
  336.7 11.7 %collective-permute-start.1 = (bf16[64,2048]{1,0:T(8,128)(2,1)}, bf16[64,2048]{1,0:T(8,128)(2,1)S(1)}, u32[]{:S(2)}, u32[]{:S(2)}) collective-permute-start(bf16[64,2048]{1,0:T(8,128)(2,1)} %get-tuple-element.91), channel_id=1, source_target_pairs={{4,0},{8,4},{12,8},{5,1},{9,5},{13,9},{6,2},{10,6},{14,10},{7,3},{... | collective-permute-start | bytes 786440 | tf_op jit(solution)/shard_map/ppermute | solution.py:795
  427.8 35.0 %all-to-all-start.7 = ((bf16[4,1312,128]{2,1,0:T(8,128)(2,1)}), bf16[4,1312,128]{2,1,0:T(8,128)(2,1)}, u32[]{:S(2)}, u32[]{:S(2)}) async-start(bf16[4,1312,128]{2,1,0:T(8,128)(2,1)} %bitcast.79), calls=%async_computation.10 | async-start | bytes 2686976 | tf_op jit(solution)/shard_map/all_to_all | solution.py:652
  432.3 38.1 %slice-start = ((bf16[4,584,256]{2,1,0:T(8,128)(2,1)}), bf16[4,256,256]{2,1,0:T(8,128)(2,1)S(1)}, s32[]{:S(2)}) async-start(bf16[4,584,256]{2,1,0:T(8,128)(2,1)} %copy-done.5), calls=%async_computation.17 | async-start | bytes 1048576 | tf_op jit(solution)/shard_map/split | solution.py:875
  432.4 3.9 collective-permute-start.2
  436.2 3.7 collective-permute-start.3
  440.0 1.2 collective-permute-start.4
  441.2 11.2 %collective-permute-start.5 = (f32[2,1024]{1,0:T(2,128)S(1)}, f32[2,1024]{1,0:T(2,128)S(1)}, u32[]{:S(2)}, u32[]{:S(2)}) collective-permute-start(f32[2,1024]{1,0:T(2,128)S(1)} %add.87), channel_id=1, source_target_pairs={{0,4},{4,0},{8,12},{12,8},{1,5},{5,1},{9,13},{13,9},{2,6},{6,2},{1... | collective-permute-start | bytes 24584 | tf_op jit(solution)/shard_map/ppermute | solution.py:716
  452.4 10.4 %collective-permute-start.6 = (f32[2,1024]{1,0:T(2,128)S(1)}, f32[2,1024]{1,0:T(2,128)S(1)}, u32[]{:S(2)}, u32[]{:S(2)}) collective-permute-start(f32[2,1024]{1,0:T(2,128)S(1)} %add.88), channel_id=1, source_target_pairs={{0,8},{4,12},{8,0},{12,4},{1,9},{5,13},{9,1},{13,5},{2,10},{6,14},... | collective-permute-start | bytes 24584 | tf_op jit(solution)/shard_map/ppermute | solution.py:716
  462.8 29.6 %all-to-all-start.8 = ((bf16[4,1024,128]{2,1,0:T(8,128)(2,1)}), bf16[4,1024,128]{2,1,0:T(8,128)(2,1)}, u32[]{:S(2)}, u32[]{:S(2)}) async-start(bf16[4,1024,128]{2,1,0:T(8,128)(2,1)} %bitcast.80), calls=%async_computation.11 | async-start | bytes 2097152 | tf_op jit(solution)/shard_map/all_to_all | solution.py:652
  468.4 5.6 %collective-permute-start.9 = (bf16[656,128]{1,0:T(8,128)(2,1)S(1)}, bf16[656,128]{1,0:T(8,128)(2,1)S(1)}, u32[]{:S(2)}, u32[]{:S(2)}) collective-permute-start(bf16[656,128]{1,0:T(8,128)(2,1)S(1)} %reduce_sum.81.mine), channel_id=1, source_target_pairs={{0,16},{16,0},{1,17},{17,1},{2,18},{18,2},{3,19},{19,3},{4,20},{20... | collective-permute-start | bytes 503816 | tf_op jit(solution)/shard_map/ppermute | solution.py:640
  478.2 20.3 %collective-permute-start.8 = (bf16[1312,128]{1,0:T(8,128)(2,1)S(1)}, bf16[1312,128]{1,0:T(8,128)(2,1)S(1)}, u32[]{:S(2)}, u32[]{:S(2)}) collective-permute-start(bf16[1312,128]{1,0:T(8,128)(2,1)S(1)} %reduce_sum.79.mine), channel_id=1, source_target_pairs={{0,16},{16,0},{1,17},{17,1},{2,18},{18,2},{3,19},{19,3},{4,20},{20... | collective-permute-start | bytes 1007624 | tf_op jit(solution)/shard_map/ppermute | solution.py:640
  494.0 7.5 %collective-permute-start.7 = (bf16[1024,128]{1,0:T(8,128)(2,1)S(1)}, bf16[1024,128]{1,0:T(8,128)(2,1)S(1)}, u32[]{:S(2)}, u32[]{:S(2)}) collective-permute-start(bf16[1024,128]{1,0:T(8,128)(2,1)S(1)} %reduce_sum.78.mine), channel_id=1, source_target_pairs={{0,16},{16,0},{1,17},{17,1},{2,18},{18,2},{3,19},{19,3},{4,20},{20... | collective-permute-start | bytes 786440 | tf_op jit(solution)/shard_map/ppermute | solution.py:640
  (19 other events, 129.7 us)
Sparse Core Ops, SparseCore 0:
  49.5 53.4 all-gather.4
  104.9 87.0 all-gather.6
  239.2 58.7 reduce-scatter.3
  301.5 84.1 reduce-scatter.7
  389.4 71.3 reduce-scatter.5
